TPU v7x, 32 devices: a whole 2x2x4 slice. The times are simulated.
32 devices in a mesh: ctx: 8 (over z, y), head: 4 (over x, core).
Axes of the slice: x: 2, y: 2, z: 4, core: 2. Of those that a mesh axis runs over, the one named last changes fastest.
Arguments:
- stream: bfloat16 [4096, 2048], P(('ctx', 'head')), may hold values from -6 to 6
- moe_gain: float32 [2048], replicated, may hold values from 0.5 to 1.5
- router: bfloat16 [2048, 64], replicated, may hold values from -0.125 to 0.125
- expert_ids: int32 [4096, 10], P(('ctx', 'head')), may hold values from 0 to 63, all different within a row; in each aligned block of 128 rows (0 to 127, 128 to 255, ...) at most 22 rows name the same one
- expert_gate: bfloat16 [64, 2048, 512], P(('ctx', 'head')), may hold values from -0.125 to 0.125
- expert_up: bfloat16 [64, 2048, 512], P(('ctx', 'head')), may hold values from -0.125 to 0.125
- expert_down: bfloat16 [64, 512, 2048], P(('ctx', 'head')), may hold values from -1 to 1
- mixer_gain: float32 [2048], replicated, may hold values from 0.5 to 1.5
- query_weight: bfloat16 [2048, 1024], P(None, 'head'), may hold values from -0.125 to 0.125
- key_weight: bfloat16 [2048, 1024], P(None, 'head'), may hold values from -0.125 to 0.125
- value_weight: bfloat16 [2048, 2048], P(None, 'head'), may hold values from -0.125 to 0.125
- output_gate: bfloat16 [2048, 2048], P(None, 'head'), may hold values from -0.125 to 0.125
- beta_weight: bfloat16 [2048, 16], P(None, 'head'), may hold values from -0.125 to 0.125
- decay_weight: bfloat16 [2048, 16], P(None, 'head'), may hold values from -0.5 to 0.5
- query_conv: float32 [4, 1024], P(None, 'head'), may hold values from -3 to 3
- key_conv: float32 [4, 1024], P(None, 'head'), may hold values from -3 to 3
- value_conv: float32 [4, 2048], P(None, 'head'), may hold values from -3 to 3
- decay_log: float32 [16], P('head'), may hold values from -12 to -2.5
- decay_bias: float32 [16], P('head'), may hold values from -2 to 1
- head_gain: float32 [128], replicated, may hold values from 0.5 to 1.5
- out_weight: bfloat16 [2048, 2048], P('head'), may hold values from -0.125 to 0.125
Outputs:
- moe_out: bfloat16 [4096, 2048], P(('ctx', 'head'))
- mixer_out: bfloat16 [4096, 2048], P(('ctx', 'head'))
Inputs may be any that keep to these rules, and one draw needn't show every extreme that they name: `expert_ids`: each row names 10 different experts; in each aligned block of 128 rows (the rows of one device) no expert is named by more than 22 rows, a bound that some block reaches.
All inputs are finite; a program needn't handle non-finite values.
Results may differ from a plain program's by a relative error of at most 0.017.
Values may be sent and summed in bfloat16 or wider, within the bound.
No kernel may reach another device: no remote copies, remote signals or barrier semaphores. Data moves between devices by JAX's collectives and lax.ppermute only.
A program may use at most 128 MiB of HBM per device.

v0:
```python
import functools
import math

import jax
import jax.numpy as jnp
from jax import lax
from jax.experimental import pallas as pl
from jax.experimental.pallas import tpu as pltpu
from jax.sharding import PartitionSpec as P

DK = 128
CHUNK = 128
GATHER_LIMIT = 32 << 20


epsilon = 1e-06
f32 = jnp.float32
bf16 = jnp.bfloat16


def passed_along(value, axis, steps):
    count = lax.axis_size(axis)
    first, last = (max(0, -steps), min(count, count - steps))
    return lax.ppermute(value, axis, [(source, source + steps) for source in range(first, last)])


def rms_rows(values, gain):
    values = values.astype(jnp.float32)
    scale = lax.rsqrt(jnp.mean(values * values, axis=-1, keepdims=True) + epsilon)
    return values * scale * gain


def after(value, *earlier):
    return lax.optimization_barrier((value, *earlier))[0]


def whole_ref(array):
    return pl.BlockSpec(array.shape, lambda *_: (0,) * array.ndim)


def worth(microseconds):
    return pl.CostEstimate(
        flops=int(microseconds * 1.15e9), bytes_accessed=int(microseconds * 1e6), transcendentals=0
    )


def contract(a, b, dims, precision=None):
    return lax.dot_general(
        a, b, (dims, ((), ())), precision=precision, preferred_element_type=f32
    )


def parts(values):
    high = values.astype(bf16)
    return high, (values - high.astype(f32)).astype(bf16)


def contract_close(a, b):
    a_high, a_low = parts(a)
    b_high, b_low = parts(b)
    doubled = jnp.concatenate([a_high, a_low], axis=1)
    if 2 * b.shape[1] <= 2 * DK:
        both = jnp.concatenate([b_high, b_low], axis=1)
        product = contract(doubled, jnp.concatenate([both, both], axis=0), ((1,), (0,)))
        return product[:, : b.shape[1]] + product[:, b.shape[1] :]
    return contract(
        doubled, jnp.concatenate([b_high, b_high], axis=0), ((1,), (0,))
    ) + contract(a_high, b_low, ((1,), (0,)))


def contract_rows(a, b):
    a_high, a_low = parts(a)
    b_high, b_low = parts(b)
    product = contract(
        jnp.concatenate([a_high, a_low], axis=1),
        jnp.concatenate(
            [jnp.concatenate([b_high, b_high], axis=1), jnp.concatenate([b_low, b_low], axis=1)],
            axis=0,
        ),
        ((1,), (1,)),
    )
    return product[:, : b.shape[0]] + product[:, b.shape[0] :]


def pair_routes(cols, picker, lines, tok_rows, slots):
    rows = cols.shape[0]
    weight_rows = contract(picker, cols, ((1,), (1,)))
    named = weight_rows > 0
    before = lax.broadcasted_iota(jnp.int32, (rows, rows), 0)
    after = lax.broadcasted_iota(jnp.int32, (rows, rows), 1)
    earlier = (before < after) & (before // tok_rows == after // tok_rows)
    rank = contract(
        jnp.where(named, 1.0, 0.0).astype(bf16),
        jnp.where(earlier, 1.0, 0.0).astype(bf16),
        ((1,), (0,)),
    )
    first_slot = lax.broadcasted_iota(jnp.int32, rank.shape, 1) // tok_rows * slots
    rank = jnp.where(named, rank.astype(jnp.int32) + first_slot, -1)
    slot = lax.broadcasted_iota(jnp.int32, (rows // tok_rows * slots, rows), 0)
    picks = [jnp.where(slot == rank[line : line + 1], 1.0, 0.0) for line in range(lines)]
    return weight_rows, picks


def collect_kernel(block_00, block_10, block_01, block_11, picker_ref, own_ref, send_ref, *, slots):
    local_experts, taken, width = own_ref.shape
    tok_rows = block_00.shape[0]
    pair = taken // 2
    for at, pair_refs in enumerate(((block_01, block_11), (block_00, block_10))):
        rows = jnp.concatenate([ref[...] for ref in pair_refs], axis=0)
        _, picks = pair_routes(
            rows[:, width:], picker_ref[...], 2 * local_experts, tok_rows, slots
        )
        picked = contract(
            jnp.concatenate(picks, axis=0).astype(bf16), rows[:, :width], ((1,), (0,))
        ).astype(bf16)
        for expert in range(local_experts):
            there = slice(at * pair, (at + 1) * pair)
            own_ref[expert, there, :] = picked[expert * pair : (expert + 1) * pair]
            line = local_experts + expert
            send_ref[expert, there, :] = picked[line * pair : (line + 1) * pair]


def expert_kernel(*refs):
    *row_refs, gate_ref, up_ref, down_ref, own_ref, send_ref = refs
    half = len(row_refs) // 2
    for sources, out_ref in ((row_refs[half:], send_ref), (row_refs[:half], own_ref)):
        rows = jnp.concatenate([ref[0] for ref in sources], axis=0)
        gate = contract(rows, gate_ref[0], ((1,), (0,)))
        up = contract(rows, up_ref[0], ((1,), (0,)))
        hidden = (gate / (1.0 + jnp.exp(-gate)) * up).astype(bf16)
        out_ref[0] = contract(hidden, down_ref[0], ((1,), (0,))).astype(bf16)


def spread_kernel(
    cols_00, cols_10, cols_01, cols_11, picker_ref, own_ref, got_ref, far_ref, near_ref, here_ref, *, slots
):
    local_experts, taken, _ = own_ref.shape
    tok_rows = cols_00.shape[0]
    pair = taken // 2
    for at, pair_refs in enumerate(((cols_01, cols_11), (cols_00, cols_10))):
        cols = jnp.concatenate([ref[...] for ref in pair_refs], axis=0)
        weight_rows, picks = pair_routes(
            cols, picker_ref[...], 2 * local_experts, tok_rows, slots
        )
        scaled = []
        for line, pick in enumerate(picks):
            result_ref = (own_ref, got_ref)[line // local_experts]
            result = result_ref[line % local_experts, at * pair : (at + 1) * pair, :]
            weight = jnp.sum(pick * weight_rows[line : line + 1], axis=1, keepdims=True)
            scaled.append((result.astype(f32) * weight).astype(bf16))
        summed = contract(
            jnp.concatenate(picks, axis=0).astype(bf16),
            jnp.concatenate(scaled, axis=0),
            ((0,), (0,)),
        ).astype(bf16)
        if at == 0:
            far_ref[...] = summed
        else:
            here_ref[...] = summed[:tok_rows]
            near_ref[...] = summed[tok_rows:]


def expert_layer_gathered(
    stream,
    moe_gain,
    router,
    expert_ids,
    expert_gate,
    expert_up,
    expert_down,
    sources,
):
    tok_rows, width = stream.shape
    local_experts, _, hidden_width = expert_gate.shape
    experts_all = local_experts * sources
    depth = sources // 8
    place = lax.axis_index(("ctx", "head"))

    def sent(value, move):
        pairs = []
        for device in range(sources):
            z, y, x, core = device // 8, device // 4 % 2, device // 2 % 2, device % 2
            z, y, x, core = move(z, y, x, core)
            pairs.append((device, ((z * 2 + y) * 2 + x) * 2 + core))
        return lax.ppermute(value, ("ctx", "head"), pairs)

    def lifted(value, steps):
        return sent(value, lambda z, y, x, core: ((z + steps) % depth, y, x, core))

    def first(value):
        return sent(value, lambda z, y, x, core: (z, y ^ (1 - core), x ^ core, core))

    def second(value):
        return sent(value, lambda z, y, x, core: (z, y ^ core, x ^ (1 - core), core))

    def swapped(value):
        return sent(value, lambda z, y, x, core: (z, y, x, 1 - core))

    normed = rms_rows(stream, moe_gain).astype(bf16)
    logits = jnp.dot(normed, router, preferred_element_type=f32)
    named = jnp.any(
        expert_ids[:, :, None] == jnp.arange(experts_all, dtype=jnp.int32)[None, None, :], axis=1
    )
    raised = jnp.where(named, jnp.exp(logits), 0.0)
    weights = raised / jnp.sum(raised, axis=1, keepdims=True)
    coarse = lax.reduce_precision(weights, 8, 7)
    packet = jnp.concatenate(
        [normed, coarse.astype(bf16), (weights - coarse).astype(bf16)], axis=1
    )

    capacity = (11 * tok_rows * expert_ids.shape[1] + 10 * experts_all - 1) // (10 * experts_all)
    slots = -(-capacity // 8) * 8
    taken = 4 * slots
    column = jnp.arange(2 * experts_all, dtype=jnp.int32)[None, :] % experts_all
    line = jnp.arange(16, dtype=jnp.int32)[:, None]
    owner = jnp.where(line < local_experts, place, place ^ 1)
    picker = (
        (line < 2 * local_experts) & (column == owner * local_experts + line % local_experts)
    ).astype(bf16)

    order = [0, *range(depth - 1, 0, -1)]
    own_rows, got_rows, outcome = {}, {}, {}
    blocks = {}
    mine = packet
    for at, steps in enumerate(order):
        if steps:
            source = packet if steps == 1 else mine
            earlier = [blocks[order[at - 1]][0]] if at > 1 else []
            if at > 1:
                earlier += blocks[order[at - 2]][1:3]
            if earlier:
                source = after(source, *earlier)
            mine = lifted(source, 1 if steps == 1 else -1)
        near = first(mine)
        blocks[steps] = (mine, near, second(mine), second(near))

    def collect(steps, *earlier):
        rows = blocks[steps][0]
        own, send = pl.pallas_call(
            functools.partial(collect_kernel, slots=slots),
            out_shape=[jax.ShapeDtypeStruct((local_experts, taken, width), bf16)] * 2,
            compiler_params=pltpu.CompilerParams(vmem_limit_bytes=48 << 20),
            cost_estimate=worth(2),
            name="collect",
        )(after(rows, *earlier) if earlier else rows, *blocks[steps][1:], picker)
        own_rows[steps] = own
        got_rows[steps] = swapped(send)

    def run_experts(members, *earlier):
        row_spec = pl.BlockSpec((1, taken, width), lambda e: (e, 0, 0))
        out_spec = pl.BlockSpec((1, len(members) * taken, width), lambda e: (e, 0, 0))
        results, send_back = pl.pallas_call(
            expert_kernel,
            grid=(local_experts,),
            in_specs=[row_spec] * (2 * len(members))
            + [
                pl.BlockSpec((1, width, hidden_width), lambda e: (e, 0, 0)),
                pl.BlockSpec((1, width, hidden_width), lambda e: (e, 0, 0)),
                pl.BlockSpec((1, hidden_width, width), lambda e: (e, 0, 0)),
            ],
            out_specs=[out_spec] * 2,
            out_shape=[jax.ShapeDtypeStruct((local_experts, len(members) * taken, width), bf16)]
            * 2,
            compiler_params=pltpu.CompilerParams(vmem_limit_bytes=56 << 20),
            cost_estimate=worth(4 + 3 * len(members)),
            name="experts",
        )(
            after(own_rows[members[0]], *earlier),
            *[own_rows[member] for member in members[1:]],
            *[got_rows[member] for member in members],
            expert_gate,
            expert_up,
            expert_down,
        )
        got_back = swapped(send_back)
        for at, member in enumerate(members):
            outcome[member] = (at, results, got_back)

    def spread(steps):
        at, results, got_back = outcome[steps]
        result_spec = pl.BlockSpec((local_experts, taken, width), lambda g: (0, at, 0))
        cols_spec = pl.BlockSpec(
            (tok_rows, 2 * experts_all), lambda g: (0, width // (2 * experts_all))
        )
        row_shape = jax.ShapeDtypeStruct((tok_rows, width), bf16)
        far_shape = jax.ShapeDtypeStruct((2 * tok_rows, width), bf16)
        return pl.pallas_call(
            functools.partial(spread_kernel, slots=slots),
            grid=(1,),
            in_specs=[cols_spec] * 4 + [whole_ref(picker), result_spec, result_spec],
            out_specs=[whole_ref(far_shape), whole_ref(row_shape), whole_ref(row_shape)],
            out_shape=[far_shape, row_shape, row_shape],
            compiler_params=pltpu.CompilerParams(vmem_limit_bytes=48 << 20),
            cost_estimate=worth(3),
            name="spread",
        )(*blocks[steps], picker, results, got_back)

    last = order[-1]
    for steps in order[:-2]:
        collect(steps, blocks[order[-2]][0])
    collect(order[-2])
    run_experts(order[:-1], blocks[last][1], blocks[last][2])
    back = order[-2:0:-1]
    ready = {steps: spread(steps) for steps in back}
    collect(last, *[far for far, _, _ in ready.values()])
    run_experts([last])
    back += [last, 0]
    carried = {}
    total = 0.0
    for at, steps in enumerate(back):
        far, near, here = ready[steps] if steps in ready else spread(steps)
        across = second(far)
        if at == 0:
            across = after(across, outcome[last][1])
        if at >= 2 and back[at - 2] in carried:
            across = after(across, carried[back[at - 2]])
        across = across.astype(f32)
        near = first((near.astype(f32) + across[tok_rows:]).astype(bf16))
        here = here.astype(f32) + across[:tok_rows] + near.astype(f32)
        if steps > 2:
            here += carried.pop(steps - 1).astype(f32)
        if steps:
            carried[steps] = lifted(here.astype(bf16), -1 if steps == 1 else 1)
        else:
            total = here
    for arrived in carried.values():
        total += arrived.astype(f32)
    return total.astype(bf16)


def expert_layer_sent(
    stream, moe_gain, router, expert_ids, expert_gate, expert_up, expert_down, sources
):
    tok_rows, model_width = stream.shape
    top_count = expert_ids.shape[1]
    local_experts = expert_gate.shape[0]
    experts_all = local_experts * sources
    capacity = (11 * tok_rows * top_count + 10 * experts_all - 1) // (10 * experts_all)
    normed = rms_rows(stream, moe_gain).astype(jnp.bfloat16)
    logits = jnp.dot(normed, router, preferred_element_type=jnp.float32)
    chosen = jnp.take_along_axis(logits, expert_ids, axis=1)
    raised = jnp.exp(chosen)
    weights = raised / jnp.sum(raised, axis=1, keepdims=True)
    flat_ids = expert_ids.reshape(-1)
    matches = (flat_ids[:, None] == jnp.arange(experts_all, dtype=jnp.int32)[None, :]).astype(
        jnp.int32
    )
    slot_index = jnp.sum((jnp.cumsum(matches, axis=0) - 1) * matches, axis=1)
    places = flat_ids * capacity + slot_index
    token_rows = jnp.arange(tok_rows * top_count, dtype=jnp.int32) // top_count
    outgoing = (
        jnp.zeros((experts_all * capacity, model_width), jnp.bfloat16)
        .at[places]
        .set(normed[token_rows])
    )
    outgoing = outgoing.reshape(sources, local_experts, capacity, model_width)
    received = lax.all_to_all(outgoing, ("ctx", "head"), split_axis=0, concat_axis=0, tiled=True)
    gate_part = jnp.einsum(
        "nesd,edh->nesh", received, expert_gate, preferred_element_type=jnp.float32
    )
    up_part = jnp.einsum("nesd,edh->nesh", received, expert_up, preferred_element_type=jnp.float32)
    hidden = (jax.nn.silu(gate_part) * up_part).astype(jnp.bfloat16)
    returned = lax.all_to_all(
        jnp.einsum(
            "nesh,ehd->nesd", hidden, expert_down, preferred_element_type=jnp.float32
        ).astype(jnp.bfloat16),
        ("ctx", "head"),
        split_axis=0,
        concat_axis=0,
        tiled=True,
    )
    gathered_rows = returned.reshape(experts_all * capacity, model_width)[places].reshape(
        tok_rows, top_count, model_width
    )
    return jnp.sum(weights[:, :, None] * gathered_rows.astype(jnp.float32), axis=1).astype(
        jnp.bfloat16
    )


def unit_inverses(strict_parts):
    size = strict_parts[0].shape[0]
    row = lax.broadcasted_iota(jnp.int32, (size, size), 0)
    col = lax.broadcasted_iota(jnp.int32, (size, size), 1)
    unit = jnp.where(row == col, 1.0, 0.0)
    joining = (row // 2 == col // 2) & (row != col)
    inverses = [unit - jnp.where(joining, part, 0.0) for part in strict_parts]
    half = 2
    while half < size:
        joining = (row // (2 * half) == col // (2 * half)) & (row // half != col // half)
        corners = [jnp.where(joining, part, 0.0) for part in strict_parts]
        if half < 8:
            steps = [contract_close(c, inverse) for c, inverse in zip(corners, inverses)]
            moves = [contract_close(inverse, step) for inverse, step in zip(inverses, steps)]
            inverses = [inverse - move for inverse, move in zip(inverses, moves)]
        else:
            starts = range(0, size, 2 * half)

            def lower_rows(array):
                return jnp.concatenate([array[at + half : at + 2 * half] for at in starts], axis=0)

            zeros = jnp.zeros((half, size), f32)
            steps = [
                contract_close(lower_rows(c), inverse) for c, inverse in zip(corners, inverses)
            ]
            steps = [
                jnp.concatenate(
                    [
                        piece
                        for at in range(0, size // 2, half)
                        for piece in (zeros, step[at : at + half])
                    ],
                    axis=0,
                )
                for step in steps
            ]
            lowers = [lower_rows(inverse) for inverse in inverses]
            lowers = [lower - contract_close(lower, step) for lower, step in zip(lowers, steps)]
            inverses = [
                jnp.concatenate(
                    [
                        piece
                        for at in starts
                        for piece in (
                            inverse[at : at + half],
                            lower[at // 2 : at // 2 + half],
                        )
                    ],
                    axis=0,
                )
                for inverse, lower in zip(inverses, lowers)
            ]
        half *= 2
    return inverses


def unit_rows(rows):
    return rows * lax.rsqrt(jnp.sum(rows * rows, axis=-1, keepdims=True) + epsilon)


def delta_kernel(
    raw_ref,
    rim_ref,
    taps_ref,
    small_ref,
    rate_ref,
    core_ref,
    reading_ref,
    moved_ref,
    extended,
    mixed,
    strengths,
    falls,
    carried,
    *,
    key_heads,
    chunk,
):
    rows, conv_cols = raw_ref.shape
    heads = moved_ref.shape[0]
    group = heads // key_heads
    tap_count = taps_ref.shape[0]
    rim = rim_ref.shape[0]
    extended[0:rim, :] = rim_ref[...]
    extended[rim : rim + rows, :] = raw_ref[...].astype(f32)
    key_at, value_at = key_heads * DK, 2 * key_heads * DK
    for start in range(0, rows, chunk):
        for first in range(0, conv_cols, DK):
            columns = slice(first, first + DK)
            summed = jnp.zeros((chunk, DK), f32)
            for tap in range(tap_count):
                offset = rim - (tap_count - 1) + start + tap
                summed += taps_ref[tap : tap + 1, columns] * extended[
                    offset : offset + chunk, columns
                ]
            value = summed / (1.0 + jnp.exp(-summed))
            if first < key_at:
                value = unit_rows(value) * DK**-0.5
            elif first < value_at:
                value = unit_rows(value)
            mixed[start : start + chunk, columns] = value
    strengths[...] = 1.0 / (1.0 + jnp.exp(-small_ref[:, :heads]))
    shifted = small_ref[:, heads:] + rate_ref[1:2, :]
    softened = jnp.maximum(shifted, 0.0) + jnp.log1p(jnp.exp(-jnp.abs(shifted)))
    falls[...] = -jnp.exp(rate_ref[0:1, :]) * softened

    row = lax.broadcasted_iota(jnp.int32, (chunk, chunk), 0)
    col = lax.broadcasted_iota(jnp.int32, (chunk, chunk), 1)
    inclusive, strict = row >= col, row > col
    lower = jnp.where(inclusive, 1.0, 0.0)
    across = lax.broadcasted_iota(jnp.int32, (DK, 2 * DK), 1)
    down = lax.broadcasted_iota(jnp.int32, (DK, 2 * DK), 0)
    carried[...] = jnp.broadcast_to(
        jnp.where(across == down + DK, 1.0, 0.0)[None], carried.shape
    )

    def advance(step, nothing):
        here = pl.ds(pl.multiple_of(step * chunk, chunk), chunk)
        fall = falls[here, :]
        strength = strengths[here, :]
        cumulative = contract(lower, fall, ((1,), (0,)), lax.Precision.HIGHEST)
        cumulative_rows = contract(fall, lower, ((0,), (1,)), lax.Precision.HIGHEST)
        owners = range(heads)
        queries = [mixed[here, k * DK : (k + 1) * DK] for k in range(key_heads)]
        keys = [mixed[here, key_at + k * DK : key_at + (k + 1) * DK] for k in range(key_heads)]
        dots = [
            contract_rows(jnp.concatenate([key, query], axis=0), key)
            for key, query in zip(keys, queries)
        ]
        totals = [cumulative[:, head : head + 1] for head in owners]
        kept = [
            jnp.where(
                inclusive,
                jnp.exp(jnp.where(inclusive, totals[head] - cumulative_rows[head : head + 1, :], 0.0)),
                0.0,
            )
            for head in owners
        ]
        own = [strength[:, head : head + 1] for head in owners]
        solvers = unit_inverses(
            [
                own[head] * jnp.where(strict, kept[head], 0.0) * dots[head // group][:chunk]
                for head in owners
            ]
        )
        risen = [jnp.exp(total) for total in totals]
        solved = [
            contract_close(
                solvers[head],
                own[head]
                * jnp.concatenate(
                    [
                        mixed[here, value_at + head * DK : value_at + (head + 1) * DK],
                        risen[head] * keys[head // group],
                    ],
                    axis=1,
                ),
            )
            for head in owners
        ]
        states = [carried[head] for head in owners]
        read = [
            contract_close(
                jnp.concatenate(
                    [solved[head][:, DK:], risen[head] * queries[head // group]], axis=0
                ),
                states[head],
            )
            for head in owners
        ]
        updates = [
            jnp.concatenate([solved[head][:, :DK], jnp.zeros((chunk, DK), f32)], axis=1)
            - read[head][:chunk]
            for head in owners
        ]
        for head in owners:
            last = totals[head][chunk - 1 :, :]
            leaving = jnp.exp(last - totals[head]) * keys[head // group]
            carried[head] = jnp.exp(last) * states[head] + contract_close(
                leaving.T, updates[head]
            )
        for head in owners:
            result = read[head][chunk:] + contract_close(
                kept[head] * dots[head // group][chunk:], updates[head]
            )
            core_ref[here, head * DK : (head + 1) * DK] = result[:, :DK]
            reading_ref[here, head * DK : (head + 1) * DK] = result[:, DK:]
        return nothing

    lax.fori_loop(0, rows // chunk, advance, 0)
    moved_ref[...] = carried[...].astype(bf16)


def project_kernel(place_ref, *refs, blocks):
    piece_refs, weight_refs, out_refs = refs[:blocks], refs[blocks : -3], refs[-3:]
    qkv_ref, gate_ref, small_ref = out_refs
    rows = jnp.concatenate([ref[...] for ref in piece_refs], axis=0)
    tok_rows = piece_refs[0].shape[0]

    def store(out_ref, first, weight_ref):
        product = contract(rows, weight_ref[...], ((1,), (0,))).astype(out_ref.dtype)
        for step in range(blocks):
            at = pl.multiple_of((place_ref[0] ^ step) * tok_rows, tok_rows)
            out_ref[pl.ds(at, tok_rows), first : first + product.shape[1]] = product[
                step * tok_rows : (step + 1) * tok_rows
            ]

    first = 0
    for weight_ref in weight_refs[:3]:
        store(qkv_ref, first, weight_ref)
        first += weight_ref.shape[1]
    store(gate_ref, 0, weight_refs[3])
    store(small_ref, 0, weight_refs[4])


def pair_kernel(second_ref, mine_ref, other_ref, moved_ref, transfer_ref):
    for head in range(mine_ref.shape[0]):
        mine, other = mine_ref[head].astype(f32), other_ref[head].astype(f32)
        late = second_ref[0] == 1
        earlier = jnp.where(late, other, mine).astype(bf16)
        later = jnp.where(late, mine, other)
        joined = contract(later[:, DK:].astype(bf16), earlier, ((1,), (0,)))
        moved_ref[head] = (joined[:, :DK] + later[:, :DK]).astype(bf16)
        transfer_ref[head] = joined[:, DK:].astype(bf16)


def finish_kernel(
    second_ref, state_ref, other_ref, core_ref, reading_ref, gate_ref, gain_ref, gated_ref
):
    states = []
    for head in range(state_ref.shape[0]):
        state = state_ref[head]
        passed = contract(other_ref[head, :, DK:], state, ((1,), (0,))) + other_ref[
            head, :, :DK
        ].astype(f32)
        states.append(jnp.where(second_ref[0] == 1, passed, state.astype(f32)))
    for head, state in enumerate(states):
        columns = slice(head * DK, (head + 1) * DK)
        core = core_ref[:, columns] + contract_close(reading_ref[:, columns], state)
        normal = (
            core
            * lax.rsqrt(jnp.mean(core * core, axis=-1, keepdims=True) + epsilon)
            * gain_ref[...]
        )
        gate = gate_ref[:, columns].astype(f32)
        gated_ref[:, columns] = (normal * (gate / (1.0 + jnp.exp(-gate)))).astype(bf16)


def output_kernel(*refs, blocks):
    row_refs, weight_refs, out_ref = refs[:blocks], refs[blocks:-1], refs[-1]
    total = 0.0
    pieces = iter(weight_refs)
    for rows_ref in row_refs:
        at = 0
        while at < rows_ref.shape[1]:
            weight_ref = next(pieces)
            depth = weight_ref.shape[0]
            total += contract(rows_ref[:, at : at + depth], weight_ref[...], ((1,), (0,)))
            at += depth
    out_ref[...] = total.astype(bf16)


def on_device(
    stream,
    moe_gain,
    router,
    expert_ids,
    expert_gate,
    expert_up,
    expert_down,
    mixer_gain,
    query_weight,
    key_weight,
    value_weight,
    output_gate,
    beta_weight,
    decay_weight,
    query_conv,
    key_conv,
    value_conv,
    decay_log,
    decay_bias,
    head_gain,
    out_weight,
):
    ctx_count = lax.axis_size("ctx")
    head_count = lax.axis_size("head")
    sources = ctx_count * head_count
    ctx_place = lax.axis_index("ctx")
    experts = (stream, moe_gain, router, expert_ids, expert_gate, expert_up, expert_down)
    if 2 * sources * stream.size <= GATHER_LIMIT and head_count == 4 and ctx_count in (6, 8):
        moe_out = expert_layer_gathered(*experts, sources)
    else:
        moe_out = expert_layer_sent(*experts, sources)
    mixer_in = rms_rows(
        stream.astype(jnp.float32) + moe_out.astype(jnp.float32), mixer_gain
    ).astype(jnp.bfloat16)
    head_place = lax.axis_index("head")

    def crossed(value, step):
        pairs = [(source, source ^ step) for source in range(head_count)]
        return lax.ppermute(value, "head", pairs)

    def from_all(value):
        across = [crossed(value, step) for step in range(2, head_count, 2)]
        received = [value, crossed(value, 1)]
        for part in across:
            received += [part, crossed(part, 1)]
        return received

    in_vmem = pl.BlockSpec(memory_space=pltpu.VMEM)
    in_smem = pl.BlockSpec(memory_space=pltpu.SMEM)
    tok_rows = stream.shape[0]
    rows = tok_rows * head_count
    key_cols, value_cols = query_weight.shape[1], value_weight.shape[1]
    heads = beta_weight.shape[1]
    pieces = from_all(mixer_in)
    qkv_raw, gate_raw, small_raw = pl.pallas_call(
        functools.partial(project_kernel, blocks=head_count),
        in_specs=[in_smem] + [in_vmem] * (head_count + 5),
        out_shape=[
            jax.ShapeDtypeStruct((rows, 2 * key_cols + value_cols), bf16),
            jax.ShapeDtypeStruct((rows, value_cols), bf16),
            jax.ShapeDtypeStruct((rows, 2 * heads), f32),
        ],
        compiler_params=pltpu.CompilerParams(vmem_limit_bytes=48 << 20),
        cost_estimate=worth(5),
        name="project",
    )(
        head_place.reshape(1),
        *pieces,
        query_weight,
        key_weight,
        value_weight,
        output_gate,
        jnp.concatenate([beta_weight, decay_weight], axis=1),
    )
    conv_cols = qkv_raw.shape[1]
    key_heads = key_cols // DK
    taps = jnp.concatenate([query_conv, key_conv, value_conv], axis=1)
    rim_len = taps.shape[0] - 1
    rim = passed_along(qkv_raw[rows - rim_len :], "ctx", 1)
    rim = jnp.concatenate([jnp.zeros((8 - rim_len, conv_cols), f32), rim.astype(f32)], axis=0)
    rates = jnp.stack([decay_log, decay_bias])
    chunk = math.gcd(rows, CHUNK)
    core, reading, moved = pl.pallas_call(
        functools.partial(delta_kernel, key_heads=key_heads, chunk=chunk),
        out_shape=(
            jax.ShapeDtypeStruct((rows, value_cols), f32),
            jax.ShapeDtypeStruct((rows, value_cols), f32),
            jax.ShapeDtypeStruct((heads, DK, 2 * DK), bf16),
        ),
        scratch_shapes=[
            pltpu.VMEM((rows + 8, conv_cols), f32),
            pltpu.VMEM((rows, conv_cols), f32),
            pltpu.VMEM((rows, heads), f32),
            pltpu.VMEM((rows, heads), f32),
            pltpu.VMEM((heads, DK, 2 * DK), f32),
        ],
        compiler_params=pltpu.CompilerParams(vmem_limit_bytes=48 << 20),
        cost_estimate=worth(16),
        name="delta",
    )(qkv_raw, rim, taps, small_raw, rates)
    half = out_weight.shape[0] // 2
    upper = [crossed(after(out_weight[:half], pieces[-1]), step) for step in range(2, head_count, 2)]
    moved = after(moved, *upper)
    lower = [crossed(after(out_weight[half:], moved), step) for step in range(2, head_count, 2)]

    in_pair = (ctx_place % 2).reshape(1)
    other = lax.ppermute(moved, "ctx", [(place, place ^ 1) for place in range(ctx_count)])
    state_shape = jax.ShapeDtypeStruct((heads, DK, DK), bf16)
    added, transfer = pl.pallas_call(
        pair_kernel,
        in_specs=[in_smem, in_vmem, in_vmem],
        out_shape=[state_shape, state_shape],
        compiler_params=pltpu.CompilerParams(vmem_limit_bytes=48 << 20),
        name="pair",
    )(in_pair, moved, other)
    state = passed_along(added, "ctx", 2)
    for hop in range(ctx_count // 2 - 2):
        leaving = jnp.einsum("hij,hjk->hik", transfer, state, preferred_element_type=f32)
        leaving = (leaving + added.astype(f32)).astype(bf16)
        if hop == ctx_count // 2 - 3:
            leaving = after(leaving, *lower)
        state = passed_along(leaving, "ctx", 2)

    gated = pl.pallas_call(
        finish_kernel,
        in_specs=[in_smem] + [in_vmem] * 6,
        out_shape=jax.ShapeDtypeStruct((rows, value_cols), bf16),
        compiler_params=pltpu.CompilerParams(vmem_limit_bytes=48 << 20),
        name="finish",
    )(in_pair, state, other, core, reading, gate_raw, head_gain.reshape(1, -1))
    gated_parts = []
    for step in range(head_count):
        part = lax.dynamic_slice_in_dim(gated, (head_place ^ step) * tok_rows, tok_rows, axis=0)
        gated_parts.append(crossed(part, step) if step else part)
    weight_parts = [out_weight, crossed(after(out_weight, moved), 1)]
    for near_pair in zip(upper, lower):
        weight_parts += near_pair
        weight_parts += [crossed(after(part, state), 1) for part in near_pair]
    mixer_out = pl.pallas_call(
        functools.partial(output_kernel, blocks=head_count),
        out_shape=jax.ShapeDtypeStruct(stream.shape, bf16),
        compiler_params=pltpu.CompilerParams(vmem_limit_bytes=48 << 20),
        name="output",
    )(*gated_parts, *weight_parts)
    return (moe_out, mixer_out)


def solution(mesh):
    return jax.shard_map(
        on_device,
        mesh=mesh,
        in_specs=(
            P(("ctx", "head"), None),
            P(),
            P(),
            P(("ctx", "head"), None),
            P(("ctx", "head"), None, None),
            P(("ctx", "head"), None, None),
            P(("ctx", "head"), None, None),
            P(),
            P(None, "head"),
            P(None, "head"),
            P(None, "head"),
            P(None, "head"),
            P(None, "head"),
            P(None, "head"),
            P(None, "head"),
            P(None, "head"),
            P(None, "head"),
            P("head"),
            P("head"),
            P(),
            P("head", None),
        ),
        out_specs=(P(("ctx", "head"), None), P(("ctx", "head"), None)),
        check_vma=False,
    )
```

profile of v0, /device:TPU:25, one launch (start us, length us, event | category | flops | bytes accessed | tf_op | source)
XLA Modules:
  0.0 315.5 jit_solution(10228409468418166451)
XLA Ops:
  7.5 12.7 %collective-permute-done.3.block_00.cols_00 = bf16[128,2176]{1,0:T(8,128)(2,1)S(1)} collective-permute-done((bf16[128,2176]{1,0:T(8,128)(2,1)S(1)}, bf16[128,2176]{1,0:T(8,128)(2,1)S(1)}, u32[]{:S(2)}, u32[]{:S(2)}) %collective-permute-start.3) | collective-permute-done | bytes 557088 | tf_op jit(solution)/shard_map/ppermute | solution.py:185
  21.4 14.2 %collective-permute-done.4.block_00.cols_00 = bf16[128,2176]{1,0:T(8,128)(2,1)} collective-permute-done((bf16[128,2176]{1,0:T(8,128)(2,1)S(1)}, bf16[128,2176]{1,0:T(8,128)(2,1)}, u32[]{:S(2)}, u32[]{:S(2)}) %collective-permute-start.4) | collective-permute-done | bytes 557088 | tf_op jit(solution)/shard_map/ppermute | solution.py:185
  38.9 8.0 %collective-permute-done.11.block_10.cols_10 = bf16[128,2176]{1,0:T(8,128)(2,1)} collective-permute-done((bf16[128,2176]{1,0:T(8,128)(2,1)}, bf16[128,2176]{1,0:T(8,128)(2,1)}, u32[]{:S(2)}, u32[]{:S(2)}) %collective-permute-start.11) | collective-permute-done | bytes 557088 | tf_op jit(solution)/shard_map/ppermute | solution.py:185
  46.9 2.3 collective-permute-start.13
  49.2 7.3 %collective-permute-done.6.block_01.cols_01 = bf16[128,2176]{1,0:T(8,128)(2,1)S(1)} collective-permute-done((bf16[128,2176]{1,0:T(8,128)(2,1)S(1)}, bf16[128,2176]{1,0:T(8,128)(2,1)S(1)}, u32[]{:S(2)}, u32[]{:S(2)}) %collective-permute-start.6) | collective-permute-done | bytes 557088 | tf_op jit(solution)/shard_map/ppermute | solution.py:185
  57.3 1.6 collective-permute-start.7
  62.5 2.3 collect.5
  66.2 2.2 collective-permute-done.12.block_01.cols_01
  68.4 6.0 %collective-permute-done.13.block_11.cols_11 = bf16[128,2176]{1,0:T(8,128)(2,1)S(1)} collective-permute-done((bf16[128,2176]{1,0:T(8,128)(2,1)}, bf16[128,2176]{1,0:T(8,128)(2,1)S(1)}, u32[]{:S(2)}, u32[]{:S(2)}) %collective-permute-start.13) | collective-permute-done | bytes 557088 | tf_op jit(solution)/shard_map/ppermute | solution.py:185
  74.4 2.5 collect.6
  80.1 10.8 %collective-permute-done.8.block_10.cols_10 = bf16[128,2176]{1,0:T(8,128)(2,1)} collective-permute-done((bf16[128,2176]{1,0:T(8,128)(2,1)S(1)}, bf16[128,2176]{1,0:T(8,128)(2,1)}, u32[]{:S(2)}, u32[]{:S(2)}) %collective-permute-start.8) | collective-permute-done | bytes 557088 | tf_op jit(solution)/shard_map/ppermute | solution.py:185
  90.9 2.6 collective-permute-done.9.block_01.cols_01
  95.8 12.7 %experts.2 = (bf16[2,288,2048]{2,1,0:T(8,128)(2,1)}, bf16[2,288,2048]{2,1,0:T(8,128)(2,1)}) custom-call(bf16[2,96,2048]{2,1,0:T(8,128)(2,1)} %copy-done.21, bf16[2,96,2048]{2,1,0:T(8,128)(2,1)} %copy-done.22, bf16[2,96,2048]{2,1,0:T(8,128)(2,1)} %copy-done.23, bf16[2,96,2048]{2,1,0:T(8,128)(2,1)} %copy-done.37, bf16[2,96,2048]{2,1,0:T(8,128)(2,1)} %copy-done.38, ...), custom_call_target="tpu_custom_call" | custom-call | flops 14949999616 | bytes 13000000 | tf_op jit(solution)/shard_map/experts/pallas_call | solution.py:252
  110.1 3.2 %collective-permute-done.17.got_ref = bf16[2,288,2048]{2,1,0:T(8,128)(2,1)S(1)} collective-permute-done((bf16[2,288,2048]{2,1,0:T(8,128)(2,1)}, bf16[2,288,2048]{2,1,0:T(8,128)(2,1)S(1)}, u32[]{:S(2)}, u32[]{:S(2)}) %collective-permute-start.17) | collective-permute-done | bytes 2359328 | tf_op jit(solution)/shard_map/ppermute | solution.py:185
  114.7 3.0 spread.5
  117.8 2.9 spread.6
  120.7 2.3 collect.7
  126.4 8.6 %experts.3 = (bf16[2,96,2048]{2,1,0:T(8,128)(2,1)}, bf16[2,96,2048]{2,1,0:T(8,128)(2,1)}) custom-call(bf16[2,96,2048]{2,1,0:T(8,128)(2,1)} %copy-done.24, bf16[2,96,2048]{2,1,0:T(8,128)(2,1)} %collective-permute-done.23.refs_1_, bf16[2,2048,512]{2,1,0:T(8,128)(2,1)} %refs_2_.1, bf16[2,2048,512]{2,1,0:T(8,128)(2,1)} %refs_3_.1, bf16[2,512,2048]{2,1,0:T(8,128)(2,1)} %refs_4_.3), custom_call_target="tpu_custom_call" | custom-call | flops 8049999872 | bytes 7000000 | tf_op jit(solution)/shard_map/experts/pallas_call | solution.py:252
  135.0 3.4 %collective-permute-done.21 = bf16[256,2048]{1,0:T(8,128)(2,1)} collective-permute-done((bf16[256,2048]{1,0:T(8,128)(2,1)S(1)}, bf16[256,2048]{1,0:T(8,128)(2,1)}, u32[]{:S(2)}, u32[]{:S(2)}) %collective-permute-start.21) | collective-permute-done | bytes 1048608 | tf_op jit(solution)/shard_map/ppermute | solution.py:185
  138.4 1.5 convert_element_type.126
  142.6 12.2 %collective-permute-done.19 = bf16[256,2048]{1,0:T(8,128)(2,1)} collective-permute-done((bf16[256,2048]{1,0:T(8,128)(2,1)S(1)}, bf16[256,2048]{1,0:T(8,128)(2,1)}, u32[]{:S(2)}, u32[]{:S(2)}) %collective-permute-start.19) | collective-permute-done | bytes 1048608 | tf_op jit(solution)/shard_map/ppermute | solution.py:185
  158.4 2.0 collective-permute-start.25
  160.4 2.2 spread.7
  163.9 2.8 spread.4
  167.1 2.9 collective-permute-done.25
  170.4 3.7 %collective-permute-start.26 = (bf16[128,2048]{1,0:T(8,128)(2,1)S(1)}, bf16[128,2048]{1,0:T(8,128)(2,1)S(1)}, u32[]{:S(2)}, u32[]{:S(2)}) collective-permute-start(bf16[128,2048]{1,0:T(8,128)(2,1)S(1)} %fusion.20), channel_id=1, source_target_pairs={{0,8},{1,9},{2,10},{3,11},{4,12},{5,13},{6,14},{7,15},{8,16},{9,17... | collective-permute-start | bytes 1572872 | tf_op jit(solution)/shard_map/ppermute | solution.py:185
  174.0 4.8 %collective-permute-done.29 = bf16[256,2048]{1,0:T(8,128)(2,1)S(1)} collective-permute-done((bf16[256,2048]{1,0:T(8,128)(2,1)S(1)}, bf16[256,2048]{1,0:T(8,128)(2,1)S(1)}, u32[]{:S(2)}, u32[]{:S(2)}) %collective-permute-start.29) | collective-permute-done | bytes 1048608 | tf_op jit(solution)/shard_map/ppermute | solution.py:185
  180.3 15.4 %collective-permute-done.18 = bf16[256,2048]{1,0:T(8,128)(2,1)S(1)} collective-permute-done((bf16[256,2048]{1,0:T(8,128)(2,1)S(1)}, bf16[256,2048]{1,0:T(8,128)(2,1)S(1)}, u32[]{:S(2)}, u32[]{:S(2)}) %collective-permute-start.18) | collective-permute-done | bytes 1048608 | tf_op jit(solution)/shard_map/ppermute | solution.py:185
  197.4 7.1 %collective-permute-done.27 = bf16[128,2048]{1,0:T(8,128)(2,1)S(1)} collective-permute-done((bf16[128,2048]{1,0:T(8,128)(2,1)S(1)}, bf16[128,2048]{1,0:T(8,128)(2,1)S(1)}, u32[]{:S(2)}, u32[]{:S(2)}) %collective-permute-start.27) | collective-permute-done | bytes 524320 | tf_op jit(solution)/shard_map/ppermute | solution.py:185
  204.5 7.8 %collective-permute-done.31 = bf16[128,2048]{1,0:T(8,128)(2,1)S(1)} collective-permute-done((bf16[128,2048]{1,0:T(8,128)(2,1)S(1)}, bf16[128,2048]{1,0:T(8,128)(2,1)S(1)}, u32[]{:S(2)}, u32[]{:S(2)}) %collective-permute-start.31) | collective-permute-done | bytes 524320 | tf_op jit(solution)/shard_map/ppermute | solution.py:185
  214.1 1.7 collective-permute-start.32
  215.7 9.7 %collective-permute-done.33.refs_2_ = bf16[128,2048]{1,0:T(8,128)(2,1)S(1)} collective-permute-done((bf16[128,2048]{1,0:T(8,128)(2,1)S(1)}, bf16[128,2048]{1,0:T(8,128)(2,1)S(1)}, u32[]{:S(2)}, u32[]{:S(2)}) %collective-permute-start.33) | collective-permute-done | bytes 524320 | tf_op jit(solution)/shard_map/ppermute | solution.py:681
  225.5 2.2 collective-permute-start.34
  227.6 2.8 fusion.26
  230.4 6.5 %project.1 = (bf16[512,1024]{1,0:T(8,128)(2,1)S(1)}, bf16[512,512]{1,0:T(8,128)(2,1)S(1)}, f32[512,8]{1,0:T(8,128)S(1)}) custom-call(s32[1]{0:T(128)} %bitcast.1.place_ref, bf16[128,2048]{1,0:T(8,128)(2,1)S(1)} %multiply_convert_fusion.refs_0_, bf16[128,2048]{1,0:T(8,128)(2,1)S(1)} %collective-permute-done.32.refs_1_, ...), custom_call_target="tpu_custom_call" | custom-call | flops 5750000128 | bytes 5000000 | tf_op jit(solution)/shard_map/project/pallas_call | solution.py:697
  237.8 2.8 collective-permute-start.35
  240.7 2.4 collective-permute-done.35
  243.1 15.7 %delta.1 = (f32[512,512]{1,0:T(8,128)S(1)}, f32[512,512]{1,0:T(8,128)S(1)}, bf16[4,128,256]{2,1,0:T(8,128)(2,1)S(1)}) custom-call(bf16[512,1024]{1,0:T(8,128)(2,1)S(1)} %get-tuple-element.81.raw_ref, f32[8,1024]{1,0:T(8,128)S(1)} %pad_convert_fusion.rim_ref, f32[4,1024]{1,0:T(4,128)S(1)} %pad_maximum_fusion.1.taps_ref, ...), custom_call_target="tpu_custom_call" | custom-call | flops 18400000000 | bytes 16000000 | tf_op jit(solution)/shard_map/delta/pallas_call | solution.py:725
  260.8 4.3 %collective-permute-done.36.refs_6_ = bf16[256,2048]{1,0:T(8,128)(2,1)S(1)} collective-permute-done((bf16[256,2048]{1,0:T(8,128)(2,1)S(1)}, bf16[256,2048]{1,0:T(8,128)(2,1)S(1)}, u32[]{:S(2)}, u32[]{:S(2)}) %collective-permute-start.36) | collective-permute-done | bytes 1048608 | tf_op jit(solution)/shard_map/ppermute | solution.py:681
  266.5 5.0 %collective-permute-done.37.other_ref = bf16[4,128,256]{2,1,0:T(8,128)(2,1)S(1)} collective-permute-done((bf16[4,128,256]{2,1,0:T(8,128)(2,1)S(1)}, bf16[4,128,256]{2,1,0:T(8,128)(2,1)S(1)}, u32[]{:S(2)}, u32[]{:S(2)}) %collective-permute-start.37) | collective-permute-done | bytes 262176 | tf_op jit(solution)/shard_map/ppermute | solution.py:749
  273.1 4.7 %collective-permute-done.38 = bf16[4,128,128]{2,1,0:T(8,128)(2,1)S(1)} collective-permute-done((bf16[4,128,128]{2,1,0:T(8,128)(2,1)S(1)}, bf16[4,128,128]{2,1,0:T(8,128)(2,1)S(1)}, u32[]{:S(2)}, u32[]{:S(2)}) %collective-permute-start.38) | collective-permute-done | bytes 131104 | tf_op jit(solution)/shard_map/ppermute | solution.py:24
  279.3 4.7 %collective-permute-done.39 = bf16[4,128,128]{2,1,0:T(8,128)(2,1)S(1)} collective-permute-done((bf16[4,128,128]{2,1,0:T(8,128)(2,1)S(1)}, bf16[4,128,128]{2,1,0:T(8,128)(2,1)S(1)}, u32[]{:S(2)}, u32[]{:S(2)}) %collective-permute-start.39) | collective-permute-done | bytes 131104 | tf_op jit(solution)/shard_map/ppermute | solution.py:24
  284.2 4.7 %collective-permute-done.40.refs_7_ = bf16[256,2048]{1,0:T(8,128)(2,1)S(1)} collective-permute-done((bf16[256,2048]{1,0:T(8,128)(2,1)}, bf16[256,2048]{1,0:T(8,128)(2,1)S(1)}, u32[]{:S(2)}, u32[]{:S(2)}) %collective-permute-start.40) | collective-permute-done | bytes 1048608 | tf_op jit(solution)/shard_map/ppermute | solution.py:681
  290.2 4.4 %collective-permute-done.41.state_ref = bf16[4,128,128]{2,1,0:T(8,128)(2,1)S(1)} collective-permute-done((bf16[4,128,128]{2,1,0:T(8,128)(2,1)S(1)}, bf16[4,128,128]{2,1,0:T(8,128)(2,1)S(1)}, u32[]{:S(2)}, u32[]{:S(2)}) %collective-permute-start.41) | collective-permute-done | bytes 131104 | tf_op jit(solution)/shard_map/ppermute | solution.py:24
  294.6 3.2 %collective-permute-start.47 = (bf16[256,2048]{1,0:T(8,128)(2,1)S(1)}, bf16[256,2048]{1,0:T(8,128)(2,1)S(1)}, u32[]{:S(2)}, u32[]{:S(2)}) collective-permute-start(bf16[256,2048]{1,0:T(8,128)(2,1)S(1)} %collective-permute-done.40.refs_7_), channel_id=1, source_target_pairs={{0,1},{1,0},{2,3},{3,2},{4,5},{5,4},{6,7},{7,6},{8,9},{9,8},{10,11... | collective-permute-start | bytes 3145736 | tf_op jit(solution)/shard_map/ppermute | solution.py:681
  304.6 3.4 %collective-permute-done.43.refs_2_ = bf16[128,512]{1,0:T(8,128)(2,1)S(1)} collective-permute-done((bf16[128,512]{1,0:T(8,128)(2,1)S(1)}, bf16[128,512]{1,0:T(8,128)(2,1)S(1)}, u32[]{:S(2)}, u32[]{:S(2)}) %collective-permute-start.43) | collective-permute-done | bytes 131104 | tf_op jit(solution)/shard_map/ppermute | solution.py:681
  308.0 3.0 collective-permute-done.44.refs_3_
  311.0 4.6 %output.1 = bf16[128,2048]{1,0:T(8,128)(2,1)} custom-call(bf16[128,512]{1,0:T(8,128)(2,1)S(1)} %get-tuple-element.103.refs_0_, bf16[128,512]{1,0:T(8,128)(2,1)S(1)} %collective-permute-done.42.refs_1_, bf16[128,512]{1,0:T(8,128)(2,1)S(1)} %collective-permute-done.43.refs_2_, bf16[128,512]{1,0:T(8,128)(2,1)S(1)} %collective-permute-done.44.refs_3_, ...), custom_call_target="tpu_custom_call" | custom-call | tf_op jit(solution)/shard_map/output/pallas_call | solution.py:781
  (181 shorter events, 57.3 us)
Async XLA Ops:
  4.8 15.3 %collective-permute-start.3 = (bf16[128,2176]{1,0:T(8,128)(2,1)S(1)}, bf16[128,2176]{1,0:T(8,128)(2,1)S(1)}, u32[]{:S(2)}, u32[]{:S(2)}) collective-permute-start(bf16[128,2176]{1,0:T(8,128)(2,1)S(1)} %concatenate.14.block_00.cols_00), channel_id=1, source_target_pairs={{0,24},{1,25},{2,26},{3,27},{4,28},{5,29},{6,30},{7,31},{8,0},{9,1... | collective-permute-start | bytes 1671176 | tf_op jit(solution)/shard_map/ppermute | solution.py:185
  5.0 15.1 %collective-permute-start = (bf16[128,2176]{1,0:T(8,128)(2,1)S(1)}, bf16[128,2176]{1,0:T(8,128)(2,1)S(1)}, u32[]{:S(2)}, u32[]{:S(2)}) collective-permute-start(bf16[128,2176]{1,0:T(8,128)(2,1)S(1)} %concatenate.14.block_00.cols_00), channel_id=1, source_target_pairs={{0,4},{1,3},{2,6},{3,1},{4,0},{5,7},{6,2},{7,5},{8,12},{9,11},{10,... | collective-permute-start | bytes 1671176 | tf_op jit(solution)/shard_map/ppermute | solution.py:185
  6.2 14.4 %collective-permute-start.1 = (bf16[128,2176]{1,0:T(8,128)(2,1)S(1)}, bf16[128,2176]{1,0:T(8,128)(2,1)S(1)}, u32[]{:S(2)}, u32[]{:S(2)}) collective-permute-start(bf16[128,2176]{1,0:T(8,128)(2,1)S(1)} %concatenate.14.block_00.cols_00), channel_id=1, source_target_pairs={{0,2},{1,5},{2,0},{3,7},{4,6},{5,1},{6,4},{7,3},{8,10},{9,13},{10,... | collective-permute-start | bytes 1671176 | tf_op jit(solution)/shard_map/ppermute | solution.py:185
  20.7 15.0 %collective-permute-start.4 = (bf16[128,2176]{1,0:T(8,128)(2,1)S(1)}, bf16[128,2176]{1,0:T(8,128)(2,1)}, u32[]{:S(2)}, u32[]{:S(2)}) collective-permute-start(bf16[128,2176]{1,0:T(8,128)(2,1)S(1)} %collective-permute-done.3.block_00.cols_00), channel_id=1, source_target_pairs={{0,24},{1,25},{2,26},{3,27},{4,28},{5,29},{6,30},{7,31},{8,0},{9,1... | collective-permute-start | bytes 1671176 | tf_op jit(solution)/shard_map/ppermute | solution.py:185
  20.8 16.5 %collective-permute-start.5 = (bf16[128,2176]{1,0:T(8,128)(2,1)S(1)}, bf16[128,2176]{1,0:T(8,128)(2,1)}, u32[]{:S(2)}, u32[]{:S(2)}) collective-permute-start(bf16[128,2176]{1,0:T(8,128)(2,1)S(1)} %collective-permute-done.3.block_00.cols_00), channel_id=1, source_target_pairs={{0,4},{1,3},{2,6},{3,1},{4,0},{5,7},{6,2},{7,5},{8,12},{9,11},{10,... | collective-permute-start | bytes 1671176 | tf_op jit(solution)/shard_map/ppermute | solution.py:185
  35.7 11.2 %collective-permute-start.11 = (bf16[128,2176]{1,0:T(8,128)(2,1)}, bf16[128,2176]{1,0:T(8,128)(2,1)}, u32[]{:S(2)}, u32[]{:S(2)}) collective-permute-start(bf16[128,2176]{1,0:T(8,128)(2,1)} %collective-permute-done.4.block_00.cols_00), channel_id=1, source_target_pairs={{0,4},{1,3},{2,6},{3,1},{4,0},{5,7},{6,2},{7,5},{8,12},{9,11},{10,... | collective-permute-start | bytes 1671176 | tf_op jit(solution)/shard_map/ppermute | solution.py:185
  35.9 23.0 %collective-permute-start.2 = (bf16[128,2176]{1,0:T(8,128)(2,1)S(1)}, bf16[128,2176]{1,0:T(8,128)(2,1)S(1)}, u32[]{:S(2)}, u32[]{:S(2)}) collective-permute-start(bf16[128,2176]{1,0:T(8,128)(2,1)S(1)} %collective-permute-done.block_10.cols_10), channel_id=1, source_target_pairs={{0,2},{1,5},{2,0},{3,7},{4,6},{5,1},{6,4},{7,3},{8,10},{9,13},{10,... | collective-permute-start | bytes 1671176 | tf_op jit(solution)/shard_map/ppermute | solution.py:185
  37.1 19.4 %collective-permute-start.6 = (bf16[128,2176]{1,0:T(8,128)(2,1)S(1)}, bf16[128,2176]{1,0:T(8,128)(2,1)S(1)}, u32[]{:S(2)}, u32[]{:S(2)}) collective-permute-start(bf16[128,2176]{1,0:T(8,128)(2,1)S(1)} %collective-permute-done.3.block_00.cols_00), channel_id=1, source_target_pairs={{0,2},{1,5},{2,0},{3,7},{4,6},{5,1},{6,4},{7,3},{8,10},{9,13},{10,... | collective-permute-start | bytes 1671176 | tf_op jit(solution)/shard_map/ppermute | solution.py:185
  37.3 25.2 %collective-permute-start.10 = (bf16[128,2176]{1,0:T(8,128)(2,1)}, bf16[128,2176]{1,0:T(8,128)(2,1)}, u32[]{:S(2)}, u32[]{:S(2)}) collective-permute-start(bf16[128,2176]{1,0:T(8,128)(2,1)} %collective-permute-done.5.block_10.cols_10), channel_id=1, source_target_pairs={{0,2},{1,5},{2,0},{3,7},{4,6},{5,1},{6,4},{7,3},{8,10},{9,13},{10,... | collective-permute-start | bytes 1671176 | tf_op jit(solution)/shard_map/ppermute | solution.py:185
  38.6 29.9 %collective-permute-start.12 = (bf16[128,2176]{1,0:T(8,128)(2,1)}, bf16[128,2176]{1,0:T(8,128)(2,1)S(1)}, u32[]{:S(2)}, u32[]{:S(2)}) collective-permute-start(bf16[128,2176]{1,0:T(8,128)(2,1)} %collective-permute-done.4.block_00.cols_00), channel_id=1, source_target_pairs={{0,2},{1,5},{2,0},{3,7},{4,6},{5,1},{6,4},{7,3},{8,10},{9,13},{10,... | collective-permute-start | bytes 1671176 | tf_op jit(solution)/shard_map/ppermute | solution.py:185
  46.9 27.5 %collective-permute-start.13 = (bf16[128,2176]{1,0:T(8,128)(2,1)}, bf16[128,2176]{1,0:T(8,128)(2,1)S(1)}, u32[]{:S(2)}, u32[]{:S(2)}) collective-permute-start(bf16[128,2176]{1,0:T(8,128)(2,1)} %collective-permute-done.11.block_10.cols_10), channel_id=1, source_target_pairs={{0,2},{1,5},{2,0},{3,7},{4,6},{5,1},{6,4},{7,3},{8,10},{9,13},{10,... | collective-permute-start | bytes 1671176 | tf_op jit(solution)/shard_map/ppermute | solution.py:185
  57.3 21.0 %collective-permute-start.7 = (bf16[128,2176]{1,0:T(8,128)(2,1)S(1)}, bf16[128,2176]{1,0:T(8,128)(2,1)S(1)}, u32[]{:S(2)}, u32[]{:S(2)}) collective-permute-start(bf16[128,2176]{1,0:T(8,128)(2,1)S(1)} %concatenate.14.block_00.cols_00), channel_id=1, source_target_pairs={{0,8},{1,9},{2,10},{3,11},{4,12},{5,13},{6,14},{7,15},{8,16},{9,17... | collective-permute-start | bytes 1671176 | tf_op jit(solution)/shard_map/ppermute | solution.py:185
  60.9 33.5 %collective-permute-start.14 = (bf16[2,96,2048]{2,1,0:T(8,128)(2,1)S(1)}, bf16[2,96,2048]{2,1,0:T(8,128)(2,1)S(1)}, u32[]{:S(2)}, u32[]{:S(2)}) collective-permute-start(bf16[2,96,2048]{2,1,0:T(8,128)(2,1)S(1)} %get-tuple-element.57), channel_id=1, source_target_pairs={{0,1},{1,0},{2,3},{3,2},{4,5},{5,4},{6,7},{7,6},{8,9},{9,8},{10,11... | collective-permute-start | bytes 2359304 | tf_op jit(solution)/shard_map/ppermute | solution.py:185
  65.7 28.7 %collective-permute-start.15 = (bf16[2,96,2048]{2,1,0:T(8,128)(2,1)S(1)}, bf16[2,96,2048]{2,1,0:T(8,128)(2,1)S(1)}, u32[]{:S(2)}, u32[]{:S(2)}) collective-permute-start(bf16[2,96,2048]{2,1,0:T(8,128)(2,1)S(1)} %get-tuple-element.58), channel_id=1, source_target_pairs={{0,1},{1,0},{2,3},{3,2},{4,5},{5,4},{6,7},{7,6},{8,9},{9,8},{10,11... | collective-permute-start | bytes 2359304 | tf_op jit(solution)/shard_map/ppermute | solution.py:185
  77.8 16.6 %collective-permute-start.16 = (bf16[2,96,2048]{2,1,0:T(8,128)(2,1)S(1)}, bf16[2,96,2048]{2,1,0:T(8,128)(2,1)S(1)}, u32[]{:S(2)}, u32[]{:S(2)}) collective-permute-start(bf16[2,96,2048]{2,1,0:T(8,128)(2,1)S(1)} %get-tuple-element.59), channel_id=1, source_target_pairs={{0,1},{1,0},{2,3},{3,2},{4,5},{5,4},{6,7},{7,6},{8,9},{9,8},{10,11... | collective-permute-start | bytes 2359304 | tf_op jit(solution)/shard_map/ppermute | solution.py:185
  78.3 12.7 %collective-permute-start.8 = (bf16[128,2176]{1,0:T(8,128)(2,1)S(1)}, bf16[128,2176]{1,0:T(8,128)(2,1)}, u32[]{:S(2)}, u32[]{:S(2)}) collective-permute-start(bf16[128,2176]{1,0:T(8,128)(2,1)S(1)} %collective-permute-done.7.block_00.cols_00), channel_id=1, source_target_pairs={{0,4},{1,3},{2,6},{3,1},{4,0},{5,7},{6,2},{7,5},{8,12},{9,11},{10,... | collective-permute-start | bytes 1671176 | tf_op jit(solution)/shard_map/ppermute | solution.py:185
  78.8 14.7 %collective-permute-start.9 = (bf16[128,2176]{1,0:T(8,128)(2,1)S(1)}, bf16[128,2176]{1,0:T(8,128)(2,1)S(1)}, u32[]{:S(2)}, u32[]{:S(2)}) collective-permute-start(bf16[128,2176]{1,0:T(8,128)(2,1)S(1)} %collective-permute-done.7.block_00.cols_00), channel_id=1, source_target_pairs={{0,2},{1,5},{2,0},{3,7},{4,6},{5,1},{6,4},{7,3},{8,10},{9,13},{10,... | collective-permute-start | bytes 1671176 | tf_op jit(solution)/shard_map/ppermute | solution.py:185
  108.5 4.8 %collective-permute-start.17 = (bf16[2,288,2048]{2,1,0:T(8,128)(2,1)}, bf16[2,288,2048]{2,1,0:T(8,128)(2,1)S(1)}, u32[]{:S(2)}, u32[]{:S(2)}) collective-permute-start(bf16[2,288,2048]{2,1,0:T(8,128)(2,1)} %get-tuple-element.61), channel_id=1, source_target_pairs={{0,1},{1,0},{2,3},{3,2},{4,5},{5,4},{6,7},{7,6},{8,9},{9,8},{10,11... | collective-permute-start | bytes 7077896 | tf_op jit(solution)/shard_map/ppermute | solution.py:185
  108.9 11.8 %collective-permute-start.22 = (bf16[128,2176]{1,0:T(8,128)(2,1)}, bf16[128,2176]{1,0:T(8,128)(2,1)S(1)}, u32[]{:S(2)}, u32[]{:S(2)}) collective-permute-start(bf16[128,2176]{1,0:T(8,128)(2,1)} %collective-permute-done.8.block_10.cols_10), channel_id=1, source_target_pairs={{0,2},{1,5},{2,0},{3,7},{4,6},{5,1},{6,4},{7,3},{8,10},{9,13},{10,... | collective-permute-start | bytes 1671176 | tf_op jit(solution)/shard_map/ppermute | solution.py:185
  124.0 2.4 collective-permute-start.23
  124.3 14.0 %collective-permute-start.21 = (bf16[256,2048]{1,0:T(8,128)(2,1)S(1)}, bf16[256,2048]{1,0:T(8,128)(2,1)}, u32[]{:S(2)}, u32[]{:S(2)}) collective-permute-start(bf16[256,2048]{1,0:T(8,128)(2,1)S(1)} %get-tuple-element.68), channel_id=1, source_target_pairs={{0,2},{1,5},{2,0},{3,7},{4,6},{5,1},{6,4},{7,3},{8,10},{9,13},{10,... | collective-permute-start | bytes 3145736 | tf_op jit(solution)/shard_map/ppermute | solution.py:185
  125.5 29.3 %collective-permute-start.19 = (bf16[256,2048]{1,0:T(8,128)(2,1)S(1)}, bf16[256,2048]{1,0:T(8,128)(2,1)}, u32[]{:S(2)}, u32[]{:S(2)}) collective-permute-start(bf16[256,2048]{1,0:T(8,128)(2,1)S(1)} %get-tuple-element.65), channel_id=1, source_target_pairs={{0,2},{1,5},{2,0},{3,7},{4,6},{5,1},{6,4},{7,3},{8,10},{9,13},{10,... | collective-permute-start | bytes 3145736 | tf_op jit(solution)/shard_map/ppermute | solution.py:185
  140.1 18.1 %collective-permute-start.24 = (bf16[128,2048]{1,0:T(8,128)(2,1)S(1)}, bf16[128,2048]{1,0:T(8,128)(2,1)S(1)}, u32[]{:S(2)}, u32[]{:S(2)}) collective-permute-start(bf16[128,2048]{1,0:T(8,128)(2,1)S(1)} %fusion.14), channel_id=1, source_target_pairs={{0,4},{1,3},{2,6},{3,1},{4,0},{5,7},{6,2},{7,5},{8,12},{9,11},{10,... | collective-permute-start | bytes 1572872 | tf_op jit(solution)/shard_map/ppermute | solution.py:185
  141.1 19.3 %collective-permute-start.28 = (bf16[2,96,2048]{2,1,0:T(8,128)(2,1)S(1)}, bf16[2,96,2048]{2,1,0:T(8,128)(2,1)S(1)}, u32[]{:S(2)}, u32[]{:S(2)}) collective-permute-start(bf16[2,96,2048]{2,1,0:T(8,128)(2,1)S(1)} %copy-done.39), channel_id=1, source_target_pairs={{0,1},{1,0},{2,3},{3,2},{4,5},{5,4},{6,7},{7,6},{8,9},{9,8},{10,11... | collective-permute-start | bytes 2359304 | tf_op jit(solution)/shard_map/ppermute | solution.py:185
  157.2 9.9 %collective-permute-start.20 = (bf16[128,2048]{1,0:T(8,128)(2,1)}, bf16[128,2048]{1,0:T(8,128)(2,1)S(1)}, u32[]{:S(2)}, u32[]{:S(2)}) collective-permute-start(bf16[128,2048]{1,0:T(8,128)(2,1)} %fusion.17), channel_id=1, source_target_pairs={{0,4},{1,3},{2,6},{3,1},{4,0},{5,7},{6,2},{7,5},{8,12},{9,11},{10,... | collective-permute-start | bytes 1572872 | tf_op jit(solution)/shard_map/ppermute | solution.py:185
  158.4 11.7 %collective-permute-start.25 = (bf16[128,2048]{1,0:T(8,128)(2,1)S(1)}, bf16[128,2048]{1,0:T(8,128)(2,1)S(1)}, u32[]{:S(2)}, u32[]{:S(2)}) collective-permute-start(bf16[128,2048]{1,0:T(8,128)(2,1)S(1)} %fusion.16), channel_id=1, source_target_pairs={{0,8},{1,9},{2,10},{3,11},{4,12},{5,13},{6,14},{7,15},{8,16},{9,17... | collective-permute-start | bytes 1572872 | tf_op jit(solution)/shard_map/ppermute | solution.py:185
  162.7 16.2 %collective-permute-start.29 = (bf16[256,2048]{1,0:T(8,128)(2,1)S(1)}, bf16[256,2048]{1,0:T(8,128)(2,1)S(1)}, u32[]{:S(2)}, u32[]{:S(2)}) collective-permute-start(bf16[256,2048]{1,0:T(8,128)(2,1)S(1)} %get-tuple-element.79), channel_id=1, source_target_pairs={{0,2},{1,5},{2,0},{3,7},{4,6},{5,1},{6,4},{7,3},{8,10},{9,13},{10,... | collective-permute-start | bytes 3145736 | tf_op jit(solution)/shard_map/ppermute | solution.py:185
  166.8 28.9 %collective-permute-start.18 = (bf16[256,2048]{1,0:T(8,128)(2,1)S(1)}, bf16[256,2048]{1,0:T(8,128)(2,1)S(1)}, u32[]{:S(2)}, u32[]{:S(2)}) collective-permute-start(bf16[256,2048]{1,0:T(8,128)(2,1)S(1)} %get-tuple-element.63), channel_id=1, source_target_pairs={{0,2},{1,5},{2,0},{3,7},{4,6},{5,1},{6,4},{7,3},{8,10},{9,13},{10,... | collective-permute-start | bytes 3145736 | tf_op jit(solution)/shard_map/ppermute | solution.py:185
  170.4 25.4 %collective-permute-start.26 = (bf16[128,2048]{1,0:T(8,128)(2,1)S(1)}, bf16[128,2048]{1,0:T(8,128)(2,1)S(1)}, u32[]{:S(2)}, u32[]{:S(2)}) collective-permute-start(bf16[128,2048]{1,0:T(8,128)(2,1)S(1)} %fusion.20), channel_id=1, source_target_pairs={{0,8},{1,9},{2,10},{3,11},{4,12},{5,13},{6,14},{7,15},{8,16},{9,17... | collective-permute-start | bytes 1572872 | tf_op jit(solution)/shard_map/ppermute | solution.py:185
  179.3 17.9 %collective-permute-start.30 = (bf16[128,2048]{1,0:T(8,128)(2,1)S(1)}, bf16[128,2048]{1,0:T(8,128)(2,1)S(1)}, u32[]{:S(2)}, u32[]{:S(2)}) collective-permute-start(bf16[128,2048]{1,0:T(8,128)(2,1)S(1)} %fusion.6), channel_id=1, source_target_pairs={{0,4},{1,3},{2,6},{3,1},{4,0},{5,7},{6,2},{7,5},{8,12},{9,11},{10,... | collective-permute-start | bytes 1572872 | tf_op jit(solution)/shard_map/ppermute | solution.py:185
  196.1 8.4 %collective-permute-start.27 = (bf16[128,2048]{1,0:T(8,128)(2,1)S(1)}, bf16[128,2048]{1,0:T(8,128)(2,1)S(1)}, u32[]{:S(2)}, u32[]{:S(2)}) collective-permute-start(bf16[128,2048]{1,0:T(8,128)(2,1)S(1)} %fusion.9), channel_id=1, source_target_pairs={{0,4},{1,3},{2,6},{3,1},{4,0},{5,7},{6,2},{7,5},{8,12},{9,11},{10,... | collective-permute-start | bytes 1572872 | tf_op jit(solution)/shard_map/ppermute | solution.py:185
  197.4 14.9 %collective-permute-start.31 = (bf16[128,2048]{1,0:T(8,128)(2,1)S(1)}, bf16[128,2048]{1,0:T(8,128)(2,1)S(1)}, u32[]{:S(2)}, u32[]{:S(2)}) collective-permute-start(bf16[128,2048]{1,0:T(8,128)(2,1)S(1)} %fusion.8), channel_id=1, source_target_pairs={{0,24},{1,25},{2,26},{3,27},{4,28},{5,29},{6,30},{7,31},{8,0},{9,1... | collective-permute-start | bytes 1572872 | tf_op jit(solution)/shard_map/ppermute | solution.py:185
  213.2 12.2 %collective-permute-start.33 = (bf16[128,2048]{1,0:T(8,128)(2,1)S(1)}, bf16[128,2048]{1,0:T(8,128)(2,1)S(1)}, u32[]{:S(2)}, u32[]{:S(2)}) collective-permute-start(bf16[128,2048]{1,0:T(8,128)(2,1)S(1)} %multiply_convert_fusion.refs_0_), channel_id=1, source_target_pairs={{0,2},{1,3},{2,0},{3,1},{4,6},{5,7},{6,4},{7,5},{8,10},{9,11},{10,... | collective-permute-start | bytes 1572872 | tf_op jit(solution)/shard_map/ppermute | solution.py:681
  214.1 16.3 %collective-permute-start.32 = (bf16[128,2048]{1,0:T(8,128)(2,1)S(1)}, bf16[128,2048]{1,0:T(8,128)(2,1)S(1)}, u32[]{:S(2)}, u32[]{:S(2)}) collective-permute-start(bf16[128,2048]{1,0:T(8,128)(2,1)S(1)} %multiply_convert_fusion.refs_0_), channel_id=1, source_target_pairs={{0,1},{1,0},{2,3},{3,2},{4,5},{5,4},{6,7},{7,6},{8,9},{9,8},{10,11... | collective-permute-start | bytes 1572872 | tf_op jit(solution)/shard_map/ppermute | solution.py:681
  225.5 4.9 %collective-permute-start.34 = (bf16[128,2048]{1,0:T(8,128)(2,1)S(1)}, bf16[128,2048]{1,0:T(8,128)(2,1)S(1)}, u32[]{:S(2)}, u32[]{:S(2)}) collective-permute-start(bf16[128,2048]{1,0:T(8,128)(2,1)S(1)} %collective-permute-done.33.refs_2_), channel_id=1, source_target_pairs={{0,1},{1,0},{2,3},{3,2},{4,5},{5,4},{6,7},{7,6},{8,9},{9,8},{10,11... | collective-permute-start | bytes 1572872 | tf_op jit(solution)/shard_map/ppermute | solution.py:681
  237.8 5.3 %collective-permute-start.35 = (bf16[3,1024]{1,0:T(4,128)(2,1)S(1)}, bf16[3,1024]{1,0:T(4,128)(2,1)S(1)}, u32[]{:S(2)}, u32[]{:S(2)}) collective-permute-start(bf16[3,1024]{1,0:T(4,128)(2,1)S(1)} %slice.41), channel_id=1, source_target_pairs={{0,4},{4,8},{8,12},{12,16},{16,20},{20,24},{24,28},{1,5},{5,9},{9,... | collective-permute-start | bytes 18440 | tf_op jit(solution)/shard_map/ppermute | solution.py:24
  240.6 24.5 %collective-permute-start.36 = (bf16[256,2048]{1,0:T(8,128)(2,1)S(1)}, bf16[256,2048]{1,0:T(8,128)(2,1)S(1)}, u32[]{:S(2)}, u32[]{:S(2)}) collective-permute-start(bf16[256,2048]{1,0:T(8,128)(2,1)S(1)} %get-tuple-element.84), channel_id=1, source_target_pairs={{0,2},{1,3},{2,0},{3,1},{4,6},{5,7},{6,4},{7,5},{8,10},{9,11},{10,... | collective-permute-start | bytes 3145736 | tf_op jit(solution)/shard_map/ppermute | solution.py:681
  265.1 23.8 %collective-permute-start.40 = (bf16[256,2048]{1,0:T(8,128)(2,1)}, bf16[256,2048]{1,0:T(8,128)(2,1)S(1)}, u32[]{:S(2)}, u32[]{:S(2)}) collective-permute-start(bf16[256,2048]{1,0:T(8,128)(2,1)} %get-tuple-element.88), channel_id=1, source_target_pairs={{0,2},{1,3},{2,0},{3,1},{4,6},{5,7},{6,4},{7,5},{8,10},{9,11},{10,... | collective-permute-start | bytes 3145736 | tf_op jit(solution)/shard_map/ppermute | solution.py:681
  265.1 6.4 %collective-permute-start.37 = (bf16[4,128,256]{2,1,0:T(8,128)(2,1)S(1)}, bf16[4,128,256]{2,1,0:T(8,128)(2,1)S(1)}, u32[]{:S(2)}, u32[]{:S(2)}) collective-permute-start(bf16[4,128,256]{2,1,0:T(8,128)(2,1)S(1)} %get-tuple-element.85.mine_ref), channel_id=1, source_target_pairs={{0,4},{4,0},{8,12},{12,8},{16,20},{20,16},{24,28},{28,24},{1,5},{5... | collective-permute-start | bytes 786440 | tf_op jit(solution)/shard_map/ppermute | solution.py:749
  265.1 45.8 %collective-permute-start.45 = (bf16[512,2048]{1,0:T(8,128)(2,1)}, bf16[512,2048]{1,0:T(8,128)(2,1)}, u32[]{:S(2)}, u32[]{:S(2)}) collective-permute-start(bf16[512,2048]{1,0:T(8,128)(2,1)} %refs_4_.5), channel_id=1, source_target_pairs={{0,1},{1,0},{2,3},{3,2},{4,5},{5,4},{6,7},{7,6},{8,9},{9,8},{10,11... | collective-permute-start | bytes 6291464 | tf_op jit(solution)/shard_map/ppermute | solution.py:681
  271.8 6.0 %collective-permute-start.38 = (bf16[4,128,128]{2,1,0:T(8,128)(2,1)S(1)}, bf16[4,128,128]{2,1,0:T(8,128)(2,1)S(1)}, u32[]{:S(2)}, u32[]{:S(2)}) collective-permute-start(bf16[4,128,128]{2,1,0:T(8,128)(2,1)S(1)} %get-tuple-element.87), channel_id=1, source_target_pairs={{0,8},{4,12},{8,16},{12,20},{16,24},{20,28},{1,9},{5,13},{9,17},{1... | collective-permute-start | bytes 393224 | tf_op jit(solution)/shard_map/ppermute | solution.py:24
  278.0 6.0 %collective-permute-start.39 = (bf16[4,128,128]{2,1,0:T(8,128)(2,1)S(1)}, bf16[4,128,128]{2,1,0:T(8,128)(2,1)S(1)}, u32[]{:S(2)}, u32[]{:S(2)}) collective-permute-start(bf16[4,128,128]{2,1,0:T(8,128)(2,1)S(1)} %fusion), channel_id=1, source_target_pairs={{0,8},{4,12},{8,16},{12,20},{16,24},{20,28},{1,9},{5,13},{9,17},{1... | collective-permute-start | bytes 393224 | tf_op jit(solution)/shard_map/ppermute | solution.py:24
  288.9 5.7 %collective-permute-start.41 = (bf16[4,128,128]{2,1,0:T(8,128)(2,1)S(1)}, bf16[4,128,128]{2,1,0:T(8,128)(2,1)S(1)}, u32[]{:S(2)}, u32[]{:S(2)}) collective-permute-start(bf16[4,128,128]{2,1,0:T(8,128)(2,1)S(1)} %fusion.1), channel_id=1, source_target_pairs={{0,8},{4,12},{8,16},{12,20},{16,24},{20,28},{1,9},{5,13},{9,17},{1... | collective-permute-start | bytes 393224 | tf_op jit(solution)/shard_map/ppermute | solution.py:24
  294.6 16.4 %collective-permute-start.47 = (bf16[256,2048]{1,0:T(8,128)(2,1)S(1)}, bf16[256,2048]{1,0:T(8,128)(2,1)S(1)}, u32[]{:S(2)}, u32[]{:S(2)}) collective-permute-start(bf16[256,2048]{1,0:T(8,128)(2,1)S(1)} %collective-permute-done.40.refs_7_), channel_id=1, source_target_pairs={{0,1},{1,0},{2,3},{3,2},{4,5},{5,4},{6,7},{7,6},{8,9},{9,8},{10,11... | collective-permute-start | bytes 3145736 | tf_op jit(solution)/shard_map/ppermute | solution.py:681
  297.8 13.2 %collective-permute-start.46 = (bf16[256,2048]{1,0:T(8,128)(2,1)S(1)}, bf16[256,2048]{1,0:T(8,128)(2,1)}, u32[]{:S(2)}, u32[]{:S(2)}) collective-permute-start(bf16[256,2048]{1,0:T(8,128)(2,1)S(1)} %collective-permute-done.36.refs_6_), channel_id=1, source_target_pairs={{0,1},{1,0},{2,3},{3,2},{4,5},{5,4},{6,7},{7,6},{8,9},{9,8},{10,11... | collective-permute-start | bytes 3145736 | tf_op jit(solution)/shard_map/ppermute | solution.py:681
  302.3 1.6 collective-permute-start.42
  302.9 5.1 %collective-permute-start.43 = (bf16[128,512]{1,0:T(8,128)(2,1)S(1)}, bf16[128,512]{1,0:T(8,128)(2,1)S(1)}, u32[]{:S(2)}, u32[]{:S(2)}) collective-permute-start(bf16[128,512]{1,0:T(8,128)(2,1)S(1)} %get-tuple-element.101), channel_id=1, source_target_pairs={{0,2},{1,3},{2,0},{3,1},{4,6},{5,7},{6,4},{7,5},{8,10},{9,11},{10,... | collective-permute-start | bytes 393224 | tf_op jit(solution)/shard_map/ppermute | solution.py:681
  303.9 7.1 %collective-permute-start.44 = (bf16[128,512]{1,0:T(8,128)(2,1)S(1)}, bf16[128,512]{1,0:T(8,128)(2,1)S(1)}, u32[]{:S(2)}, u32[]{:S(2)}) collective-permute-start(bf16[128,512]{1,0:T(8,128)(2,1)S(1)} %get-tuple-element.100), channel_id=1, source_target_pairs={{0,3},{1,2},{2,1},{3,0},{4,7},{5,6},{6,5},{7,4},{8,11},{9,10},{10,... | collective-permute-start | bytes 393224 | tf_op jit(solution)/shard_map/ppermute | solution.py:681
  (41 other events, 195.6 us)
where the time goes:
time: 317 us; the launch traced here: 316 us
  waiting for transfers between devices  170 us (54%)
  Pallas kernels  68.5 us (22%)
  starting transfers between devices  46.9 us (15%)
  local copies, waits for them, and re-layouts  18.3 us (6%)
  other arithmetic  9.73 us (3%)
    ppermute x32, waiting for transfers between devices, sent(): return lax.ppermute(value, ('ctx', 'head'), pairs)  123 us
    ppermute x32, starting transfers between devices, sent(): return lax.ppermute(value, ('ctx', 'head'), pairs)  30.4 us
    ppermute x11, waiting for transfers between devices, crossed(): return lax.ppermute(value, 'head', pairs)  26 us
    pallas_call x2, Pallas kernels, run_experts(): pl.pallas_call(expert_kernel, grid=(local_experts,), in_specs=[row_spec]...  21.2 us
    ppermute x4, waiting for transfers between devices, passed_along(): lax.ppermute(value, axis, [(source, source + steps) for source in range(f...  16.2 us
    pallas_call x1, Pallas kernels, on_device(): pl.pallas_call(functools.partial(delta_kernel, key_heads=key_heads, chunk...  15.7 us
    unnamed x82, local copies, waits for them, and re-layouts  14.9 us
    pallas_call x4, Pallas kernels, spread(): pl.pallas_call(functools.partial(spread_kernel, slots=slots), grid=(1,),...  11 us
  transfers between devices with their start and end apart: 48, of which 30 were waited for; matrix products, arithmetic and copies ran while one was open for 3% of the time, Pallas kernels for 13%

commit v1 on v0

--- a/solution.py
+++ b/solution.py
@@ -231,13 +231,21 @@
             if earlier:
                 source = after(source, *earlier)
             mine = lifted(source, 1 if steps == 1 else -1)
-        near = first(mine)
-        blocks[steps] = (mine, near, second(mine), second(near))
+        onward = mine
+        if at:
+            onward = after(mine, *blocks[order[at - 1]][1:3])
+        near = first(onward)
+        blocks[steps] = (mine, near, second(onward), second(near))
+
+    picked_spec = pl.BlockSpec((local_experts, taken, width), lambda g: (0, 0, 0))
 
     def collect(steps, *earlier):
         rows = blocks[steps][0]
         own, send = pl.pallas_call(
             functools.partial(collect_kernel, slots=slots),
+            grid=(1,),
+            in_specs=[whole_ref(packet)] * 4 + [whole_ref(picker)],
+            out_specs=[picked_spec] * 2,
             out_shape=[jax.ShapeDtypeStruct((local_experts, taken, width), bf16)] * 2,
             compiler_params=pltpu.CompilerParams(vmem_limit_bytes=48 << 20),
             cost_estimate=worth(2),
@@ -298,8 +306,8 @@
     last = order[-1]
     for steps in order[:-2]:
         collect(steps, blocks[order[-2]][0])
-    collect(order[-2])
-    run_experts(order[:-1], blocks[last][1], blocks[last][2])
+    collect(order[-2], *blocks[last][:3])
+    run_experts(order[:-1])
     back = order[-2:0:-1]
     ready = {steps: spread(steps) for steps in back}
     collect(last, *[far for far, _, _ in ready.values()])
@@ -310,8 +318,6 @@
     for at, steps in enumerate(back):
         far, near, here = ready[steps] if steps in ready else spread(steps)
         across = second(far)
-        if at == 0:
-            across = after(across, outcome[last][1])
         if at >= 2 and back[at - 2] in carried:
             across = after(across, carried[back[at - 2]])
         across = across.astype(f32)
@@ -441,7 +447,8 @@
     raw_ref,
     rim_ref,
     taps_ref,
-    small_ref,
+    beta_ref,
+    decay_ref,
     rate_ref,
     core_ref,
     reading_ref,
@@ -478,8 +485,8 @@
             elif first < value_at:
                 value = unit_rows(value)
             mixed[start : start + chunk, columns] = value
-    strengths[...] = 1.0 / (1.0 + jnp.exp(-small_ref[:, :heads]))
-    shifted = small_ref[:, heads:] + rate_ref[1:2, :]
+    strengths[...] = 1.0 / (1.0 + jnp.exp(-beta_ref[...]))
+    shifted = decay_ref[...] + rate_ref[1:2, :]
     softened = jnp.maximum(shifted, 0.0) + jnp.log1p(jnp.exp(-jnp.abs(shifted)))
     falls[...] = -jnp.exp(rate_ref[0:1, :]) * softened
 
@@ -571,25 +578,36 @@
 
 
 def project_kernel(place_ref, *refs, blocks):
-    piece_refs, weight_refs, out_refs = refs[:blocks], refs[blocks : -3], refs[-3:]
-    qkv_ref, gate_ref, small_ref = out_refs
-    rows = jnp.concatenate([ref[...] for ref in piece_refs], axis=0)
+    piece_refs, halo_refs = refs[:blocks], refs[blocks : 2 * blocks]
+    weight_refs, out_refs = refs[2 * blocks : -5], refs[-5:]
+    qkv_ref, gate_ref, beta_ref, decay_ref, rim_ref = out_refs
     tok_rows = piece_refs[0].shape[0]
+    halo_rows = halo_refs[0].shape[0]
+    halo = sum(
+        jnp.where((place_ref[0] ^ step) == blocks - 1, 1.0, 0.0) * halo_refs[step][...].astype(f32)
+        for step in range(blocks)
+    ).astype(bf16)
+    rows = jnp.concatenate([ref[...] for ref in piece_refs] + [halo], axis=0)
 
     def store(out_ref, first, weight_ref):
         product = contract(rows, weight_ref[...], ((1,), (0,))).astype(out_ref.dtype)
+        last = first + product.shape[1]
         for step in range(blocks):
             at = pl.multiple_of((place_ref[0] ^ step) * tok_rows, tok_rows)
-            out_ref[pl.ds(at, tok_rows), first : first + product.shape[1]] = product[
+            out_ref[pl.ds(at, tok_rows), first:last] = product[
                 step * tok_rows : (step + 1) * tok_rows
             ]
+        return product[blocks * tok_rows :]
 
     first = 0
     for weight_ref in weight_refs[:3]:
-        store(qkv_ref, first, weight_ref)
-        first += weight_ref.shape[1]
+        rim = store(qkv_ref, first, weight_ref)
+        last = first + weight_ref.shape[1]
+        rim_ref[:, first:last] = rim.astype(f32)
+        first = last
     store(gate_ref, 0, weight_refs[3])
-    store(small_ref, 0, weight_refs[4])
+    store(beta_ref, 0, weight_refs[4])
+    store(decay_ref, 0, weight_refs[5])
 
 
 def pair_kernel(second_ref, mine_ref, other_ref, moved_ref, transfer_ref):
@@ -689,18 +707,23 @@
 
     in_vmem = pl.BlockSpec(memory_space=pltpu.VMEM)
     in_smem = pl.BlockSpec(memory_space=pltpu.SMEM)
-    tok_rows = stream.shape[0]
+    tok_rows, width = stream.shape
     rows = tok_rows * head_count
     key_cols, value_cols = query_weight.shape[1], value_weight.shape[1]
     heads = beta_weight.shape[1]
+    rim_len = 16
+    halos = from_all(passed_along(mixer_in[tok_rows - rim_len :], "ctx", 1))
     pieces = from_all(mixer_in)
-    qkv_raw, gate_raw, small_raw = pl.pallas_call(
+    conv_cols = 2 * key_cols + value_cols
+    qkv_raw, gate_raw, beta_raw, decay_raw, rim = pl.pallas_call(
         functools.partial(project_kernel, blocks=head_count),
-        in_specs=[in_smem] + [in_vmem] * (head_count + 5),
+        in_specs=[in_smem] + [in_vmem] * (2 * head_count + 6),
         out_shape=[
-            jax.ShapeDtypeStruct((rows, 2 * key_cols + value_cols), bf16),
+            jax.ShapeDtypeStruct((rows, conv_cols), bf16),
             jax.ShapeDtypeStruct((rows, value_cols), bf16),
-            jax.ShapeDtypeStruct((rows, 2 * heads), f32),
+            jax.ShapeDtypeStruct((rows, heads), f32),
+            jax.ShapeDtypeStruct((rows, heads), f32),
+            jax.ShapeDtypeStruct((rim_len, conv_cols), f32),
         ],
         compiler_params=pltpu.CompilerParams(vmem_limit_bytes=48 << 20),
         cost_estimate=worth(5),
@@ -708,18 +731,16 @@
     )(
         head_place.reshape(1),
         *pieces,
+        *halos,
         query_weight,
         key_weight,
         value_weight,
         output_gate,
-        jnp.concatenate([beta_weight, decay_weight], axis=1),
-    )
-    conv_cols = qkv_raw.shape[1]
+        beta_weight,
+        decay_weight,
+    )
     key_heads = key_cols // DK
     taps = jnp.concatenate([query_conv, key_conv, value_conv], axis=1)
-    rim_len = taps.shape[0] - 1
-    rim = passed_along(qkv_raw[rows - rim_len :], "ctx", 1)
-    rim = jnp.concatenate([jnp.zeros((8 - rim_len, conv_cols), f32), rim.astype(f32)], axis=0)
     rates = jnp.stack([decay_log, decay_bias])
     chunk = math.gcd(rows, CHUNK)
     core, reading, moved = pl.pallas_call(
@@ -730,7 +751,7 @@
             jax.ShapeDtypeStruct((heads, DK, 2 * DK), bf16),
         ),
         scratch_shapes=[
-            pltpu.VMEM((rows + 8, conv_cols), f32),
+            pltpu.VMEM((rows + rim_len, conv_cols), f32),
             pltpu.VMEM((rows, conv_cols), f32),
             pltpu.VMEM((rows, heads), f32),
             pltpu.VMEM((rows, heads), f32),
@@ -739,14 +760,14 @@
         compiler_params=pltpu.CompilerParams(vmem_limit_bytes=48 << 20),
         cost_estimate=worth(16),
         name="delta",
-    )(qkv_raw, rim, taps, small_raw, rates)
+    )(qkv_raw, rim, taps, beta_raw, decay_raw, rates)
     half = out_weight.shape[0] // 2
     upper = [crossed(after(out_weight[:half], pieces[-1]), step) for step in range(2, head_count, 2)]
-    moved = after(moved, *upper)
     lower = [crossed(after(out_weight[half:], moved), step) for step in range(2, head_count, 2)]
 
     in_pair = (ctx_place % 2).reshape(1)
     other = lax.ppermute(moved, "ctx", [(place, place ^ 1) for place in range(ctx_count)])
+    other = after(other, *upper)
     state_shape = jax.ShapeDtypeStruct((heads, DK, DK), bf16)
     added, transfer = pl.pallas_call(
         pair_kernel,
@@ -765,7 +786,11 @@
 
     gated = pl.pallas_call(
         finish_kernel,
-        in_specs=[in_smem] + [in_vmem] * 6,
+        grid=(head_count,),
+        in_specs=[in_smem, whole_ref(state), whole_ref(other)]
+        + [pl.BlockSpec((tok_rows, value_cols), lambda block: (block, 0))] * 3
+        + [pl.BlockSpec((1, DK), lambda block: (0, 0))],
+        out_specs=pl.BlockSpec((tok_rows, value_cols), lambda block: (block, 0)),
         out_shape=jax.ShapeDtypeStruct((rows, value_cols), bf16),
         compiler_params=pltpu.CompilerParams(vmem_limit_bytes=48 << 20),
         name="finish",
@@ -780,6 +805,10 @@
         weight_parts += [crossed(after(part, state), 1) for part in near_pair]
     mixer_out = pl.pallas_call(
         functools.partial(output_kernel, blocks=head_count),
+        grid=(4,),
+        in_specs=[whole_ref(part) for part in gated_parts]
+        + [pl.BlockSpec((part.shape[0], width // 4), lambda n: (0, n)) for part in weight_parts],
+        out_specs=pl.BlockSpec((tok_rows, width // 4), lambda n: (0, n)),
         out_shape=jax.ShapeDtypeStruct(stream.shape, bf16),
         compiler_params=pltpu.CompilerParams(vmem_limit_bytes=48 << 20),
         name="output",

time: 317 us -> 306 us (0.965)
  waiting for transfers between devices: 170 us -> 158 us
    ppermute x32, waiting for transfers between devices: 123 us -> 117 us  [sent(): return lax.ppermute(value, ('ctx', 'head'), pairs)]
    ppermute x11 -> x14, waiting for transfers between devices: 26 us -> 22.2 us  [crossed(): return lax.ppermute(value, 'head', pairs)]
    ppermute x32, starting transfers between devices: 30.4 us -> 26.7 us  [sent(): return lax.ppermute(value, ('ctx', 'head'), pairs)]
    ppermute x11 -> x14, starting transfers between devices: 9.87 us -> 11.4 us  [crossed(): return lax.ppermute(value, 'head', pairs)]
    unnamed x82 -> x80, local copies, waits for them, and re-layouts: 14.9 us -> 14.6 us
  transfers between devices with their start and end apart: 48 -> 51, of which waited for: 30 -> 32; matrix products, arithmetic and copies ran while one was open for 3% -> 3% of each run, Pallas kernels for 13% -> 18%
where the time goes in v1:
time: 306 us; the launch traced here: 305 us
  waiting for transfers between devices  158 us (52%)
  Pallas kernels  70.9 us (23%)
  starting transfers between devices  45.8 us (15%)
  local copies, waits for them, and re-layouts  18.2 us (6%)
  other arithmetic  9.44 us (3%)
    ppermute x32, waiting for transfers between devices, sent(): return lax.ppermute(value, ('ctx', 'head'), pairs)  117 us
    ppermute x32, starting transfers between devices, sent(): return lax.ppermute(value, ('ctx', 'head'), pairs)  26.7 us
    ppermute x14, waiting for transfers between devices, crossed(): return lax.ppermute(value, 'head', pairs)  22.2 us
    pallas_call x2, Pallas kernels, run_experts(): pl.pallas_call(expert_kernel, grid=(local_experts,), in_specs=[row_spec]...  21.1 us
    pallas_call x1, Pallas kernels, on_device(): pl.pallas_call(functools.partial(delta_kernel, key_heads=key_heads, chunk...  15.8 us
    unnamed x80, local copies, waits for them, and re-layouts  14.6 us
    ppermute x4, waiting for transfers between devices, passed_along(): lax.ppermute(value, axis, [(source, source + steps) for source in range(f...  13.8 us
    ppermute x14, starting transfers between devices, crossed(): return lax.ppermute(value, 'head', pairs)  11.4 us
  transfers between devices with their start and end apart: 51, of which 32 were waited for; matrix products, arithmetic and copies ran while one was open for 3% of the time, Pallas kernels for 18%

profile of v1, /device:TPU:25, one launch (start us, length us, event | category | flops | bytes accessed | tf_op | source)
XLA Modules:
  0.0 304.6 jit_solution(18403759763591575929)
XLA Ops:
  7.5 9.3 %collective-permute-done.block_10.cols_10 = bf16[128,2176]{1,0:T(8,128)(2,1)S(1)} collective-permute-done((bf16[128,2176]{1,0:T(8,128)(2,1)S(1)}, bf16[128,2176]{1,0:T(8,128)(2,1)S(1)}, u32[]{:S(2)}, u32[]{:S(2)}) %collective-permute-start) | collective-permute-done | bytes 557088 | tf_op jit(solution)/shard_map/ppermute | solution.py:185
  16.8 3.9 %collective-permute-done.1.block_01.cols_01 = bf16[128,2176]{1,0:T(8,128)(2,1)S(1)} collective-permute-done((bf16[128,2176]{1,0:T(8,128)(2,1)S(1)}, bf16[128,2176]{1,0:T(8,128)(2,1)S(1)}, u32[]{:S(2)}, u32[]{:S(2)}) %collective-permute-start.1) | collective-permute-done | bytes 557088 | tf_op jit(solution)/shard_map/ppermute | solution.py:185
  22.5 11.1 %collective-permute-done.5.block_10.cols_10 = bf16[128,2176]{1,0:T(8,128)(2,1)} collective-permute-done((bf16[128,2176]{1,0:T(8,128)(2,1)S(1)}, bf16[128,2176]{1,0:T(8,128)(2,1)}, u32[]{:S(2)}, u32[]{:S(2)}) %collective-permute-start.5) | collective-permute-done | bytes 557088 | tf_op jit(solution)/shard_map/ppermute | solution.py:185
  33.5 2.3 collective-permute-done.4.block_00.cols_00
  36.7 2.4 collective-permute-start.8
  41.1 9.1 %collective-permute-done.8.block_00.cols_00 = bf16[128,2176]{1,0:T(8,128)(2,1)S(1)} collective-permute-done((bf16[128,2176]{1,0:T(8,128)(2,1)S(1)}, bf16[128,2176]{1,0:T(8,128)(2,1)S(1)}, u32[]{:S(2)}, u32[]{:S(2)}) %collective-permute-start.8) | collective-permute-done | bytes 557088 | tf_op jit(solution)/shard_map/ppermute | solution.py:185
  50.2 1.8 collective-permute-done.9.block_10.cols_10
  55.8 5.3 %collective-permute-done.2.block_11.cols_11 = bf16[128,2176]{1,0:T(8,128)(2,1)S(1)} collective-permute-done((bf16[128,2176]{1,0:T(8,128)(2,1)S(1)}, bf16[128,2176]{1,0:T(8,128)(2,1)S(1)}, u32[]{:S(2)}, u32[]{:S(2)}) %collective-permute-start.2) | collective-permute-done | bytes 557088 | tf_op jit(solution)/shard_map/ppermute | solution.py:185
  62.2 3.4 %collective-permute-start.14 = (bf16[2,96,2048]{2,1,0:T(8,128)(2,1)S(1)}, bf16[2,96,2048]{2,1,0:T(8,128)(2,1)S(1)}, u32[]{:S(2)}, u32[]{:S(2)}) collective-permute-start(bf16[2,96,2048]{2,1,0:T(8,128)(2,1)S(1)} %get-tuple-element.64), channel_id=1, source_target_pairs={{0,1},{1,0},{2,3},{3,2},{4,5},{5,4},{6,7},{7,6},{8,9},{9,8},{10,11... | collective-permute-start | bytes 2359304 | tf_op jit(solution)/shard_map/ppermute | solution.py:185
  65.6 6.5 %collective-permute-done.7.block_11.cols_11 = bf16[128,2176]{1,0:T(8,128)(2,1)} collective-permute-done((bf16[128,2176]{1,0:T(8,128)(2,1)}, bf16[128,2176]{1,0:T(8,128)(2,1)}, u32[]{:S(2)}, u32[]{:S(2)}) %collective-permute-start.7) | collective-permute-done | bytes 557088 | tf_op jit(solution)/shard_map/ppermute | solution.py:185
  72.0 2.3 collect.5
  75.5 2.5 collective-permute-done.12.block_01.cols_01
  78.8 4.9 %collective-permute-done.13.block_11.cols_11 = bf16[128,2176]{1,0:T(8,128)(2,1)S(1)} collective-permute-done((bf16[128,2176]{1,0:T(8,128)(2,1)}, bf16[128,2176]{1,0:T(8,128)(2,1)S(1)}, u32[]{:S(2)}, u32[]{:S(2)}) %collective-permute-start.13) | collective-permute-done | bytes 557088 | tf_op jit(solution)/shard_map/ppermute | solution.py:185
  83.7 2.5 collect.6
  87.5 1.9 collective-permute-done.16.refs_5_
  90.3 12.6 %experts.2 = (bf16[2,288,2048]{2,1,0:T(8,128)(2,1)}, bf16[2,288,2048]{2,1,0:T(8,128)(2,1)}) custom-call(bf16[2,96,2048]{2,1,0:T(8,128)(2,1)} %copy-done.18, bf16[2,96,2048]{2,1,0:T(8,128)(2,1)} %copy-done.19, bf16[2,96,2048]{2,1,0:T(8,128)(2,1)} %copy-done.21, bf16[2,96,2048]{2,1,0:T(8,128)(2,1)} %copy-done.36, bf16[2,96,2048]{2,1,0:T(8,128)(2,1)} %copy-done.37, ...), custom_call_target="tpu_custom_call" | custom-call | flops 14949999616 | bytes 13000000 | tf_op jit(solution)/shard_map/experts/pallas_call | solution.py:260
  103.7 4.0 %collective-permute-done.17.got_ref = bf16[2,288,2048]{2,1,0:T(8,128)(2,1)S(1)} collective-permute-done((bf16[2,288,2048]{2,1,0:T(8,128)(2,1)}, bf16[2,288,2048]{2,1,0:T(8,128)(2,1)S(1)}, u32[]{:S(2)}, u32[]{:S(2)}) %collective-permute-start.17) | collective-permute-done | bytes 2359328 | tf_op jit(solution)/shard_map/ppermute | solution.py:185
  109.1 3.0 spread.6
  112.5 2.9 spread.5
  115.4 2.3 collect.7
  119.4 6.7 %collective-permute-done.21 = bf16[256,2048]{1,0:T(8,128)(2,1)S(1)} collective-permute-done((bf16[256,2048]{1,0:T(8,128)(2,1)S(1)}, bf16[256,2048]{1,0:T(8,128)(2,1)S(1)}, u32[]{:S(2)}, u32[]{:S(2)}) %collective-permute-start.21) | collective-permute-done | bytes 1048608 | tf_op jit(solution)/shard_map/ppermute | solution.py:185
  127.7 8.5 %experts.3 = (bf16[2,96,2048]{2,1,0:T(8,128)(2,1)}, bf16[2,96,2048]{2,1,0:T(8,128)(2,1)}) custom-call(bf16[2,96,2048]{2,1,0:T(8,128)(2,1)} %copy-done.20, bf16[2,96,2048]{2,1,0:T(8,128)(2,1)} %collective-permute-done.27.refs_1_, bf16[2,2048,512]{2,1,0:T(8,128)(2,1)} %refs_2_.1, bf16[2,2048,512]{2,1,0:T(8,128)(2,1)} %refs_3_.1, bf16[2,512,2048]{2,1,0:T(8,128)(2,1)} %refs_4_.2), custom_call_target="tpu_custom_call" | custom-call | flops 8049999872 | bytes 7000000 | tf_op jit(solution)/shard_map/experts/pallas_call | solution.py:260
  137.6 5.5 %collective-permute-done.19 = bf16[256,2048]{1,0:T(8,128)(2,1)} collective-permute-done((bf16[256,2048]{1,0:T(8,128)(2,1)S(1)}, bf16[256,2048]{1,0:T(8,128)(2,1)}, u32[]{:S(2)}, u32[]{:S(2)}) %collective-permute-start.19) | collective-permute-done | bytes 1048608 | tf_op jit(solution)/shard_map/ppermute | solution.py:185
  143.0 1.5 convert_element_type.120
  147.1 2.2 spread.7
  149.7 2.9 spread.4
  154.3 5.4 %collective-permute-done.23 = bf16[128,2048]{1,0:T(8,128)(2,1)S(1)} collective-permute-done((bf16[128,2048]{1,0:T(8,128)(2,1)S(1)}, bf16[128,2048]{1,0:T(8,128)(2,1)S(1)}, u32[]{:S(2)}, u32[]{:S(2)}) %collective-permute-start.23) | collective-permute-done | bytes 524320 | tf_op jit(solution)/shard_map/ppermute | solution.py:185
  161.1 1.7 collective-permute-start.24
  162.8 4.1 %collective-permute-done.29 = bf16[256,2048]{1,0:T(8,128)(2,1)S(1)} collective-permute-done((bf16[256,2048]{1,0:T(8,128)(2,1)S(1)}, bf16[256,2048]{1,0:T(8,128)(2,1)S(1)}, u32[]{:S(2)}, u32[]{:S(2)}) %collective-permute-start.29) | collective-permute-done | bytes 1048608 | tf_op jit(solution)/shard_map/ppermute | solution.py:185
  168.2 15.2 %collective-permute-done.18 = bf16[256,2048]{1,0:T(8,128)(2,1)S(1)} collective-permute-done((bf16[256,2048]{1,0:T(8,128)(2,1)S(1)}, bf16[256,2048]{1,0:T(8,128)(2,1)S(1)}, u32[]{:S(2)}, u32[]{:S(2)}) %collective-permute-start.18) | collective-permute-done | bytes 1048608 | tf_op jit(solution)/shard_map/ppermute | solution.py:185
  185.4 6.8 %collective-permute-done.25 = bf16[128,2048]{1,0:T(8,128)(2,1)S(1)} collective-permute-done((bf16[128,2048]{1,0:T(8,128)(2,1)S(1)}, bf16[128,2048]{1,0:T(8,128)(2,1)S(1)}, u32[]{:S(2)}, u32[]{:S(2)}) %collective-permute-start.25) | collective-permute-done | bytes 524320 | tf_op jit(solution)/shard_map/ppermute | solution.py:185
  192.2 7.8 %collective-permute-done.31 = bf16[128,2048]{1,0:T(8,128)(2,1)S(1)} collective-permute-done((bf16[128,2048]{1,0:T(8,128)(2,1)S(1)}, bf16[128,2048]{1,0:T(8,128)(2,1)S(1)}, u32[]{:S(2)}, u32[]{:S(2)}) %collective-permute-start.31) | collective-permute-done | bytes 524320 | tf_op jit(solution)/shard_map/ppermute | solution.py:185
  202.8 2.7 collective-permute-start.35
  205.5 8.7 %collective-permute-done.33.refs_2_ = bf16[128,2048]{1,0:T(8,128)(2,1)S(1)} collective-permute-done((bf16[128,2048]{1,0:T(8,128)(2,1)S(1)}, bf16[128,2048]{1,0:T(8,128)(2,1)S(1)}, u32[]{:S(2)}, u32[]{:S(2)}) %collective-permute-start.33) | collective-permute-done | bytes 524320 | tf_op jit(solution)/shard_map/ppermute | solution.py:699
  215.4 3.1 %fusion.26 = (bf16[256,2048]{1,0:T(8,128)(2,1)}, bf16[256,2048]{1,0:T(8,128)(2,1)}) fusion(bf16[512,2048]{1,0:T(8,128)(2,1)} %refs_4_.3), kind=kLoop, calls=%fused_computation.58 | loop fusion | bytes 4194304 | tf_op jit(solution)/shard_map/slice | solution.py:766
  220.6 2.4 collective-permute-done.37.refs_6_
  226.6 7.6 %project.1 = (bf16[512,1024]{1,0:T(8,128)(2,1)S(1)}, bf16[512,512]{1,0:T(8,128)(2,1)S(1)}, f32[512,4]{1,0:T(8,128)S(1)}, f32[512,4]{1,0:T(8,128)S(1)}, f32[16,1024]{1,0:T(8,128)S(1)}) custom-call(s32[1]{0:T(128)} %bitcast.1.place_ref, bf16[128,2048]{1,0:T(8,128)(2,1)S(1)} %multiply_convert_fusion.refs_0_, bf16[128,2048]{1,0:T(8,128)(2,1)} %collective-permute-done.32.refs_1_, ...), custom_call_target="tpu_custom_call" | custom-call | flops 5750000128 | bytes 5000000 | tf_op jit(solution)/shard_map/project/pallas_call | solution.py:718
  235.0 15.8 %delta.1 = (f32[512,512]{1,0:T(8,128)S(1)}, f32[512,512]{1,0:T(8,128)S(1)}, bf16[4,128,256]{2,1,0:T(8,128)(2,1)S(1)}) custom-call(bf16[512,1024]{1,0:T(8,128)(2,1)S(1)} %get-tuple-element.87.raw_ref, f32[16,1024]{1,0:T(8,128)S(1)} %get-tuple-element.88.rim_ref, f32[4,1024]{1,0:T(4,128)S(1)} %pad_maximum_fusion.taps_ref, ...), custom_call_target="tpu_custom_call" | custom-call | flops 18400000000 | bytes 16000000 | tf_op jit(solution)/shard_map/delta/pallas_call | solution.py:746
  255.1 5.4 %collective-permute-done.39.other_ref = bf16[4,128,256]{2,1,0:T(8,128)(2,1)S(1)} collective-permute-done((bf16[4,128,256]{2,1,0:T(8,128)(2,1)S(1)}, bf16[4,128,256]{2,1,0:T(8,128)(2,1)S(1)}, u32[]{:S(2)}, u32[]{:S(2)}) %collective-permute-start.39) | collective-permute-done | bytes 262176 | tf_op jit(solution)/shard_map/ppermute | solution.py:769
  262.1 4.7 %collective-permute-done.41 = bf16[4,128,128]{2,1,0:T(8,128)(2,1)S(1)} collective-permute-done((bf16[4,128,128]{2,1,0:T(8,128)(2,1)S(1)}, bf16[4,128,128]{2,1,0:T(8,128)(2,1)S(1)}, u32[]{:S(2)}, u32[]{:S(2)}) %collective-permute-start.41) | collective-permute-done | bytes 131104 | tf_op jit(solution)/shard_map/ppermute | solution.py:24
  268.3 4.7 %collective-permute-done.42 = bf16[4,128,128]{2,1,0:T(8,128)(2,1)S(1)} collective-permute-done((bf16[4,128,128]{2,1,0:T(8,128)(2,1)S(1)}, bf16[4,128,128]{2,1,0:T(8,128)(2,1)S(1)}, u32[]{:S(2)}, u32[]{:S(2)}) %collective-permute-start.42) | collective-permute-done | bytes 131104 | tf_op jit(solution)/shard_map/ppermute | solution.py:24
  273.2 4.3 %collective-permute-done.43.refs_7_ = bf16[256,2048]{1,0:T(8,128)(2,1)S(1)} collective-permute-done((bf16[256,2048]{1,0:T(8,128)(2,1)}, bf16[256,2048]{1,0:T(8,128)(2,1)S(1)}, u32[]{:S(2)}, u32[]{:S(2)}) %collective-permute-start.43) | collective-permute-done | bytes 1048608 | tf_op jit(solution)/shard_map/ppermute | solution.py:699
  278.7 4.4 %collective-permute-done.44.state_ref = bf16[4,128,128]{2,1,0:T(8,128)(2,1)S(1)} collective-permute-done((bf16[4,128,128]{2,1,0:T(8,128)(2,1)S(1)}, bf16[4,128,128]{2,1,0:T(8,128)(2,1)S(1)}, u32[]{:S(2)}, u32[]{:S(2)}) %collective-permute-start.44) | collective-permute-done | bytes 131104 | tf_op jit(solution)/shard_map/ppermute | solution.py:24
  283.2 2.3 collective-permute-start.50
  288.9 2.0 finish.1
  293.3 3.4 %collective-permute-done.46.refs_2_ = bf16[128,512]{1,0:T(8,128)(2,1)S(1)} collective-permute-done((bf16[128,512]{1,0:T(8,128)(2,1)S(1)}, bf16[128,512]{1,0:T(8,128)(2,1)S(1)}, u32[]{:S(2)}, u32[]{:S(2)}) %collective-permute-start.46) | collective-permute-done | bytes 131104 | tf_op jit(solution)/shard_map/ppermute | solution.py:699
  296.7 3.0 collective-permute-done.47.refs_3_
  299.6 4.9 %output.1 = bf16[128,2048]{1,0:T(8,128)(2,1)} custom-call(bf16[128,512]{1,0:T(8,128)(2,1)S(1)} %get-tuple-element.111.refs_0_, bf16[128,512]{1,0:T(8,128)(2,1)S(1)} %collective-permute-done.45.refs_1_, bf16[128,512]{1,0:T(8,128)(2,1)S(1)} %collective-permute-done.46.refs_2_, bf16[128,512]{1,0:T(8,128)(2,1)S(1)} %collective-permute-done.47.refs_3_, ...), custom_call_target="tpu_custom_call" | custom-call | tf_op jit(solution)/shard_map/output/pallas_call | solution.py:806
  (182 shorter events, 61.8 us)
Async XLA Ops:
  4.8 12.0 %collective-permute-start = (bf16[128,2176]{1,0:T(8,128)(2,1)S(1)}, bf16[128,2176]{1,0:T(8,128)(2,1)S(1)}, u32[]{:S(2)}, u32[]{:S(2)}) collective-permute-start(bf16[128,2176]{1,0:T(8,128)(2,1)S(1)} %concatenate.6.block_00.cols_00), channel_id=1, source_target_pairs={{0,4},{1,3},{2,6},{3,1},{4,0},{5,7},{6,2},{7,5},{8,12},{9,11},{10,... | collective-permute-start | bytes 1671176 | tf_op jit(solution)/shard_map/ppermute | solution.py:185
  6.1 14.6 %collective-permute-start.1 = (bf16[128,2176]{1,0:T(8,128)(2,1)S(1)}, bf16[128,2176]{1,0:T(8,128)(2,1)S(1)}, u32[]{:S(2)}, u32[]{:S(2)}) collective-permute-start(bf16[128,2176]{1,0:T(8,128)(2,1)S(1)} %concatenate.6.block_00.cols_00), channel_id=1, source_target_pairs={{0,2},{1,5},{2,0},{3,7},{4,6},{5,1},{6,4},{7,3},{8,10},{9,13},{10,... | collective-permute-start | bytes 1671176 | tf_op jit(solution)/shard_map/ppermute | solution.py:185
  7.3 14.7 %collective-permute-start.3 = (bf16[128,2176]{1,0:T(8,128)(2,1)S(1)}, bf16[128,2176]{1,0:T(8,128)(2,1)S(1)}, u32[]{:S(2)}, u32[]{:S(2)}) collective-permute-start(bf16[128,2176]{1,0:T(8,128)(2,1)S(1)} %concatenate.6.block_00.cols_00), channel_id=1, source_target_pairs={{0,24},{1,25},{2,26},{3,27},{4,28},{5,29},{6,30},{7,31},{8,0},{9,1... | collective-permute-start | bytes 1671176 | tf_op jit(solution)/shard_map/ppermute | solution.py:185
  22.0 11.5 %collective-permute-start.5 = (bf16[128,2176]{1,0:T(8,128)(2,1)S(1)}, bf16[128,2176]{1,0:T(8,128)(2,1)}, u32[]{:S(2)}, u32[]{:S(2)}) collective-permute-start(bf16[128,2176]{1,0:T(8,128)(2,1)S(1)} %collective-permute-done.3.block_00.cols_00), channel_id=1, source_target_pairs={{0,4},{1,3},{2,6},{3,1},{4,0},{5,7},{6,2},{7,5},{8,12},{9,11},{10,... | collective-permute-start | bytes 1671176 | tf_op jit(solution)/shard_map/ppermute | solution.py:185
  22.2 13.6 %collective-permute-start.4 = (bf16[128,2176]{1,0:T(8,128)(2,1)S(1)}, bf16[128,2176]{1,0:T(8,128)(2,1)}, u32[]{:S(2)}, u32[]{:S(2)}) collective-permute-start(bf16[128,2176]{1,0:T(8,128)(2,1)S(1)} %collective-permute-done.3.block_00.cols_00), channel_id=1, source_target_pairs={{0,24},{1,25},{2,26},{3,27},{4,28},{5,29},{6,30},{7,31},{8,0},{9,1... | collective-permute-start | bytes 1671176 | tf_op jit(solution)/shard_map/ppermute | solution.py:185
  22.3 13.6 %collective-permute-start.6 = (bf16[128,2176]{1,0:T(8,128)(2,1)S(1)}, bf16[128,2176]{1,0:T(8,128)(2,1)S(1)}, u32[]{:S(2)}, u32[]{:S(2)}) collective-permute-start(bf16[128,2176]{1,0:T(8,128)(2,1)S(1)} %collective-permute-done.3.block_00.cols_00), channel_id=1, source_target_pairs={{0,2},{1,5},{2,0},{3,7},{4,6},{5,1},{6,4},{7,3},{8,10},{9,13},{10,... | collective-permute-start | bytes 1671176 | tf_op jit(solution)/shard_map/ppermute | solution.py:185
  36.7 13.5 %collective-permute-start.8 = (bf16[128,2176]{1,0:T(8,128)(2,1)S(1)}, bf16[128,2176]{1,0:T(8,128)(2,1)S(1)}, u32[]{:S(2)}, u32[]{:S(2)}) collective-permute-start(bf16[128,2176]{1,0:T(8,128)(2,1)S(1)} %concatenate.6.block_00.cols_00), channel_id=1, source_target_pairs={{0,8},{1,9},{2,10},{3,11},{4,12},{5,13},{6,14},{7,15},{8,16},{9,17... | collective-permute-start | bytes 1671176 | tf_op jit(solution)/shard_map/ppermute | solution.py:185
  39.0 12.9 %collective-permute-start.9 = (bf16[128,2176]{1,0:T(8,128)(2,1)}, bf16[128,2176]{1,0:T(8,128)(2,1)}, u32[]{:S(2)}, u32[]{:S(2)}) collective-permute-start(bf16[128,2176]{1,0:T(8,128)(2,1)} %collective-permute-done.4.block_00.cols_00), channel_id=1, source_target_pairs={{0,4},{1,3},{2,6},{3,1},{4,0},{5,7},{6,2},{7,5},{8,12},{9,11},{10,... | collective-permute-start | bytes 1671176 | tf_op jit(solution)/shard_map/ppermute | solution.py:185
  39.3 13.6 %collective-permute-start.10 = (bf16[128,2176]{1,0:T(8,128)(2,1)}, bf16[128,2176]{1,0:T(8,128)(2,1)}, u32[]{:S(2)}, u32[]{:S(2)}) collective-permute-start(bf16[128,2176]{1,0:T(8,128)(2,1)} %collective-permute-done.4.block_00.cols_00), channel_id=1, source_target_pairs={{0,2},{1,5},{2,0},{3,7},{4,6},{5,1},{6,4},{7,3},{8,10},{9,13},{10,... | collective-permute-start | bytes 1671176 | tf_op jit(solution)/shard_map/ppermute | solution.py:185
  39.6 21.5 %collective-permute-start.2 = (bf16[128,2176]{1,0:T(8,128)(2,1)S(1)}, bf16[128,2176]{1,0:T(8,128)(2,1)S(1)}, u32[]{:S(2)}, u32[]{:S(2)}) collective-permute-start(bf16[128,2176]{1,0:T(8,128)(2,1)S(1)} %collective-permute-done.block_10.cols_10), channel_id=1, source_target_pairs={{0,2},{1,5},{2,0},{3,7},{4,6},{5,1},{6,4},{7,3},{8,10},{9,13},{10,... | collective-permute-start | bytes 1671176 | tf_op jit(solution)/shard_map/ppermute | solution.py:185
  40.7 31.3 %collective-permute-start.7 = (bf16[128,2176]{1,0:T(8,128)(2,1)}, bf16[128,2176]{1,0:T(8,128)(2,1)}, u32[]{:S(2)}, u32[]{:S(2)}) collective-permute-start(bf16[128,2176]{1,0:T(8,128)(2,1)} %collective-permute-done.5.block_10.cols_10), channel_id=1, source_target_pairs={{0,2},{1,5},{2,0},{3,7},{4,6},{5,1},{6,4},{7,3},{8,10},{9,13},{10,... | collective-permute-start | bytes 1671176 | tf_op jit(solution)/shard_map/ppermute | solution.py:185
  52.9 22.6 %collective-permute-start.11 = (bf16[128,2176]{1,0:T(8,128)(2,1)S(1)}, bf16[128,2176]{1,0:T(8,128)(2,1)}, u32[]{:S(2)}, u32[]{:S(2)}) collective-permute-start(bf16[128,2176]{1,0:T(8,128)(2,1)S(1)} %collective-permute-done.8.block_00.cols_00), channel_id=1, source_target_pairs={{0,4},{1,3},{2,6},{3,1},{4,0},{5,7},{6,2},{7,5},{8,12},{9,11},{10,... | collective-permute-start | bytes 1671176 | tf_op jit(solution)/shard_map/ppermute | solution.py:185
  54.2 23.8 %collective-permute-start.12 = (bf16[128,2176]{1,0:T(8,128)(2,1)S(1)}, bf16[128,2176]{1,0:T(8,128)(2,1)S(1)}, u32[]{:S(2)}, u32[]{:S(2)}) collective-permute-start(bf16[128,2176]{1,0:T(8,128)(2,1)S(1)} %collective-permute-done.8.block_00.cols_00), channel_id=1, source_target_pairs={{0,2},{1,5},{2,0},{3,7},{4,6},{5,1},{6,4},{7,3},{8,10},{9,13},{10,... | collective-permute-start | bytes 1671176 | tf_op jit(solution)/shard_map/ppermute | solution.py:185
  54.7 29.0 %collective-permute-start.13 = (bf16[128,2176]{1,0:T(8,128)(2,1)}, bf16[128,2176]{1,0:T(8,128)(2,1)S(1)}, u32[]{:S(2)}, u32[]{:S(2)}) collective-permute-start(bf16[128,2176]{1,0:T(8,128)(2,1)} %collective-permute-done.9.block_10.cols_10), channel_id=1, source_target_pairs={{0,2},{1,5},{2,0},{3,7},{4,6},{5,1},{6,4},{7,3},{8,10},{9,13},{10,... | collective-permute-start | bytes 1671176 | tf_op jit(solution)/shard_map/ppermute | solution.py:185
  62.2 25.3 %collective-permute-start.14 = (bf16[2,96,2048]{2,1,0:T(8,128)(2,1)S(1)}, bf16[2,96,2048]{2,1,0:T(8,128)(2,1)S(1)}, u32[]{:S(2)}, u32[]{:S(2)}) collective-permute-start(bf16[2,96,2048]{2,1,0:T(8,128)(2,1)S(1)} %get-tuple-element.64), channel_id=1, source_target_pairs={{0,1},{1,0},{2,3},{3,2},{4,5},{5,4},{6,7},{7,6},{8,9},{9,8},{10,11... | collective-permute-start | bytes 2359304 | tf_op jit(solution)/shard_map/ppermute | solution.py:185
  75.3 12.2 %collective-permute-start.15 = (bf16[2,96,2048]{2,1,0:T(8,128)(2,1)S(1)}, bf16[2,96,2048]{2,1,0:T(8,128)(2,1)S(1)}, u32[]{:S(2)}, u32[]{:S(2)}) collective-permute-start(bf16[2,96,2048]{2,1,0:T(8,128)(2,1)S(1)} %get-tuple-element.65), channel_id=1, source_target_pairs={{0,1},{1,0},{2,3},{3,2},{4,5},{5,4},{6,7},{7,6},{8,9},{9,8},{10,11... | collective-permute-start | bytes 2359304 | tf_op jit(solution)/shard_map/ppermute | solution.py:185
  102.9 4.8 %collective-permute-start.17 = (bf16[2,288,2048]{2,1,0:T(8,128)(2,1)}, bf16[2,288,2048]{2,1,0:T(8,128)(2,1)S(1)}, u32[]{:S(2)}, u32[]{:S(2)}) collective-permute-start(bf16[2,288,2048]{2,1,0:T(8,128)(2,1)} %get-tuple-element.68), channel_id=1, source_target_pairs={{0,1},{1,0},{2,3},{3,2},{4,5},{5,4},{6,7},{7,6},{8,9},{9,8},{10,11... | collective-permute-start | bytes 7077896 | tf_op jit(solution)/shard_map/ppermute | solution.py:185
  103.3 12.0 %collective-permute-start.26 = (bf16[128,2176]{1,0:T(8,128)(2,1)}, bf16[128,2176]{1,0:T(8,128)(2,1)S(1)}, u32[]{:S(2)}, u32[]{:S(2)}) collective-permute-start(bf16[128,2176]{1,0:T(8,128)(2,1)} %collective-permute-done.11.block_10.cols_10), channel_id=1, source_target_pairs={{0,2},{1,5},{2,0},{3,7},{4,6},{5,1},{6,4},{7,3},{8,10},{9,13},{10,... | collective-permute-start | bytes 1671176 | tf_op jit(solution)/shard_map/ppermute | solution.py:185
  112.1 14.0 %collective-permute-start.21 = (bf16[256,2048]{1,0:T(8,128)(2,1)S(1)}, bf16[256,2048]{1,0:T(8,128)(2,1)S(1)}, u32[]{:S(2)}, u32[]{:S(2)}) collective-permute-start(bf16[256,2048]{1,0:T(8,128)(2,1)S(1)} %get-tuple-element.75), channel_id=1, source_target_pairs={{0,2},{1,5},{2,0},{3,7},{4,6},{5,1},{6,4},{7,3},{8,10},{9,13},{10,... | collective-permute-start | bytes 3145736 | tf_op jit(solution)/shard_map/ppermute | solution.py:185
  117.8 10.0 %collective-permute-start.27 = (bf16[2,96,2048]{2,1,0:T(8,128)(2,1)S(1)}, bf16[2,96,2048]{2,1,0:T(8,128)(2,1)}, u32[]{:S(2)}, u32[]{:S(2)}) collective-permute-start(bf16[2,96,2048]{2,1,0:T(8,128)(2,1)S(1)} %get-tuple-element.81), channel_id=1, source_target_pairs={{0,1},{1,0},{2,3},{3,2},{4,5},{5,4},{6,7},{7,6},{8,9},{9,8},{10,11... | collective-permute-start | bytes 2359304 | tf_op jit(solution)/shard_map/ppermute | solution.py:185
  119.0 24.0 %collective-permute-start.19 = (bf16[256,2048]{1,0:T(8,128)(2,1)S(1)}, bf16[256,2048]{1,0:T(8,128)(2,1)}, u32[]{:S(2)}, u32[]{:S(2)}) collective-permute-start(bf16[256,2048]{1,0:T(8,128)(2,1)S(1)} %get-tuple-element.72), channel_id=1, source_target_pairs={{0,2},{1,5},{2,0},{3,7},{4,6},{5,1},{6,4},{7,3},{8,10},{9,13},{10,... | collective-permute-start | bytes 3145736 | tf_op jit(solution)/shard_map/ppermute | solution.py:185
  126.5 20.1 %collective-permute-start.22 = (bf16[128,2048]{1,0:T(8,128)(2,1)S(1)}, bf16[128,2048]{1,0:T(8,128)(2,1)S(1)}, u32[]{:S(2)}, u32[]{:S(2)}) collective-permute-start(bf16[128,2048]{1,0:T(8,128)(2,1)S(1)} %fusion.14), channel_id=1, source_target_pairs={{0,4},{1,3},{2,6},{3,1},{4,0},{5,7},{6,2},{7,5},{8,12},{9,11},{10,... | collective-permute-start | bytes 1572872 | tf_op jit(solution)/shard_map/ppermute | solution.py:185
  136.3 10.8 %collective-permute-start.28 = (bf16[2,96,2048]{2,1,0:T(8,128)(2,1)}, bf16[2,96,2048]{2,1,0:T(8,128)(2,1)S(1)}, u32[]{:S(2)}, u32[]{:S(2)}) collective-permute-start(bf16[2,96,2048]{2,1,0:T(8,128)(2,1)} %get-tuple-element.83), channel_id=1, source_target_pairs={{0,1},{1,0},{2,3},{3,2},{4,5},{5,4},{6,7},{7,6},{8,9},{9,8},{10,11... | collective-permute-start | bytes 2359304 | tf_op jit(solution)/shard_map/ppermute | solution.py:185
  145.4 8.9 %collective-permute-start.20 = (bf16[128,2048]{1,0:T(8,128)(2,1)}, bf16[128,2048]{1,0:T(8,128)(2,1)}, u32[]{:S(2)}, u32[]{:S(2)}) collective-permute-start(bf16[128,2048]{1,0:T(8,128)(2,1)} %fusion.17), channel_id=1, source_target_pairs={{0,4},{1,3},{2,6},{3,1},{4,0},{5,7},{6,2},{7,5},{8,12},{9,11},{10,... | collective-permute-start | bytes 1572872 | tf_op jit(solution)/shard_map/ppermute | solution.py:185
  146.8 13.0 %collective-permute-start.23 = (bf16[128,2048]{1,0:T(8,128)(2,1)S(1)}, bf16[128,2048]{1,0:T(8,128)(2,1)S(1)}, u32[]{:S(2)}, u32[]{:S(2)}) collective-permute-start(bf16[128,2048]{1,0:T(8,128)(2,1)S(1)} %fusion.16), channel_id=1, source_target_pairs={{0,8},{1,9},{2,10},{3,11},{4,12},{5,13},{6,14},{7,15},{8,16},{9,17... | collective-permute-start | bytes 1572872 | tf_op jit(solution)/shard_map/ppermute | solution.py:185
  149.3 17.6 %collective-permute-start.29 = (bf16[256,2048]{1,0:T(8,128)(2,1)S(1)}, bf16[256,2048]{1,0:T(8,128)(2,1)S(1)}, u32[]{:S(2)}, u32[]{:S(2)}) collective-permute-start(bf16[256,2048]{1,0:T(8,128)(2,1)S(1)} %get-tuple-element.85), channel_id=1, source_target_pairs={{0,2},{1,5},{2,0},{3,7},{4,6},{5,1},{6,4},{7,3},{8,10},{9,13},{10,... | collective-permute-start | bytes 3145736 | tf_op jit(solution)/shard_map/ppermute | solution.py:185
  152.6 30.8 %collective-permute-start.18 = (bf16[256,2048]{1,0:T(8,128)(2,1)S(1)}, bf16[256,2048]{1,0:T(8,128)(2,1)S(1)}, u32[]{:S(2)}, u32[]{:S(2)}) collective-permute-start(bf16[256,2048]{1,0:T(8,128)(2,1)S(1)} %get-tuple-element.70), channel_id=1, source_target_pairs={{0,2},{1,5},{2,0},{3,7},{4,6},{5,1},{6,4},{7,3},{8,10},{9,13},{10,... | collective-permute-start | bytes 3145736 | tf_op jit(solution)/shard_map/ppermute | solution.py:185
  161.1 22.3 %collective-permute-start.24 = (bf16[128,2048]{1,0:T(8,128)(2,1)S(1)}, bf16[128,2048]{1,0:T(8,128)(2,1)S(1)}, u32[]{:S(2)}, u32[]{:S(2)}) collective-permute-start(bf16[128,2048]{1,0:T(8,128)(2,1)S(1)} %fusion.20), channel_id=1, source_target_pairs={{0,8},{1,9},{2,10},{3,11},{4,12},{5,13},{6,14},{7,15},{8,16},{9,17... | collective-permute-start | bytes 1572872 | tf_op jit(solution)/shard_map/ppermute | solution.py:185
  167.3 17.5 %collective-permute-start.30 = (bf16[128,2048]{1,0:T(8,128)(2,1)S(1)}, bf16[128,2048]{1,0:T(8,128)(2,1)S(1)}, u32[]{:S(2)}, u32[]{:S(2)}) collective-permute-start(bf16[128,2048]{1,0:T(8,128)(2,1)S(1)} %fusion.6), channel_id=1, source_target_pairs={{0,4},{1,3},{2,6},{3,1},{4,0},{5,7},{6,2},{7,5},{8,12},{9,11},{10,... | collective-permute-start | bytes 1572872 | tf_op jit(solution)/shard_map/ppermute | solution.py:185
  183.8 8.4 %collective-permute-start.25 = (bf16[128,2048]{1,0:T(8,128)(2,1)S(1)}, bf16[128,2048]{1,0:T(8,128)(2,1)S(1)}, u32[]{:S(2)}, u32[]{:S(2)}) collective-permute-start(bf16[128,2048]{1,0:T(8,128)(2,1)S(1)} %fusion.9), channel_id=1, source_target_pairs={{0,4},{1,3},{2,6},{3,1},{4,0},{5,7},{6,2},{7,5},{8,12},{9,11},{10,... | collective-permute-start | bytes 1572872 | tf_op jit(solution)/shard_map/ppermute | solution.py:185
  185.0 15.0 %collective-permute-start.31 = (bf16[128,2048]{1,0:T(8,128)(2,1)S(1)}, bf16[128,2048]{1,0:T(8,128)(2,1)S(1)}, u32[]{:S(2)}, u32[]{:S(2)}) collective-permute-start(bf16[128,2048]{1,0:T(8,128)(2,1)S(1)} %fusion.8), channel_id=1, source_target_pairs={{0,24},{1,25},{2,26},{3,27},{4,28},{5,29},{6,30},{7,31},{8,0},{9,1... | collective-permute-start | bytes 1572872 | tf_op jit(solution)/shard_map/ppermute | solution.py:185
  200.9 13.3 %collective-permute-start.33 = (bf16[128,2048]{1,0:T(8,128)(2,1)S(1)}, bf16[128,2048]{1,0:T(8,128)(2,1)S(1)}, u32[]{:S(2)}, u32[]{:S(2)}) collective-permute-start(bf16[128,2048]{1,0:T(8,128)(2,1)S(1)} %multiply_convert_fusion.refs_0_), channel_id=1, source_target_pairs={{0,2},{1,3},{2,0},{3,1},{4,6},{5,7},{6,4},{7,5},{8,10},{9,11},{10,... | collective-permute-start | bytes 1572872 | tf_op jit(solution)/shard_map/ppermute | solution.py:699
  202.0 23.5 %collective-permute-start.32 = (bf16[128,2048]{1,0:T(8,128)(2,1)S(1)}, bf16[128,2048]{1,0:T(8,128)(2,1)}, u32[]{:S(2)}, u32[]{:S(2)}) collective-permute-start(bf16[128,2048]{1,0:T(8,128)(2,1)S(1)} %multiply_convert_fusion.refs_0_), channel_id=1, source_target_pairs={{0,1},{1,0},{2,3},{3,2},{4,5},{5,4},{6,7},{7,6},{8,9},{9,8},{10,11... | collective-permute-start | bytes 1572872 | tf_op jit(solution)/shard_map/ppermute | solution.py:699
  202.8 16.4 %collective-permute-start.35 = (bf16[16,2048]{1,0:T(8,128)(2,1)S(1)}, bf16[16,2048]{1,0:T(8,128)(2,1)S(1)}, u32[]{:S(2)}, u32[]{:S(2)}) collective-permute-start(bf16[16,2048]{1,0:T(8,128)(2,1)S(1)} %slice.52), channel_id=1, source_target_pairs={{0,4},{4,8},{8,12},{12,16},{16,20},{20,24},{24,28},{1,5},{5,9},{9,... | collective-permute-start | bytes 196616 | tf_op jit(solution)/shard_map/ppermute | solution.py:24
  214.3 9.5 %collective-permute-start.34 = (bf16[128,2048]{1,0:T(8,128)(2,1)S(1)}, bf16[128,2048]{1,0:T(8,128)(2,1)S(1)}, u32[]{:S(2)}, u32[]{:S(2)}) collective-permute-start(bf16[128,2048]{1,0:T(8,128)(2,1)S(1)} %collective-permute-done.33.refs_2_), channel_id=1, source_target_pairs={{0,1},{1,0},{2,3},{3,2},{4,5},{5,4},{6,7},{7,6},{8,9},{9,8},{10,11... | collective-permute-start | bytes 1572872 | tf_op jit(solution)/shard_map/ppermute | solution.py:699
  219.1 3.8 %collective-permute-start.37 = (bf16[16,2048]{1,0:T(8,128)(2,1)S(1)}, bf16[16,2048]{1,0:T(8,128)(2,1)S(1)}, u32[]{:S(2)}, u32[]{:S(2)}) collective-permute-start(bf16[16,2048]{1,0:T(8,128)(2,1)S(1)} %collective-permute-done.35.refs_4_), channel_id=1, source_target_pairs={{0,2},{1,3},{2,0},{3,1},{4,6},{5,7},{6,4},{7,5},{8,10},{9,11},{10,... | collective-permute-start | bytes 196616 | tf_op jit(solution)/shard_map/ppermute | solution.py:699
  220.2 5.3 %collective-permute-start.36 = (bf16[16,2048]{1,0:T(8,128)(2,1)S(1)}, bf16[16,2048]{1,0:T(8,128)(2,1)S(1)}, u32[]{:S(2)}, u32[]{:S(2)}) collective-permute-start(bf16[16,2048]{1,0:T(8,128)(2,1)S(1)} %collective-permute-done.35.refs_4_), channel_id=1, source_target_pairs={{0,1},{1,0},{2,3},{3,2},{4,5},{5,4},{6,7},{7,6},{8,9},{9,8},{10,11... | collective-permute-start | bytes 196616 | tf_op jit(solution)/shard_map/ppermute | solution.py:699
  224.5 36.0 %collective-permute-start.40 = (bf16[256,2048]{1,0:T(8,128)(2,1)}, bf16[256,2048]{1,0:T(8,128)(2,1)S(1)}, u32[]{:S(2)}, u32[]{:S(2)}) collective-permute-start(bf16[256,2048]{1,0:T(8,128)(2,1)} %get-tuple-element.92), channel_id=1, source_target_pairs={{0,2},{1,3},{2,0},{3,1},{4,6},{5,7},{6,4},{7,5},{8,10},{9,11},{10,... | collective-permute-start | bytes 3145736 | tf_op jit(solution)/shard_map/ppermute | solution.py:699
  252.8 24.7 %collective-permute-start.43 = (bf16[256,2048]{1,0:T(8,128)(2,1)}, bf16[256,2048]{1,0:T(8,128)(2,1)S(1)}, u32[]{:S(2)}, u32[]{:S(2)}) collective-permute-start(bf16[256,2048]{1,0:T(8,128)(2,1)} %get-tuple-element.96), channel_id=1, source_target_pairs={{0,2},{1,3},{2,0},{3,1},{4,6},{5,7},{6,4},{7,5},{8,10},{9,11},{10,... | collective-permute-start | bytes 3145736 | tf_op jit(solution)/shard_map/ppermute | solution.py:699
  253.2 7.3 %collective-permute-start.39 = (bf16[4,128,256]{2,1,0:T(8,128)(2,1)S(1)}, bf16[4,128,256]{2,1,0:T(8,128)(2,1)S(1)}, u32[]{:S(2)}, u32[]{:S(2)}) collective-permute-start(bf16[4,128,256]{2,1,0:T(8,128)(2,1)S(1)} %get-tuple-element.91.mine_ref), channel_id=1, source_target_pairs={{0,4},{4,0},{8,12},{12,8},{16,20},{20,16},{24,28},{28,24},{1,5},{5... | collective-permute-start | bytes 786440 | tf_op jit(solution)/shard_map/ppermute | solution.py:769
  254.3 45.4 %collective-permute-start.48 = (bf16[512,2048]{1,0:T(8,128)(2,1)}, bf16[512,2048]{1,0:T(8,128)(2,1)}, u32[]{:S(2)}, u32[]{:S(2)}) collective-permute-start(bf16[512,2048]{1,0:T(8,128)(2,1)} %refs_4_.3), channel_id=1, source_target_pairs={{0,1},{1,0},{2,3},{3,2},{4,5},{5,4},{6,7},{7,6},{8,9},{9,8},{10,11... | collective-permute-start | bytes 6291464 | tf_op jit(solution)/shard_map/ppermute | solution.py:699
  260.8 6.0 %collective-permute-start.41 = (bf16[4,128,128]{2,1,0:T(8,128)(2,1)S(1)}, bf16[4,128,128]{2,1,0:T(8,128)(2,1)S(1)}, u32[]{:S(2)}, u32[]{:S(2)}) collective-permute-start(bf16[4,128,128]{2,1,0:T(8,128)(2,1)S(1)} %get-tuple-element.95), channel_id=1, source_target_pairs={{0,8},{4,12},{8,16},{12,20},{16,24},{20,28},{1,9},{5,13},{9,17},{1... | collective-permute-start | bytes 393224 | tf_op jit(solution)/shard_map/ppermute | solution.py:24
  267.0 6.0 %collective-permute-start.42 = (bf16[4,128,128]{2,1,0:T(8,128)(2,1)S(1)}, bf16[4,128,128]{2,1,0:T(8,128)(2,1)S(1)}, u32[]{:S(2)}, u32[]{:S(2)}) collective-permute-start(bf16[4,128,128]{2,1,0:T(8,128)(2,1)S(1)} %fusion), channel_id=1, source_target_pairs={{0,8},{4,12},{8,16},{12,20},{16,24},{20,28},{1,9},{5,13},{9,17},{1... | collective-permute-start | bytes 393224 | tf_op jit(solution)/shard_map/ppermute | solution.py:24
  277.4 5.7 %collective-permute-start.44 = (bf16[4,128,128]{2,1,0:T(8,128)(2,1)S(1)}, bf16[4,128,128]{2,1,0:T(8,128)(2,1)S(1)}, u32[]{:S(2)}, u32[]{:S(2)}) collective-permute-start(bf16[4,128,128]{2,1,0:T(8,128)(2,1)S(1)} %fusion.1), channel_id=1, source_target_pairs={{0,8},{4,12},{8,16},{12,20},{16,24},{20,28},{1,9},{5,13},{9,17},{1... | collective-permute-start | bytes 393224 | tf_op jit(solution)/shard_map/ppermute | solution.py:24
  283.2 16.5 %collective-permute-start.50 = (bf16[256,2048]{1,0:T(8,128)(2,1)S(1)}, bf16[256,2048]{1,0:T(8,128)(2,1)S(1)}, u32[]{:S(2)}, u32[]{:S(2)}) collective-permute-start(bf16[256,2048]{1,0:T(8,128)(2,1)S(1)} %collective-permute-done.43.refs_7_), channel_id=1, source_target_pairs={{0,1},{1,0},{2,3},{3,2},{4,5},{5,4},{6,7},{7,6},{8,9},{9,8},{10,11... | collective-permute-start | bytes 3145736 | tf_op jit(solution)/shard_map/ppermute | solution.py:699
  285.4 14.2 %collective-permute-start.49 = (bf16[256,2048]{1,0:T(8,128)(2,1)S(1)}, bf16[256,2048]{1,0:T(8,128)(2,1)}, u32[]{:S(2)}, u32[]{:S(2)}) collective-permute-start(bf16[256,2048]{1,0:T(8,128)(2,1)S(1)} %collective-permute-done.40.refs_6_), channel_id=1, source_target_pairs={{0,1},{1,0},{2,3},{3,2},{4,5},{5,4},{6,7},{7,6},{8,9},{9,8},{10,11... | collective-permute-start | bytes 3145736 | tf_op jit(solution)/shard_map/ppermute | solution.py:699
  291.6 5.1 %collective-permute-start.46 = (bf16[128,512]{1,0:T(8,128)(2,1)S(1)}, bf16[128,512]{1,0:T(8,128)(2,1)S(1)}, u32[]{:S(2)}, u32[]{:S(2)}) collective-permute-start(bf16[128,512]{1,0:T(8,128)(2,1)S(1)} %get-tuple-element.109), channel_id=1, source_target_pairs={{0,2},{1,3},{2,0},{3,1},{4,6},{5,7},{6,4},{7,5},{8,10},{9,11},{10,... | collective-permute-start | bytes 393224 | tf_op jit(solution)/shard_map/ppermute | solution.py:699
  292.6 7.1 %collective-permute-start.47 = (bf16[128,512]{1,0:T(8,128)(2,1)S(1)}, bf16[128,512]{1,0:T(8,128)(2,1)S(1)}, u32[]{:S(2)}, u32[]{:S(2)}) collective-permute-start(bf16[128,512]{1,0:T(8,128)(2,1)S(1)} %get-tuple-element.108), channel_id=1, source_target_pairs={{0,3},{1,2},{2,1},{3,0},{4,7},{5,6},{6,5},{7,4},{8,11},{9,10},{10,... | collective-permute-start | bytes 393224 | tf_op jit(solution)/shard_map/ppermute | solution.py:699
  (42 other events, 303.8 us)

commit v2 on v1

--- a/solution.py
+++ b/solution.py
@@ -131,33 +131,36 @@
         out_ref[0] = contract(hidden, down_ref[0], ((1,), (0,))).astype(bf16)
 
 
-def spread_kernel(
-    cols_00, cols_10, cols_01, cols_11, picker_ref, own_ref, got_ref, far_ref, near_ref, here_ref, *, slots
-):
-    local_experts, taken, _ = own_ref.shape
-    tok_rows = cols_00.shape[0]
-    pair = taken // 2
-    for at, pair_refs in enumerate(((cols_01, cols_11), (cols_00, cols_10))):
-        cols = jnp.concatenate([ref[...] for ref in pair_refs], axis=0)
-        weight_rows, picks = pair_routes(
-            cols, picker_ref[...], 2 * local_experts, tok_rows, slots
-        )
-        scaled = []
-        for line, pick in enumerate(picks):
-            result_ref = (own_ref, got_ref)[line // local_experts]
-            result = result_ref[line % local_experts, at * pair : (at + 1) * pair, :]
-            weight = jnp.sum(pick * weight_rows[line : line + 1], axis=1, keepdims=True)
-            scaled.append((result.astype(f32) * weight).astype(bf16))
-        summed = contract(
-            jnp.concatenate(picks, axis=0).astype(bf16),
-            jnp.concatenate(scaled, axis=0),
-            ((0,), (0,)),
-        ).astype(bf16)
-        if at == 0:
-            far_ref[...] = summed
-        else:
-            here_ref[...] = summed[:tok_rows]
-            near_ref[...] = summed[tok_rows:]
+def spread_kernel(*refs, slots, places):
+    *cols_refs, picker_ref, own_ref, got_ref, far_ref, near_ref, here_ref = refs
+    local_experts = own_ref.shape[0]
+    tok_rows = cols_refs[0].shape[0]
+    pair = 2 * slots
+    for group, place in enumerate(places):
+        cols_00, cols_10, cols_01, cols_11 = cols_refs[4 * group : 4 * group + 4]
+        for at, pair_refs in enumerate(((cols_01, cols_11), (cols_00, cols_10))):
+            cols = jnp.concatenate([ref[...] for ref in pair_refs], axis=0)
+            weight_rows, picks = pair_routes(
+                cols, picker_ref[...], 2 * local_experts, tok_rows, slots
+            )
+            first = (2 * place + at) * pair
+            scaled = []
+            for line, pick in enumerate(picks):
+                result_ref = (own_ref, got_ref)[line // local_experts]
+                result = result_ref[line % local_experts, first : first + pair, :]
+                weight = jnp.sum(pick * weight_rows[line : line + 1], axis=1, keepdims=True)
+                scaled.append((result.astype(f32) * weight).astype(bf16))
+            summed = contract(
+                jnp.concatenate(picks, axis=0).astype(bf16),
+                jnp.concatenate(scaled, axis=0),
+                ((0,), (0,)),
+            ).astype(bf16)
+            if at == 0:
+                far_ref[group, 0] = summed[:tok_rows]
+                far_ref[group, 1] = summed[tok_rows:]
+            else:
+                here_ref[group] = summed[:tok_rows]
+                near_ref[group] = summed[tok_rows:]
 
 
 def expert_layer_gathered(
@@ -169,6 +172,7 @@
     expert_up,
     expert_down,
     sources,
+    early,
 ):
     tok_rows, width = stream.shape
     local_experts, _, hidden_width = expert_gate.shape
@@ -247,7 +251,7 @@
             in_specs=[whole_ref(packet)] * 4 + [whole_ref(picker)],
             out_specs=[picked_spec] * 2,
             out_shape=[jax.ShapeDtypeStruct((local_experts, taken, width), bf16)] * 2,
-            compiler_params=pltpu.CompilerParams(vmem_limit_bytes=48 << 20),
+            compiler_params=pltpu.CompilerParams(vmem_limit_bytes=24 << 20),
             cost_estimate=worth(2),
             name="collect",
         )(after(rows, *earlier) if earlier else rows, *blocks[steps][1:], picker)
@@ -269,7 +273,7 @@
             out_specs=[out_spec] * 2,
             out_shape=[jax.ShapeDtypeStruct((local_experts, len(members) * taken, width), bf16)]
             * 2,
-            compiler_params=pltpu.CompilerParams(vmem_limit_bytes=56 << 20),
+            compiler_params=pltpu.CompilerParams(vmem_limit_bytes=40 << 20),
             cost_estimate=worth(4 + 3 * len(members)),
             name="experts",
         )(
@@ -284,54 +288,53 @@
         for at, member in enumerate(members):
             outcome[member] = (at, results, got_back)
 
-    def spread(steps):
-        at, results, got_back = outcome[steps]
-        result_spec = pl.BlockSpec((local_experts, taken, width), lambda g: (0, at, 0))
+    def spread(members):
+        places = [outcome[member][0] for member in members]
+        _, results, got_back = outcome[members[0]]
         cols_spec = pl.BlockSpec(
             (tok_rows, 2 * experts_all), lambda g: (0, width // (2 * experts_all))
         )
-        row_shape = jax.ShapeDtypeStruct((tok_rows, width), bf16)
-        far_shape = jax.ShapeDtypeStruct((2 * tok_rows, width), bf16)
+        row_shape = jax.ShapeDtypeStruct((len(members), tok_rows, width), bf16)
+        far_shape = jax.ShapeDtypeStruct((len(members), 2, tok_rows, width), bf16)
         return pl.pallas_call(
-            functools.partial(spread_kernel, slots=slots),
+            functools.partial(spread_kernel, slots=slots, places=places),
             grid=(1,),
-            in_specs=[cols_spec] * 4 + [whole_ref(picker), result_spec, result_spec],
+            in_specs=[cols_spec] * (4 * len(members))
+            + [whole_ref(picker), whole_ref(results), whole_ref(results)],
             out_specs=[whole_ref(far_shape), whole_ref(row_shape), whole_ref(row_shape)],
             out_shape=[far_shape, row_shape, row_shape],
-            compiler_params=pltpu.CompilerParams(vmem_limit_bytes=48 << 20),
-            cost_estimate=worth(3),
+            compiler_params=pltpu.CompilerParams(vmem_limit_bytes=28 << 20),
+            cost_estimate=worth(3 * len(members)),
             name="spread",
-        )(*blocks[steps], picker, results, got_back)
-
-    last = order[-1]
+        )(*(block for member in members for block in blocks[member]), picker, results, got_back)
+
+    last, batch = order[-1], order[-2:0:-1]
     for steps in order[:-2]:
         collect(steps, blocks[order[-2]][0])
     collect(order[-2], *blocks[last][:3])
     run_experts(order[:-1])
-    back = order[-2:0:-1]
-    ready = {steps: spread(steps) for steps in back}
-    collect(last, *[far for far, _, _ in ready.values()])
+    far, near, here = spread(batch)
+    collect(last, far)
     run_experts([last])
-    back += [last, 0]
-    carried = {}
-    total = 0.0
-    for at, steps in enumerate(back):
-        far, near, here = ready[steps] if steps in ready else spread(steps)
-        across = second(far)
-        if at >= 2 and back[at - 2] in carried:
-            across = after(across, carried[back[at - 2]])
-        across = across.astype(f32)
-        near = first((near.astype(f32) + across[tok_rows:]).astype(bf16))
-        here = here.astype(f32) + across[:tok_rows] + near.astype(f32)
-        if steps > 2:
-            here += carried.pop(steps - 1).astype(f32)
-        if steps:
-            carried[steps] = lifted(here.astype(bf16), -1 if steps == 1 else 1)
-        else:
-            total = here
-    for arrived in carried.values():
-        total += arrived.astype(f32)
-    return total.astype(bf16)
+    far_last, near_last, here_last = spread([last])
+    far_own, near_own, here_own = spread([0])
+
+    def joined(near, here, direct, diagonal):
+        near = first((near.astype(f32) + diagonal.astype(f32)).astype(bf16))
+        return here.astype(f32) + direct.astype(f32) + near.astype(f32)
+
+    across = after(second(far), far_last, far_own)
+    sums = joined(near, here, across[:, 0], across[:, 1])
+    moving = lifted(sums[0].astype(bf16), 1)
+    for at in range(1, len(batch)):
+        moving = lifted((sums[at] + moving.astype(f32)).astype(bf16), 1)
+    across = second(far_last)
+    sums = joined(near_last, here_last, across[:, 0], across[:, 1])
+    rising = lifted(sums[0].astype(bf16), -1)
+    diagonal = after(second(far_own[0, 1]), moving)
+    total = joined(near_own[0], here_own[0], second(far_own[0, 0]), diagonal)
+    total += moving.astype(f32) + rising.astype(f32)
+    return after(total, *early).astype(bf16)
 
 
 def expert_layer_sent(
@@ -444,11 +447,15 @@
 
 
 def delta_kernel(
-    raw_ref,
+    place_ref,
+    near_raw,
+    far_raw,
+    near_beta,
+    far_beta,
+    near_decay,
+    far_decay,
     rim_ref,
     taps_ref,
-    beta_ref,
-    decay_ref,
     rate_ref,
     core_ref,
     reading_ref,
@@ -461,14 +468,25 @@
     *,
     key_heads,
     chunk,
+    tok_rows,
 ):
-    rows, conv_cols = raw_ref.shape
+    rows, conv_cols = near_raw.shape[0] + far_raw.shape[0], near_raw.shape[1]
     heads = moved_ref.shape[0]
     group = heads // key_heads
     tap_count = taps_ref.shape[0]
     rim = rim_ref.shape[0]
     extended[0:rim, :] = rim_ref[...]
-    extended[rim : rim + rows, :] = raw_ref[...].astype(f32)
+    step = 0
+    for part_refs in ((near_raw, near_beta, near_decay), (far_raw, far_beta, far_decay)):
+        for first in range(0, part_refs[0].shape[0], tok_rows):
+            at = pl.multiple_of((place_ref[0] ^ step) * tok_rows, tok_rows)
+            part = slice(first, first + tok_rows)
+            extended[pl.ds(rim + at, tok_rows), :] = part_refs[0][part, :].astype(f32)
+            strengths[pl.ds(at, tok_rows), :] = 1.0 / (1.0 + jnp.exp(-part_refs[1][part, :]))
+            shifted = part_refs[2][part, :] + rate_ref[1:2, :]
+            softened = jnp.maximum(shifted, 0.0) + jnp.log1p(jnp.exp(-jnp.abs(shifted)))
+            falls[pl.ds(at, tok_rows), :] = -jnp.exp(rate_ref[0:1, :]) * softened
+            step += 1
     key_at, value_at = key_heads * DK, 2 * key_heads * DK
     for start in range(0, rows, chunk):
         for first in range(0, conv_cols, DK):
@@ -485,11 +503,6 @@
             elif first < value_at:
                 value = unit_rows(value)
             mixed[start : start + chunk, columns] = value
-    strengths[...] = 1.0 / (1.0 + jnp.exp(-beta_ref[...]))
-    shifted = decay_ref[...] + rate_ref[1:2, :]
-    softened = jnp.maximum(shifted, 0.0) + jnp.log1p(jnp.exp(-jnp.abs(shifted)))
-    falls[...] = -jnp.exp(rate_ref[0:1, :]) * softened
-
     row = lax.broadcasted_iota(jnp.int32, (chunk, chunk), 0)
     col = lax.broadcasted_iota(jnp.int32, (chunk, chunk), 1)
     inclusive, strict = row >= col, row > col
@@ -577,37 +590,32 @@
     moved_ref[...] = carried[...].astype(bf16)
 
 
-def project_kernel(place_ref, *refs, blocks):
-    piece_refs, halo_refs = refs[:blocks], refs[blocks : 2 * blocks]
-    weight_refs, out_refs = refs[2 * blocks : -5], refs[-5:]
-    qkv_ref, gate_ref, beta_ref, decay_ref, rim_ref = out_refs
-    tok_rows = piece_refs[0].shape[0]
-    halo_rows = halo_refs[0].shape[0]
-    halo = sum(
-        jnp.where((place_ref[0] ^ step) == blocks - 1, 1.0, 0.0) * halo_refs[step][...].astype(f32)
-        for step in range(blocks)
-    ).astype(bf16)
-    rows = jnp.concatenate([ref[...] for ref in piece_refs] + [halo], axis=0)
-
-    def store(out_ref, first, weight_ref):
-        product = contract(rows, weight_ref[...], ((1,), (0,))).astype(out_ref.dtype)
-        last = first + product.shape[1]
-        for step in range(blocks):
-            at = pl.multiple_of((place_ref[0] ^ step) * tok_rows, tok_rows)
-            out_ref[pl.ds(at, tok_rows), first:last] = product[
-                step * tok_rows : (step + 1) * tok_rows
-            ]
-        return product[blocks * tok_rows :]
-
+def project_kernel(place_ref, *refs, blocks, halos):
+    row_refs, halo_refs = refs[:blocks], refs[blocks : blocks + halos]
+    weight_refs, out_refs = refs[blocks + halos : blocks + halos + 6], refs[blocks + halos + 6 :]
+    pieces = [ref[...] for ref in row_refs]
+    rows = blocks * row_refs[0].shape[0]
+    if halos:
+        pieces.append(
+            sum(
+                jnp.where((place_ref[0] ^ step) == halos - 1, 1.0, 0.0) * ref[...].astype(f32)
+                for step, ref in enumerate(halo_refs)
+            ).astype(bf16)
+        )
+    pieces = jnp.concatenate(pieces, axis=0)
+    qkv_ref, gate_ref, beta_ref, decay_ref = out_refs[:4]
     first = 0
     for weight_ref in weight_refs[:3]:
-        rim = store(qkv_ref, first, weight_ref)
+        product = contract(pieces, weight_ref[...], ((1,), (0,))).astype(bf16)
         last = first + weight_ref.shape[1]
-        rim_ref[:, first:last] = rim.astype(f32)
+        qkv_ref[:, first:last] = product[:rows]
+        if halos:
+            out_refs[4][:, first:last] = product[rows:].astype(f32)
         first = last
-    store(gate_ref, 0, weight_refs[3])
-    store(beta_ref, 0, weight_refs[4])
-    store(decay_ref, 0, weight_refs[5])
+    pieces = pieces[:rows]
+    gate_ref[...] = contract(pieces, weight_refs[3][...], ((1,), (0,))).astype(bf16)
+    beta_ref[...] = contract(pieces, weight_refs[4][...], ((1,), (0,)))
+    decay_ref[...] = contract(pieces, weight_refs[5][...], ((1,), (0,)))
 
 
 def pair_kernel(second_ref, mine_ref, other_ref, moved_ref, transfer_ref):
@@ -622,7 +630,7 @@
 
 
 def finish_kernel(
-    second_ref, state_ref, other_ref, core_ref, reading_ref, gate_ref, gain_ref, gated_ref
+    where_ref, state_ref, other_ref, core_ref, reading_ref, gate_ref, gain_ref, gated_ref
 ):
     states = []
     for head in range(state_ref.shape[0]):
@@ -630,7 +638,7 @@
         passed = contract(other_ref[head, :, DK:], state, ((1,), (0,))) + other_ref[
             head, :, :DK
         ].astype(f32)
-        states.append(jnp.where(second_ref[0] == 1, passed, state.astype(f32)))
+        states.append(jnp.where(where_ref[0] == 1, passed, state.astype(f32)))
     for head, state in enumerate(states):
         columns = slice(head * DK, (head + 1) * DK)
         core = core_ref[:, columns] + contract_close(reading_ref[:, columns], state)
@@ -643,9 +651,9 @@
         gated_ref[:, columns] = (normal * (gate / (1.0 + jnp.exp(-gate)))).astype(bf16)
 
 
-def output_kernel(*refs, blocks):
-    row_refs, weight_refs, out_ref = refs[:blocks], refs[blocks:-1], refs[-1]
-    total = 0.0
+def output_kernel(*refs, blocks, begun):
+    row_refs, weight_refs, out_ref = refs[:blocks], refs[blocks : -1 - begun], refs[-1]
+    total = refs[-2][...] if begun else 0.0
     pieces = iter(weight_refs)
     for rows_ref in row_refs:
         at = 0
@@ -654,7 +662,7 @@
             depth = weight_ref.shape[0]
             total += contract(rows_ref[:, at : at + depth], weight_ref[...], ((1,), (0,)))
             at += depth
-    out_ref[...] = total.astype(bf16)
+    out_ref[...] = total.astype(out_ref.dtype)
 
 
 def on_device(
@@ -685,8 +693,10 @@
     sources = ctx_count * head_count
     ctx_place = lax.axis_index("ctx")
     experts = (stream, moe_gain, router, expert_ids, expert_gate, expert_up, expert_down)
+    cut = out_weight.shape[0] * 5 // 128 * 16
+    out_halves = (out_weight[:cut], out_weight[cut:])
     if 2 * sources * stream.size <= GATHER_LIMIT and head_count == 4 and ctx_count in (6, 8):
-        moe_out = expert_layer_gathered(*experts, sources)
+        moe_out = expert_layer_gathered(*experts, sources, out_halves)
     else:
         moe_out = expert_layer_sent(*experts, sources)
     mixer_in = rms_rows(
@@ -698,11 +708,15 @@
         pairs = [(source, source ^ step) for source in range(head_count)]
         return lax.ppermute(value, "head", pairs)
 
-    def from_all(value):
-        across = [crossed(value, step) for step in range(2, head_count, 2)]
-        received = [value, crossed(value, 1)]
-        for part in across:
-            received += [part, crossed(part, 1)]
+
+    def from_chip(value, *earlier):
+        return [after(value, *earlier) if earlier else value, crossed(value, 1)]
+
+    def from_others(value, *earlier):
+        received = []
+        for step in range(2, head_count, 2):
+            part = crossed(value, step)
+            received += [part, crossed(after(part, *earlier) if earlier else part, 1)]
         return received
 
     in_vmem = pl.BlockSpec(memory_space=pltpu.VMEM)
@@ -712,39 +726,44 @@
     key_cols, value_cols = query_weight.shape[1], value_weight.shape[1]
     heads = beta_weight.shape[1]
     rim_len = 16
-    halos = from_all(passed_along(mixer_in[tok_rows - rim_len :], "ctx", 1))
-    pieces = from_all(mixer_in)
+    halo = passed_along(mixer_in[tok_rows - rim_len :], "ctx", 1)
+    halos = from_chip(halo) + from_others(halo)
     conv_cols = 2 * key_cols + value_cols
-    qkv_raw, gate_raw, beta_raw, decay_raw, rim = pl.pallas_call(
-        functools.partial(project_kernel, blocks=head_count),
-        in_specs=[in_smem] + [in_vmem] * (2 * head_count + 6),
-        out_shape=[
-            jax.ShapeDtypeStruct((rows, conv_cols), bf16),
-            jax.ShapeDtypeStruct((rows, value_cols), bf16),
-            jax.ShapeDtypeStruct((rows, heads), f32),
-            jax.ShapeDtypeStruct((rows, heads), f32),
-            jax.ShapeDtypeStruct((rim_len, conv_cols), f32),
-        ],
-        compiler_params=pltpu.CompilerParams(vmem_limit_bytes=48 << 20),
-        cost_estimate=worth(5),
-        name="project",
-    )(
-        head_place.reshape(1),
-        *pieces,
-        *halos,
-        query_weight,
-        key_weight,
-        value_weight,
-        output_gate,
-        beta_weight,
-        decay_weight,
-    )
+    matrices = (
+        query_weight, key_weight, value_weight, output_gate, beta_weight, decay_weight
+    )
+
+    def project(pieces, halos):
+        count = len(pieces) * tok_rows
+        shapes = [
+            jax.ShapeDtypeStruct((count, conv_cols), bf16),
+            jax.ShapeDtypeStruct((count, value_cols), bf16),
+            jax.ShapeDtypeStruct((count, heads), f32),
+            jax.ShapeDtypeStruct((count, heads), f32),
+        ]
+        if halos:
+            shapes.append(jax.ShapeDtypeStruct((rim_len, conv_cols), f32))
+        return pl.pallas_call(
+            functools.partial(project_kernel, blocks=len(pieces), halos=len(halos)),
+            in_specs=[in_smem] + [in_vmem] * (len(pieces) + len(halos) + 6),
+            out_shape=shapes,
+            compiler_params=pltpu.CompilerParams(vmem_limit_bytes=28 << 20),
+            cost_estimate=worth(4),
+            name="project",
+        )(head_place.reshape(1), *pieces, *halos, *matrices)
+
+    near_raw = project(from_chip(mixer_in, halo), [])
+    far_pieces = from_others(mixer_in, near_raw[0], halos[2])
+    far_raw = project(far_pieces, halos)
+    rim = far_raw[4]
+    gate_raw = jnp.concatenate([near_raw[1], far_raw[1]], axis=0)
     key_heads = key_cols // DK
     taps = jnp.concatenate([query_conv, key_conv, value_conv], axis=1)
     rates = jnp.stack([decay_log, decay_bias])
     chunk = math.gcd(rows, CHUNK)
     core, reading, moved = pl.pallas_call(
-        functools.partial(delta_kernel, key_heads=key_heads, chunk=chunk),
+        functools.partial(delta_kernel, key_heads=key_heads, chunk=chunk, tok_rows=tok_rows),
+        in_specs=[in_smem] + [in_vmem] * 9,
         out_shape=(
             jax.ShapeDtypeStruct((rows, value_cols), f32),
             jax.ShapeDtypeStruct((rows, value_cols), f32),
@@ -757,13 +776,19 @@
             pltpu.VMEM((rows, heads), f32),
             pltpu.VMEM((heads, DK, 2 * DK), f32),
         ],
-        compiler_params=pltpu.CompilerParams(vmem_limit_bytes=48 << 20),
+        compiler_params=pltpu.CompilerParams(vmem_limit_bytes=24 << 20),
         cost_estimate=worth(16),
         name="delta",
-    )(qkv_raw, rim, taps, beta_raw, decay_raw, rates)
-    half = out_weight.shape[0] // 2
-    upper = [crossed(after(out_weight[:half], pieces[-1]), step) for step in range(2, head_count, 2)]
-    lower = [crossed(after(out_weight[half:], moved), step) for step in range(2, head_count, 2)]
+    )(
+        head_place.reshape(1),
+        *(array for kind in (0, 2, 3) for array in (near_raw[kind], far_raw[kind])),
+        rim,
+        taps,
+        rates,
+    )
+    start_upper, start_lower = after(out_halves[0], far_pieces[-1]), after(out_halves[1], moved)
+    upper = [crossed(start_upper, step) for step in range(2, head_count, 2)]
+    lower = [crossed(start_lower, step) for step in range(2, head_count, 2)]
 
     in_pair = (ctx_place % 2).reshape(1)
     other = lax.ppermute(moved, "ctx", [(place, place ^ 1) for place in range(ctx_count)])
@@ -773,7 +798,7 @@
         pair_kernel,
         in_specs=[in_smem, in_vmem, in_vmem],
         out_shape=[state_shape, state_shape],
-        compiler_params=pltpu.CompilerParams(vmem_limit_bytes=48 << 20),
+        compiler_params=pltpu.CompilerParams(vmem_limit_bytes=8 << 20),
         name="pair",
     )(in_pair, moved, other)
     state = passed_along(added, "ctx", 2)
@@ -786,33 +811,57 @@
 
     gated = pl.pallas_call(
         finish_kernel,
-        grid=(head_count,),
-        in_specs=[in_smem, whole_ref(state), whole_ref(other)]
-        + [pl.BlockSpec((tok_rows, value_cols), lambda block: (block, 0))] * 3
-        + [pl.BlockSpec((1, DK), lambda block: (0, 0))],
-        out_specs=pl.BlockSpec((tok_rows, value_cols), lambda block: (block, 0)),
+        grid_spec=pltpu.PrefetchScalarGridSpec(
+            num_scalar_prefetch=1,
+            grid=(head_count,),
+            in_specs=[whole_ref(state), whole_ref(other)]
+            + [
+                pl.BlockSpec((tok_rows, value_cols), lambda step, where: (where[1] ^ step, 0)),
+                pl.BlockSpec((tok_rows, value_cols), lambda step, where: (where[1] ^ step, 0)),
+                pl.BlockSpec((tok_rows, value_cols), lambda step, where: (step, 0)),
+                pl.BlockSpec((1, DK), lambda step, where: (0, 0)),
+            ],
+            out_specs=pl.BlockSpec((tok_rows, value_cols), lambda step, where: (step, 0)),
+        ),
         out_shape=jax.ShapeDtypeStruct((rows, value_cols), bf16),
-        compiler_params=pltpu.CompilerParams(vmem_limit_bytes=48 << 20),
+        compiler_params=pltpu.CompilerParams(vmem_limit_bytes=12 << 20),
         name="finish",
-    )(in_pair, state, other, core, reading, gate_raw, head_gain.reshape(1, -1))
+    )(
+        jnp.stack([ctx_place % 2, head_place]),
+        state,
+        other,
+        core,
+        reading,
+        gate_raw,
+        head_gain.reshape(1, -1),
+    )
     gated_parts = []
     for step in range(head_count):
-        part = lax.dynamic_slice_in_dim(gated, (head_place ^ step) * tok_rows, tok_rows, axis=0)
+        part = gated[step * tok_rows : (step + 1) * tok_rows]
         gated_parts.append(crossed(part, step) if step else part)
-    weight_parts = [out_weight, crossed(after(out_weight, moved), 1)]
-    for near_pair in zip(upper, lower):
-        weight_parts += near_pair
-        weight_parts += [crossed(after(part, state), 1) for part in near_pair]
-    mixer_out = pl.pallas_call(
-        functools.partial(output_kernel, blocks=head_count),
-        grid=(4,),
-        in_specs=[whole_ref(part) for part in gated_parts]
-        + [pl.BlockSpec((part.shape[0], width // 4), lambda n: (0, n)) for part in weight_parts],
-        out_specs=pl.BlockSpec((tok_rows, width // 4), lambda n: (0, n)),
-        out_shape=jax.ShapeDtypeStruct(stream.shape, bf16),
-        compiler_params=pltpu.CompilerParams(vmem_limit_bytes=48 << 20),
-        name="output",
-    )(*gated_parts, *weight_parts)
+    near_weights = [out_weight, crossed(after(out_weight, moved), 1)]
+    far_weights = []
+    for shard in zip(upper, lower):
+        far_weights += shard
+        far_weights += [crossed(after(part, state), 1) for part in shard]
+
+    def multiplied(parts, weights, begun, kind):
+        columns = pl.BlockSpec((tok_rows, width // 4), lambda n: (0, n))
+        return pl.pallas_call(
+            functools.partial(output_kernel, blocks=len(parts), begun=len(begun)),
+            grid=(4,),
+            in_specs=[whole_ref(part) for part in parts]
+            + [pl.BlockSpec((part.shape[0], width // 4), lambda n: (0, n)) for part in weights]
+            + [columns] * len(begun),
+            out_specs=columns,
+            out_shape=jax.ShapeDtypeStruct(stream.shape, kind),
+            compiler_params=pltpu.CompilerParams(vmem_limit_bytes=20 << 20),
+            cost_estimate=worth(3),
+            name="output",
+        )(*parts, *weights, *begun)
+
+    begun = multiplied(gated_parts[:2], near_weights, [], f32)
+    mixer_out = multiplied(gated_parts[2:], far_weights, [begun], bf16)
     return (moe_out, mixer_out)
 
 

time: 306 us -> 307 us (level)
  starting transfers between devices: 45.8 us -> 55.4 us
  Pallas kernels: 70.9 us -> 66.5 us
    ppermute x14, waiting for transfers between devices: 22.2 us -> 6.16 us  [crossed(): return lax.ppermute(value, 'head', pairs)]
    ppermute x14, starting transfers between devices: 11.4 us -> 25.1 us  [crossed(): return lax.ppermute(value, 'head', pairs)]
    ppermute x32 -> x31, waiting for transfers between devices: 117 us -> 126 us  [sent(): return lax.ppermute(value, ('ctx', 'head'), pairs)]
    pallas_call x2, Pallas kernels: 21.1 us -> 16.6 us  [run_experts(): pl.pallas_call(expert_kernel, grid=(local_experts,), in_specs=[row_spec]...]
    unnamed x80 -> x66, local copies, waits for them, and re-layouts: 14.6 us -> 11.4 us
    ppermute x32 -> x31, starting transfers between devices: 26.7 us -> 24.2 us  [sent(): return lax.ppermute(value, ('ctx', 'head'), pairs)]
    pallas_call x7 -> x8, Pallas kernels: 25.5 us -> 24.3 us  [the longest x2 7.43 us: multiplied(): pl.pallas_call(functools.partial(output_kernel, blocks=len(parts), begun=...]
  transfers between devices with their start and end apart: 51 -> 50, of which waited for: 32 -> 29; matrix products, arithmetic and copies ran while one was open for 3% -> 3% of each run, Pallas kernels for 18% -> 17%
where the time goes in v2:
time: 307 us; the launch traced here: 304 us
  waiting for transfers between devices  156 us (51%)
  Pallas kernels  66.5 us (22%)
  starting transfers between devices  55.4 us (18%)
  local copies, waits for them, and re-layouts  15.6 us (5%)
  other arithmetic  9.51 us (3%)
    ppermute x31, waiting for transfers between devices, sent(): return lax.ppermute(value, ('ctx', 'head'), pairs)  126 us
    ppermute x14, starting transfers between devices, crossed(): return lax.ppermute(value, 'head', pairs)  25.1 us
    ppermute x31, starting transfers between devices, sent(): return lax.ppermute(value, ('ctx', 'head'), pairs)  24.2 us
    pallas_call x2, Pallas kernels, run_experts(): pl.pallas_call(expert_kernel, grid=(local_experts,), in_specs=[row_spec]...  16.6 us
    ppermute x4, waiting for transfers between devices, passed_along(): lax.ppermute(value, axis, [(source, source + steps) for source in range(f...  16.4 us
    pallas_call x1, Pallas kernels, on_device(): pl.pallas_call(functools.partial(delta_kernel, key_heads=key_heads, chunk...  16.4 us
    unnamed x66, local copies, waits for them, and re-layouts  11.4 us
    pallas_call x4, Pallas kernels, collect(): pl.pallas_call(functools.partial(collect_kernel, slots=slots), grid=(1,),...  8.01 us
  transfers between devices with their start and end apart: 50, of which 29 were waited for; matrix products, arithmetic and copies ran while one was open for 3% of the time, Pallas kernels for 17%

profile of v2, /device:TPU:25, one launch (start us, length us, event | category | flops | bytes accessed | tf_op | source)
XLA Modules:
  0.0 304.5 jit_solution(2114850379773251893)
XLA Ops:
  7.5 9.3 %collective-permute-done.block_10.refs_1_ = bf16[128,2176]{1,0:T(8,128)(2,1)S(1)} collective-permute-done((bf16[128,2176]{1,0:T(8,128)(2,1)S(1)}, bf16[128,2176]{1,0:T(8,128)(2,1)S(1)}, u32[]{:S(2)}, u32[]{:S(2)}) %collective-permute-start) | collective-permute-done | bytes 557088 | tf_op jit(solution)/shard_map/ppermute | solution.py:189
  16.8 3.9 %collective-permute-done.1.block_01.refs_2_ = bf16[128,2176]{1,0:T(8,128)(2,1)S(1)} collective-permute-done((bf16[128,2176]{1,0:T(8,128)(2,1)S(1)}, bf16[128,2176]{1,0:T(8,128)(2,1)S(1)}, u32[]{:S(2)}, u32[]{:S(2)}) %collective-permute-start.1) | collective-permute-done | bytes 557088 | tf_op jit(solution)/shard_map/ppermute | solution.py:189
  22.5 11.1 %collective-permute-done.5.block_10.refs_5_ = bf16[128,2176]{1,0:T(8,128)(2,1)} collective-permute-done((bf16[128,2176]{1,0:T(8,128)(2,1)S(1)}, bf16[128,2176]{1,0:T(8,128)(2,1)}, u32[]{:S(2)}, u32[]{:S(2)}) %collective-permute-start.5) | collective-permute-done | bytes 557088 | tf_op jit(solution)/shard_map/ppermute | solution.py:189
  33.5 2.3 collective-permute-done.4.block_00.refs_0_
  36.7 2.4 collective-permute-start.8
  41.1 9.1 %collective-permute-done.8.block_00.refs_0_ = bf16[128,2176]{1,0:T(8,128)(2,1)S(1)} collective-permute-done((bf16[128,2176]{1,0:T(8,128)(2,1)S(1)}, bf16[128,2176]{1,0:T(8,128)(2,1)S(1)}, u32[]{:S(2)}, u32[]{:S(2)}) %collective-permute-start.8) | collective-permute-done | bytes 557088 | tf_op jit(solution)/shard_map/ppermute | solution.py:189
  50.2 1.8 collective-permute-done.9.block_10.refs_1_
  55.8 5.3 %collective-permute-done.2.block_11.refs_3_ = bf16[128,2176]{1,0:T(8,128)(2,1)} collective-permute-done((bf16[128,2176]{1,0:T(8,128)(2,1)S(1)}, bf16[128,2176]{1,0:T(8,128)(2,1)}, u32[]{:S(2)}, u32[]{:S(2)}) %collective-permute-start.2) | collective-permute-done | bytes 557088 | tf_op jit(solution)/shard_map/ppermute | solution.py:189
  61.1 2.1 collect.4
  63.3 3.5 %collective-permute-start.14 = (bf16[2,96,2048]{2,1,0:T(8,128)(2,1)S(1)}, bf16[2,96,2048]{2,1,0:T(8,128)(2,1)S(1)}, u32[]{:S(2)}, u32[]{:S(2)}) collective-permute-start(bf16[2,96,2048]{2,1,0:T(8,128)(2,1)S(1)} %get-tuple-element.69), channel_id=1, source_target_pairs={{0,1},{1,0},{2,3},{3,2},{4,5},{5,4},{6,7},{7,6},{8,9},{9,8},{10,11... | collective-permute-start | bytes 2359304 | tf_op jit(solution)/shard_map/ppermute | solution.py:189
  66.7 5.3 %collective-permute-done.7.block_11.refs_7_ = bf16[128,2176]{1,0:T(8,128)(2,1)} collective-permute-done((bf16[128,2176]{1,0:T(8,128)(2,1)}, bf16[128,2176]{1,0:T(8,128)(2,1)}, u32[]{:S(2)}, u32[]{:S(2)}) %collective-permute-start.7) | collective-permute-done | bytes 557088 | tf_op jit(solution)/shard_map/ppermute | solution.py:189
  72.1 2.3 collect.5
  74.7 3.3 %collective-permute-done.12.block_01.refs_2_ = bf16[128,2176]{1,0:T(8,128)(2,1)S(1)} collective-permute-done((bf16[128,2176]{1,0:T(8,128)(2,1)S(1)}, bf16[128,2176]{1,0:T(8,128)(2,1)S(1)}, u32[]{:S(2)}, u32[]{:S(2)}) %collective-permute-start.12) | collective-permute-done | bytes 557088 | tf_op jit(solution)/shard_map/ppermute | solution.py:189
  78.0 5.7 %collective-permute-done.13.block_11.refs_3_ = bf16[128,2176]{1,0:T(8,128)(2,1)S(1)} collective-permute-done((bf16[128,2176]{1,0:T(8,128)(2,1)}, bf16[128,2176]{1,0:T(8,128)(2,1)S(1)}, u32[]{:S(2)}, u32[]{:S(2)}) %collective-permute-start.13) | collective-permute-done | bytes 557088 | tf_op jit(solution)/shard_map/ppermute | solution.py:189
  83.7 2.5 collect.6
  86.7 1.9 collective-permute-done.16.refs_5_
  88.6 10.2 %experts.2 = (bf16[2,288,2048]{2,1,0:T(8,128)(2,1)S(1)}, bf16[2,288,2048]{2,1,0:T(8,128)(2,1)S(1)}) custom-call(bf16[2,96,2048]{2,1,0:T(8,128)(2,1)S(1)} %get-tuple-element.60.refs_0_, bf16[2,96,2048]{2,1,0:T(8,128)(2,1)S(1)} %get-tuple-element.63.refs_1_, bf16[2,96,2048]{2,1,0:T(8,128)(2,1)S(1)} %get-tuple-element.68.refs_2_, ...), custom_call_target="tpu_custom_call" | custom-call | flops 14949999616 | bytes 13000000 | tf_op jit(solution)/shard_map/experts/pallas_call | solution.py:264
  99.6 3.8 %collective-permute-done.17.refs_6_.refs_10_ = bf16[2,288,2048]{2,1,0:T(8,128)(2,1)S(1)} collective-permute-done((bf16[2,288,2048]{2,1,0:T(8,128)(2,1)S(1)}, bf16[2,288,2048]{2,1,0:T(8,128)(2,1)S(1)}, u32[]{:S(2)}, u32[]{:S(2)}) %collective-permute-start.17) | collective-permute-done | bytes 2359328 | tf_op jit(solution)/shard_map/ppermute | solution.py:189
  103.4 3.6 %spread.4 = (bf16[2,2,128,2048]{3,2,1,0:T(8,128)(2,1)S(1)}, bf16[2,128,2048]{2,1,0:T(8,128)(2,1)S(1)}, bf16[2,128,2048]{2,1,0:T(8,128)(2,1)S(1)}) custom-call(bf16[128,2176]{1,0:T(8,128)(2,1)} %collective-permute-done.4.block_00.refs_0_, bf16[128,2176]{1,0:T(8,128)(2,1)} %collective-permute-done.9.block_10.refs_1_, ...), custom_call_target="tpu_custom_call" | custom-call | flops 6899999744 | bytes 6000000 | tf_op jit(solution)/shard_map/spread/pallas_call | solution.py:299
  112.0 6.4 %experts.3 = (bf16[2,96,2048]{2,1,0:T(8,128)(2,1)S(1)}, bf16[2,96,2048]{2,1,0:T(8,128)(2,1)S(1)}) custom-call(bf16[2,96,2048]{2,1,0:T(8,128)(2,1)S(1)} %get-tuple-element.80.refs_0_, bf16[2,96,2048]{2,1,0:T(8,128)(2,1)S(1)} %collective-permute-done.22.refs_1_, bf16[2,2048,512]{2,1,0:T(8,128)(2,1)S(1)} %copy-done.10, bf16[2,2048,512]{2,1,0:T(8,128)(2,1)S(1)} %copy-done.11, ...), custom_call_target="tpu_custom_call" | custom-call | flops 8049999872 | bytes 7000000 | tf_op jit(solution)/shard_map/experts/pallas_call | solution.py:264
  119.6 2.2 spread.3
  123.3 13.8 %collective-permute-done.20 = bf16[2,2,128,2048]{3,2,0,1:T(8,128)(2,1)} collective-permute-done((bf16[2,2,128,2048]{3,2,0,1:T(8,128)(2,1)}, bf16[2,2,128,2048]{3,2,0,1:T(8,128)(2,1)}, u32[]{:S(2)}, u32[]{:S(2)}) %collective-permute-start.20) | collective-permute-done | bytes 2097184 | tf_op jit(solution)/shard_map/ppermute | solution.py:189
  137.2 1.6 fusion
  140.4 21.6 %collective-permute-done.24 = bf16[2,128,2048]{2,1,0:T(8,128)(2,1)S(1)} collective-permute-done((bf16[2,128,2048]{2,1,0:T(8,128)(2,1)S(1)}, bf16[2,128,2048]{2,1,0:T(8,128)(2,1)S(1)}, u32[]{:S(2)}, u32[]{:S(2)}) %collective-permute-start.24) | collective-permute-done | bytes 1048608 | tf_op jit(solution)/shard_map/ppermute | solution.py:189
  162.0 1.8 fusion.1
  165.7 8.1 %collective-permute-done.25 = bf16[128,2048]{1,0:T(8,128)(2,1)S(1)} collective-permute-done((bf16[128,2048]{1,0:T(8,128)(2,1)S(1)}, bf16[128,2048]{1,0:T(8,128)(2,1)S(1)}, u32[]{:S(2)}, u32[]{:S(2)}) %collective-permute-start.25) | collective-permute-done | bytes 524320 | tf_op jit(solution)/shard_map/ppermute | solution.py:189
  173.9 2.2 collective-permute-start.26
  176.8 8.5 %collective-permute-done.26 = bf16[128,2048]{1,0:T(8,128)(2,1)S(1)} collective-permute-done((bf16[128,2048]{1,0:T(8,128)(2,1)S(1)}, bf16[128,2048]{1,0:T(8,128)(2,1)S(1)}, u32[]{:S(2)}, u32[]{:S(2)}) %collective-permute-start.26) | collective-permute-done | bytes 524320 | tf_op jit(solution)/shard_map/ppermute | solution.py:189
  188.8 7.4 %collective-permute-done.30 = bf16[128,2048]{1,0:T(8,128)(2,1)S(1)} collective-permute-done((bf16[128,2048]{1,0:T(8,128)(2,1)S(1)}, bf16[128,2048]{1,0:T(8,128)(2,1)S(1)}, u32[]{:S(2)}, u32[]{:S(2)}) %collective-permute-start.30) | collective-permute-done | bytes 524320 | tf_op jit(solution)/shard_map/ppermute | solution.py:189
  197.2 6.8 %collective-permute-start.32 = (bf16[128,2048]{1,0:T(8,128)(2,1)S(1)}, bf16[128,2048]{1,0:T(8,128)(2,1)}, u32[]{:S(2)}, u32[]{:S(2)}) collective-permute-start(bf16[128,2048]{1,0:T(8,128)(2,1)S(1)} %multiply_convert_fusion.refs_0_), channel_id=1, source_target_pairs={{0,1},{1,0},{2,3},{3,2},{4,5},{5,4},{6,7},{7,6},{8,9},{9,8},{10,11... | collective-permute-start | bytes 1572872 | tf_op jit(solution)/shard_map/ppermute | solution.py:709
  204.0 8.3 %collective-permute-start.33 = (bf16[128,2048]{1,0:T(8,128)(2,1)S(1)}, bf16[128,2048]{1,0:T(8,128)(2,1)}, u32[]{:S(2)}, u32[]{:S(2)}) collective-permute-start(bf16[128,2048]{1,0:T(8,128)(2,1)S(1)} %multiply_convert_fusion.refs_0_), channel_id=1, source_target_pairs={{0,2},{1,3},{2,0},{3,1},{4,6},{5,7},{6,4},{7,5},{8,10},{9,11},{10,... | collective-permute-start | bytes 1572872 | tf_op jit(solution)/shard_map/ppermute | solution.py:709
  212.3 2.1 collective-permute-start.31
  215.9 2.4 collective-permute-done.31.refs_2_
  219.7 1.6 copy-done.12
  221.3 1.6 copy-done.13
  225.4 3.4 %project.2 = (bf16[256,1024]{1,0:T(8,128)(2,1)S(1)}, bf16[256,512]{1,0:T(8,128)(2,1)S(1)}, f32[256,4]{1,0:T(8,128)S(1)}, f32[256,4]{1,0:T(8,128)S(1)}) custom-call(s32[1]{0:T(128)} %bitcast.12.place_ref, bf16[128,2048]{1,0:T(8,128)(2,1)S(1)} %multiply_convert_fusion.refs_0_, bf16[128,2048]{1,0:T(8,128)(2,1)} %collective-permute-done.32.refs_1_, ...), custom_call_target="tpu_custom_call" | custom-call | flops 4600000000 | bytes 4000000 | tf_op jit(solution)/shard_map/project/pallas_call | solution.py:746
  234.1 3.5 %project.3 = (bf16[256,1024]{1,0:T(8,128)(2,1)S(1)}, bf16[256,512]{1,0:T(8,128)(2,1)S(1)}, f32[256,4]{1,0:T(8,128)S(1)}, f32[256,4]{1,0:T(8,128)S(1)}, f32[16,1024]{1,0:T(8,128)S(1)}) custom-call(s32[1]{0:T(128)} %bitcast.12.place_ref, bf16[128,2048]{1,0:T(8,128)(2,1)} %collective-permute-done.33.refs_0_, ...), custom_call_target="tpu_custom_call" | custom-call | flops 4600000000 | bytes 4000000 | tf_op jit(solution)/shard_map/project/pallas_call | solution.py:746
  238.3 16.4 %delta.1 = (f32[512,512]{1,0:T(8,128)S(1)}, f32[512,512]{1,0:T(8,128)S(1)}, bf16[4,128,256]{2,1,0:T(8,128)(2,1)}) custom-call(s32[1]{0:T(128)} %bitcast.12.place_ref, bf16[256,1024]{1,0:T(8,128)(2,1)S(1)} %get-tuple-element.92.near_raw, bf16[256,1024]{1,0:T(8,128)(2,1)S(1)} %get-tuple-element.94.far_raw, f32[256,4]{1,0:T(8,128)S(1)} %get-tuple-element.95.near_beta, ...), custom_call_target="tpu_custom_call" | custom-call | flops 18400000000 | bytes 16000000 | tf_op jit(solution)/shard_map/delta/pallas_call | solution.py:764
  256.4 6.9 %collective-permute-done.38.other_ref = bf16[4,128,256]{2,1,0:T(8,128)(2,1)S(1)} collective-permute-done((bf16[4,128,256]{2,1,0:T(8,128)(2,1)}, bf16[4,128,256]{2,1,0:T(8,128)(2,1)S(1)}, u32[]{:S(2)}, u32[]{:S(2)}) %collective-permute-start.38) | collective-permute-done | bytes 262176 | tf_op jit(solution)/shard_map/ppermute | solution.py:794
  265.7 4.8 %collective-permute-done.40 = bf16[4,128,128]{2,1,0:T(8,128)(2,1)S(1)} collective-permute-done((bf16[4,128,128]{2,1,0:T(8,128)(2,1)S(1)}, bf16[4,128,128]{2,1,0:T(8,128)(2,1)S(1)}, u32[]{:S(2)}, u32[]{:S(2)}) %collective-permute-start.40) | collective-permute-done | bytes 131104 | tf_op jit(solution)/shard_map/ppermute | solution.py:24
  272.0 4.8 %collective-permute-done.41 = bf16[4,128,128]{2,1,0:T(8,128)(2,1)S(1)} collective-permute-done((bf16[4,128,128]{2,1,0:T(8,128)(2,1)S(1)}, bf16[4,128,128]{2,1,0:T(8,128)(2,1)S(1)}, u32[]{:S(2)}, u32[]{:S(2)}) %collective-permute-start.41) | collective-permute-done | bytes 131104 | tf_op jit(solution)/shard_map/ppermute | solution.py:24
  277.0 2.9 collective-permute-done.42.refs_3_
  281.2 4.4 %collective-permute-done.43.state_ref = bf16[4,128,128]{2,1,0:T(8,128)(2,1)S(1)} collective-permute-done((bf16[4,128,128]{2,1,0:T(8,128)(2,1)S(1)}, bf16[4,128,128]{2,1,0:T(8,128)(2,1)S(1)}, u32[]{:S(2)}, u32[]{:S(2)}) %collective-permute-start.43) | collective-permute-done | bytes 131104 | tf_op jit(solution)/shard_map/ppermute | solution.py:24
  285.6 2.2 collective-permute-start.46
  289.0 2.6 finish.1
  294.9 3.2 %output.2.refs_6_ = f32[128,2048]{1,0:T(8,128)S(1)} custom-call(bf16[128,512]{1,0:T(8,128)(2,1)S(1)} %get-tuple-element.117.refs_0_, bf16[128,512]{1,0:T(8,128)(2,1)S(1)} %collective-permute-done.48.refs_1_, bf16[512,2048]{1,0:T(8,128)(2,1)S(1)} %copy-done.2, bf16[512,2048]{1,0:T(8,128)(2,1)} %collective-permute-done.49.refs_3_), custom_call_target="tpu_custom_call" | custom-call | flops 3449999872 | bytes 3000000 | tf_op jit(solution)/shard_map/output/pallas_call | solution.py:850
  298.2 2.1 collective-permute-done.45.refs_1_
  300.3 4.2 %output.3 = bf16[128,2048]{1,0:T(8,128)(2,1)} custom-call(bf16[128,512]{1,0:T(8,128)(2,1)S(1)} %collective-permute-done.44.refs_0_, bf16[128,512]{1,0:T(8,128)(2,1)S(1)} %collective-permute-done.45.refs_1_, bf16[320,2048]{1,0:T(8,128)(2,1)} %collective-permute-done.39.refs_2_, bf16[192,2048]{1,0:T(8,128)(2,1)} %collective-permute-done.42.refs_3_, ...), custom_call_target="tpu_custom_call" | custom-call | flops 3449999872 | bytes 3000000 | tf_op jit(solution)/shard_map/output/pallas_call | solution.py:850
  (169 shorter events, 56.1 us)
Async XLA Ops:
  4.8 12.0 %collective-permute-start = (bf16[128,2176]{1,0:T(8,128)(2,1)S(1)}, bf16[128,2176]{1,0:T(8,128)(2,1)S(1)}, u32[]{:S(2)}, u32[]{:S(2)}) collective-permute-start(bf16[128,2176]{1,0:T(8,128)(2,1)S(1)} %concatenate.9.block_00.refs_0_), channel_id=1, source_target_pairs={{0,4},{1,3},{2,6},{3,1},{4,0},{5,7},{6,2},{7,5},{8,12},{9,11},{10,... | collective-permute-start | bytes 1671176 | tf_op jit(solution)/shard_map/ppermute | solution.py:189
  6.1 14.6 %collective-permute-start.1 = (bf16[128,2176]{1,0:T(8,128)(2,1)S(1)}, bf16[128,2176]{1,0:T(8,128)(2,1)S(1)}, u32[]{:S(2)}, u32[]{:S(2)}) collective-permute-start(bf16[128,2176]{1,0:T(8,128)(2,1)S(1)} %concatenate.9.block_00.refs_0_), channel_id=1, source_target_pairs={{0,2},{1,5},{2,0},{3,7},{4,6},{5,1},{6,4},{7,3},{8,10},{9,13},{10,... | collective-permute-start | bytes 1671176 | tf_op jit(solution)/shard_map/ppermute | solution.py:189
  7.3 14.7 %collective-permute-start.3 = (bf16[128,2176]{1,0:T(8,128)(2,1)S(1)}, bf16[128,2176]{1,0:T(8,128)(2,1)S(1)}, u32[]{:S(2)}, u32[]{:S(2)}) collective-permute-start(bf16[128,2176]{1,0:T(8,128)(2,1)S(1)} %concatenate.9.block_00.refs_0_), channel_id=1, source_target_pairs={{0,24},{1,25},{2,26},{3,27},{4,28},{5,29},{6,30},{7,31},{8,0},{9,1... | collective-permute-start | bytes 1671176 | tf_op jit(solution)/shard_map/ppermute | solution.py:189
  22.0 11.5 %collective-permute-start.5 = (bf16[128,2176]{1,0:T(8,128)(2,1)S(1)}, bf16[128,2176]{1,0:T(8,128)(2,1)}, u32[]{:S(2)}, u32[]{:S(2)}) collective-permute-start(bf16[128,2176]{1,0:T(8,128)(2,1)S(1)} %collective-permute-done.3.block_00.refs_4_), channel_id=1, source_target_pairs={{0,4},{1,3},{2,6},{3,1},{4,0},{5,7},{6,2},{7,5},{8,12},{9,11},{10,... | collective-permute-start | bytes 1671176 | tf_op jit(solution)/shard_map/ppermute | solution.py:189
  22.2 13.6 %collective-permute-start.4 = (bf16[128,2176]{1,0:T(8,128)(2,1)S(1)}, bf16[128,2176]{1,0:T(8,128)(2,1)}, u32[]{:S(2)}, u32[]{:S(2)}) collective-permute-start(bf16[128,2176]{1,0:T(8,128)(2,1)S(1)} %collective-permute-done.3.block_00.refs_4_), channel_id=1, source_target_pairs={{0,24},{1,25},{2,26},{3,27},{4,28},{5,29},{6,30},{7,31},{8,0},{9,1... | collective-permute-start | bytes 1671176 | tf_op jit(solution)/shard_map/ppermute | solution.py:189
  22.3 13.6 %collective-permute-start.6 = (bf16[128,2176]{1,0:T(8,128)(2,1)S(1)}, bf16[128,2176]{1,0:T(8,128)(2,1)S(1)}, u32[]{:S(2)}, u32[]{:S(2)}) collective-permute-start(bf16[128,2176]{1,0:T(8,128)(2,1)S(1)} %collective-permute-done.3.block_00.refs_4_), channel_id=1, source_target_pairs={{0,2},{1,5},{2,0},{3,7},{4,6},{5,1},{6,4},{7,3},{8,10},{9,13},{10,... | collective-permute-start | bytes 1671176 | tf_op jit(solution)/shard_map/ppermute | solution.py:189
  36.7 13.5 %collective-permute-start.8 = (bf16[128,2176]{1,0:T(8,128)(2,1)S(1)}, bf16[128,2176]{1,0:T(8,128)(2,1)S(1)}, u32[]{:S(2)}, u32[]{:S(2)}) collective-permute-start(bf16[128,2176]{1,0:T(8,128)(2,1)S(1)} %concatenate.9.block_00.refs_0_), channel_id=1, source_target_pairs={{0,8},{1,9},{2,10},{3,11},{4,12},{5,13},{6,14},{7,15},{8,16},{9,17... | collective-permute-start | bytes 1671176 | tf_op jit(solution)/shard_map/ppermute | solution.py:189
  39.0 12.9 %collective-permute-start.9 = (bf16[128,2176]{1,0:T(8,128)(2,1)}, bf16[128,2176]{1,0:T(8,128)(2,1)}, u32[]{:S(2)}, u32[]{:S(2)}) collective-permute-start(bf16[128,2176]{1,0:T(8,128)(2,1)} %collective-permute-done.4.block_00.refs_0_), channel_id=1, source_target_pairs={{0,4},{1,3},{2,6},{3,1},{4,0},{5,7},{6,2},{7,5},{8,12},{9,11},{10,... | collective-permute-start | bytes 1671176 | tf_op jit(solution)/shard_map/ppermute | solution.py:189
  39.3 13.6 %collective-permute-start.10 = (bf16[128,2176]{1,0:T(8,128)(2,1)}, bf16[128,2176]{1,0:T(8,128)(2,1)}, u32[]{:S(2)}, u32[]{:S(2)}) collective-permute-start(bf16[128,2176]{1,0:T(8,128)(2,1)} %collective-permute-done.4.block_00.refs_0_), channel_id=1, source_target_pairs={{0,2},{1,5},{2,0},{3,7},{4,6},{5,1},{6,4},{7,3},{8,10},{9,13},{10,... | collective-permute-start | bytes 1671176 | tf_op jit(solution)/shard_map/ppermute | solution.py:189
  39.6 21.5 %collective-permute-start.2 = (bf16[128,2176]{1,0:T(8,128)(2,1)S(1)}, bf16[128,2176]{1,0:T(8,128)(2,1)}, u32[]{:S(2)}, u32[]{:S(2)}) collective-permute-start(bf16[128,2176]{1,0:T(8,128)(2,1)S(1)} %collective-permute-done.block_10.refs_1_), channel_id=1, source_target_pairs={{0,2},{1,5},{2,0},{3,7},{4,6},{5,1},{6,4},{7,3},{8,10},{9,13},{10,... | collective-permute-start | bytes 1671176 | tf_op jit(solution)/shard_map/ppermute | solution.py:189
  40.8 31.3 %collective-permute-start.7 = (bf16[128,2176]{1,0:T(8,128)(2,1)}, bf16[128,2176]{1,0:T(8,128)(2,1)}, u32[]{:S(2)}, u32[]{:S(2)}) collective-permute-start(bf16[128,2176]{1,0:T(8,128)(2,1)} %collective-permute-done.5.block_10.refs_5_), channel_id=1, source_target_pairs={{0,2},{1,5},{2,0},{3,7},{4,6},{5,1},{6,4},{7,3},{8,10},{9,13},{10,... | collective-permute-start | bytes 1671176 | tf_op jit(solution)/shard_map/ppermute | solution.py:189
  52.9 21.8 %collective-permute-start.11 = (bf16[128,2176]{1,0:T(8,128)(2,1)S(1)}, bf16[128,2176]{1,0:T(8,128)(2,1)S(1)}, u32[]{:S(2)}, u32[]{:S(2)}) collective-permute-start(bf16[128,2176]{1,0:T(8,128)(2,1)S(1)} %collective-permute-done.8.block_00.refs_0_), channel_id=1, source_target_pairs={{0,4},{1,3},{2,6},{3,1},{4,0},{5,7},{6,2},{7,5},{8,12},{9,11},{10,... | collective-permute-start | bytes 1671176 | tf_op jit(solution)/shard_map/ppermute | solution.py:189
  54.3 23.8 %collective-permute-start.12 = (bf16[128,2176]{1,0:T(8,128)(2,1)S(1)}, bf16[128,2176]{1,0:T(8,128)(2,1)S(1)}, u32[]{:S(2)}, u32[]{:S(2)}) collective-permute-start(bf16[128,2176]{1,0:T(8,128)(2,1)S(1)} %collective-permute-done.8.block_00.refs_0_), channel_id=1, source_target_pairs={{0,2},{1,5},{2,0},{3,7},{4,6},{5,1},{6,4},{7,3},{8,10},{9,13},{10,... | collective-permute-start | bytes 1671176 | tf_op jit(solution)/shard_map/ppermute | solution.py:189
  54.7 29.0 %collective-permute-start.13 = (bf16[128,2176]{1,0:T(8,128)(2,1)}, bf16[128,2176]{1,0:T(8,128)(2,1)S(1)}, u32[]{:S(2)}, u32[]{:S(2)}) collective-permute-start(bf16[128,2176]{1,0:T(8,128)(2,1)} %collective-permute-done.9.block_10.refs_1_), channel_id=1, source_target_pairs={{0,2},{1,5},{2,0},{3,7},{4,6},{5,1},{6,4},{7,3},{8,10},{9,13},{10,... | collective-permute-start | bytes 1671176 | tf_op jit(solution)/shard_map/ppermute | solution.py:189
  63.3 23.4 %collective-permute-start.14 = (bf16[2,96,2048]{2,1,0:T(8,128)(2,1)S(1)}, bf16[2,96,2048]{2,1,0:T(8,128)(2,1)S(1)}, u32[]{:S(2)}, u32[]{:S(2)}) collective-permute-start(bf16[2,96,2048]{2,1,0:T(8,128)(2,1)S(1)} %get-tuple-element.69), channel_id=1, source_target_pairs={{0,1},{1,0},{2,3},{3,2},{4,5},{5,4},{6,7},{7,6},{8,9},{9,8},{10,11... | collective-permute-start | bytes 2359304 | tf_op jit(solution)/shard_map/ppermute | solution.py:189
  74.4 12.3 %collective-permute-start.15 = (bf16[2,96,2048]{2,1,0:T(8,128)(2,1)S(1)}, bf16[2,96,2048]{2,1,0:T(8,128)(2,1)S(1)}, u32[]{:S(2)}, u32[]{:S(2)}) collective-permute-start(bf16[2,96,2048]{2,1,0:T(8,128)(2,1)S(1)} %get-tuple-element.70), channel_id=1, source_target_pairs={{0,1},{1,0},{2,3},{3,2},{4,5},{5,4},{6,7},{7,6},{8,9},{9,8},{10,11... | collective-permute-start | bytes 2359304 | tf_op jit(solution)/shard_map/ppermute | solution.py:189
  98.8 4.6 %collective-permute-start.17 = (bf16[2,288,2048]{2,1,0:T(8,128)(2,1)S(1)}, bf16[2,288,2048]{2,1,0:T(8,128)(2,1)S(1)}, u32[]{:S(2)}, u32[]{:S(2)}) collective-permute-start(bf16[2,288,2048]{2,1,0:T(8,128)(2,1)S(1)} %get-tuple-element.73), channel_id=1, source_target_pairs={{0,1},{1,0},{2,3},{3,2},{4,5},{5,4},{6,7},{7,6},{8,9},{9,8},{10,11... | collective-permute-start | bytes 7077896 | tf_op jit(solution)/shard_map/ppermute | solution.py:189
  99.3 8.7 %collective-permute-start.21 = (bf16[128,2176]{1,0:T(8,128)(2,1)S(1)}, bf16[128,2176]{1,0:T(8,128)(2,1)S(1)}, u32[]{:S(2)}, u32[]{:S(2)}) collective-permute-start(bf16[128,2176]{1,0:T(8,128)(2,1)S(1)} %collective-permute-done.11.block_10.refs_1_), channel_id=1, source_target_pairs={{0,2},{1,5},{2,0},{3,7},{4,6},{5,1},{6,4},{7,3},{8,10},{9,13},{10,... | collective-permute-start | bytes 1671176 | tf_op jit(solution)/shard_map/ppermute | solution.py:189
  109.1 3.0 collective-permute-start.22
  111.7 25.5 %collective-permute-start.20 = (bf16[2,2,128,2048]{3,2,0,1:T(8,128)(2,1)}, bf16[2,2,128,2048]{3,2,0,1:T(8,128)(2,1)}, u32[]{:S(2)}, u32[]{:S(2)}) collective-permute-start(bf16[2,2,128,2048]{3,2,0,1:T(8,128)(2,1)} %copy.32), channel_id=1, source_target_pairs={{0,2},{1,5},{2,0},{3,7},{4,6},{5,1},{6,4},{7,3},{8,10},{9,13},{10,... | collective-permute-start | bytes 6291464 | tf_op jit(solution)/shard_map/ppermute | solution.py:189
  118.4 3.4 %collective-permute-start.23 = (bf16[2,96,2048]{2,1,0:T(8,128)(2,1)S(1)}, bf16[2,96,2048]{2,1,0:T(8,128)(2,1)S(1)}, u32[]{:S(2)}, u32[]{:S(2)}) collective-permute-start(bf16[2,96,2048]{2,1,0:T(8,128)(2,1)S(1)} %get-tuple-element.83), channel_id=1, source_target_pairs={{0,1},{1,0},{2,3},{3,2},{4,5},{5,4},{6,7},{7,6},{8,9},{9,8},{10,11... | collective-permute-start | bytes 2359304 | tf_op jit(solution)/shard_map/ppermute | solution.py:189
  138.8 23.2 %collective-permute-start.24 = (bf16[2,128,2048]{2,1,0:T(8,128)(2,1)S(1)}, bf16[2,128,2048]{2,1,0:T(8,128)(2,1)S(1)}, u32[]{:S(2)}, u32[]{:S(2)}) collective-permute-start(bf16[2,128,2048]{2,1,0:T(8,128)(2,1)S(1)} %fusion), channel_id=1, source_target_pairs={{0,4},{1,3},{2,6},{3,1},{4,0},{5,7},{6,2},{7,5},{8,12},{9,11},{10,... | collective-permute-start | bytes 3145736 | tf_op jit(solution)/shard_map/ppermute | solution.py:189
  140.0 25.0 %collective-permute-start.28 = (bf16[1,2,128,2048]{3,2,1,0:T(8,128)(2,1)S(1)}, bf16[1,2,128,2048]{3,2,1,0:T(8,128)(2,1)S(1)}, u32[]{:S(2)}, u32[]{:S(2)}) collective-permute-start(bf16[1,2,128,2048]{3,2,1,0:T(8,128)(2,1)S(1)} %get-tuple-element.84), channel_id=1, source_target_pairs={{0,2},{1,5},{2,0},{3,7},{4,6},{5,1},{6,4},{7,3},{8,10},{9,13},{10,... | collective-permute-start | bytes 3145736 | tf_op jit(solution)/shard_map/ppermute | solution.py:189
  163.8 9.9 %collective-permute-start.25 = (bf16[128,2048]{1,0:T(8,128)(2,1)S(1)}, bf16[128,2048]{1,0:T(8,128)(2,1)S(1)}, u32[]{:S(2)}, u32[]{:S(2)}) collective-permute-start(bf16[128,2048]{1,0:T(8,128)(2,1)S(1)} %fusion.17), channel_id=1, source_target_pairs={{0,8},{1,9},{2,10},{3,11},{4,12},{5,13},{6,14},{7,15},{8,16},{9,17... | collective-permute-start | bytes 1572872 | tf_op jit(solution)/shard_map/ppermute | solution.py:189
  165.2 10.9 %collective-permute-start.29 = (bf16[1,128,2048]{2,1,0:T(8,128)(2,1)S(1)}, bf16[1,128,2048]{2,1,0:T(8,128)(2,1)S(1)}, u32[]{:S(2)}, u32[]{:S(2)}) collective-permute-start(bf16[1,128,2048]{2,1,0:T(8,128)(2,1)S(1)} %fusion.10), channel_id=1, source_target_pairs={{0,4},{1,3},{2,6},{3,1},{4,0},{5,7},{6,2},{7,5},{8,12},{9,11},{10,... | collective-permute-start | bytes 1572872 | tf_op jit(solution)/shard_map/ppermute | solution.py:189
  165.4 11.4 %collective-permute-start.19 = (bf16[128,2048]{1,0:T(8,128)(2,1)S(1)}, bf16[128,2048]{1,0:T(8,128)(2,1)S(1)}, u32[]{:S(2)}, u32[]{:S(2)}) collective-permute-start(bf16[128,2048]{1,0:T(8,128)(2,1)S(1)} %get-tuple-element.115), channel_id=1, source_target_pairs={{0,2},{1,5},{2,0},{3,7},{4,6},{5,1},{6,4},{7,3},{8,10},{9,13},{10,... | collective-permute-start | bytes 1572872 | tf_op jit(solution)/shard_map/ppermute | solution.py:189
  173.9 11.4 %collective-permute-start.26 = (bf16[128,2048]{1,0:T(8,128)(2,1)S(1)}, bf16[128,2048]{1,0:T(8,128)(2,1)S(1)}, u32[]{:S(2)}, u32[]{:S(2)}) collective-permute-start(bf16[128,2048]{1,0:T(8,128)(2,1)S(1)} %fusion.9), channel_id=1, source_target_pairs={{0,8},{1,9},{2,10},{3,11},{4,12},{5,13},{6,14},{7,15},{8,16},{9,17... | collective-permute-start | bytes 1572872 | tf_op jit(solution)/shard_map/ppermute | solution.py:189
  176.1 12.8 %collective-permute-start.18 = (bf16[128,2048]{1,0:T(8,128)(2,1)S(1)}, bf16[128,2048]{1,0:T(8,128)(2,1)S(1)}, u32[]{:S(2)}, u32[]{:S(2)}) collective-permute-start(bf16[128,2048]{1,0:T(8,128)(2,1)S(1)} %get-tuple-element.114), channel_id=1, source_target_pairs={{0,2},{1,5},{2,0},{3,7},{4,6},{5,1},{6,4},{7,3},{8,10},{9,13},{10,... | collective-permute-start | bytes 1572872 | tf_op jit(solution)/shard_map/ppermute | solution.py:189
  176.3 19.9 %collective-permute-start.30 = (bf16[128,2048]{1,0:T(8,128)(2,1)S(1)}, bf16[128,2048]{1,0:T(8,128)(2,1)S(1)}, u32[]{:S(2)}, u32[]{:S(2)}) collective-permute-start(bf16[128,2048]{1,0:T(8,128)(2,1)S(1)} %fusion.16), channel_id=1, source_target_pairs={{0,24},{1,25},{2,26},{3,27},{4,28},{5,29},{6,30},{7,31},{8,0},{9,1... | collective-permute-start | bytes 1572872 | tf_op jit(solution)/shard_map/ppermute | solution.py:189
  185.4 10.8 %collective-permute-start.27 = (bf16[128,2048]{1,0:T(8,128)(2,1)S(1)}, bf16[128,2048]{1,0:T(8,128)(2,1)S(1)}, u32[]{:S(2)}, u32[]{:S(2)}) collective-permute-start(bf16[128,2048]{1,0:T(8,128)(2,1)S(1)} %fusion.13), channel_id=1, source_target_pairs={{0,4},{1,3},{2,6},{3,1},{4,0},{5,7},{6,2},{7,5},{8,12},{9,11},{10,... | collective-permute-start | bytes 1572872 | tf_op jit(solution)/shard_map/ppermute | solution.py:189
  197.2 21.5 %collective-permute-start.32 = (bf16[128,2048]{1,0:T(8,128)(2,1)S(1)}, bf16[128,2048]{1,0:T(8,128)(2,1)}, u32[]{:S(2)}, u32[]{:S(2)}) collective-permute-start(bf16[128,2048]{1,0:T(8,128)(2,1)S(1)} %multiply_convert_fusion.refs_0_), channel_id=1, source_target_pairs={{0,1},{1,0},{2,3},{3,2},{4,5},{5,4},{6,7},{7,6},{8,9},{9,8},{10,11... | collective-permute-start | bytes 1572872 | tf_op jit(solution)/shard_map/ppermute | solution.py:709
  204.0 25.5 %collective-permute-start.33 = (bf16[128,2048]{1,0:T(8,128)(2,1)S(1)}, bf16[128,2048]{1,0:T(8,128)(2,1)}, u32[]{:S(2)}, u32[]{:S(2)}) collective-permute-start(bf16[128,2048]{1,0:T(8,128)(2,1)S(1)} %multiply_convert_fusion.refs_0_), channel_id=1, source_target_pairs={{0,2},{1,3},{2,0},{3,1},{4,6},{5,7},{6,4},{7,5},{8,10},{9,11},{10,... | collective-permute-start | bytes 1572872 | tf_op jit(solution)/shard_map/ppermute | solution.py:709
  212.3 5.9 %collective-permute-start.31 = (bf16[16,2048]{1,0:T(8,128)(2,1)S(1)}, bf16[16,2048]{1,0:T(8,128)(2,1)S(1)}, u32[]{:S(2)}, u32[]{:S(2)}) collective-permute-start(bf16[16,2048]{1,0:T(8,128)(2,1)S(1)} %slice.65), channel_id=1, source_target_pairs={{0,4},{4,8},{8,12},{12,16},{16,20},{20,24},{24,28},{1,5},{5,9},{9,... | collective-permute-start | bytes 196616 | tf_op jit(solution)/shard_map/ppermute | solution.py:24
  218.2 11.3 %collective-permute-start.34 = (bf16[16,2048]{1,0:T(8,128)(2,1)S(1)}, bf16[16,2048]{1,0:T(8,128)(2,1)S(1)}, u32[]{:S(2)}, u32[]{:S(2)}) collective-permute-start(bf16[16,2048]{1,0:T(8,128)(2,1)S(1)} %collective-permute-done.31.refs_2_), channel_id=1, source_target_pairs={{0,2},{1,3},{2,0},{3,1},{4,6},{5,7},{6,4},{7,5},{8,10},{9,11},{10,... | collective-permute-start | bytes 196616 | tf_op jit(solution)/shard_map/ppermute | solution.py:709
  229.5 3.0 collective-permute-start.35
  230.8 3.3 %collective-permute-start.36 = (bf16[16,2048]{1,0:T(8,128)(2,1)S(1)}, bf16[16,2048]{1,0:T(8,128)(2,1)S(1)}, u32[]{:S(2)}, u32[]{:S(2)}) collective-permute-start(bf16[16,2048]{1,0:T(8,128)(2,1)S(1)} %collective-permute-done.31.refs_2_), channel_id=1, source_target_pairs={{0,1},{1,0},{2,3},{3,2},{4,5},{5,4},{6,7},{7,6},{8,9},{9,8},{10,11... | collective-permute-start | bytes 196616 | tf_op jit(solution)/shard_map/ppermute | solution.py:709
  230.9 3.2 %collective-permute-start.37 = (bf16[16,2048]{1,0:T(8,128)(2,1)S(1)}, bf16[16,2048]{1,0:T(8,128)(2,1)S(1)}, u32[]{:S(2)}, u32[]{:S(2)}) collective-permute-start(bf16[16,2048]{1,0:T(8,128)(2,1)S(1)} %collective-permute-done.34.refs_4_), channel_id=1, source_target_pairs={{0,1},{1,0},{2,3},{3,2},{4,5},{5,4},{6,7},{7,6},{8,9},{9,8},{10,11... | collective-permute-start | bytes 196616 | tf_op jit(solution)/shard_map/ppermute | solution.py:709
  232.5 30.7 %collective-permute-start.39 = (bf16[320,2048]{1,0:T(8,128)(2,1)}, bf16[320,2048]{1,0:T(8,128)(2,1)}, u32[]{:S(2)}, u32[]{:S(2)}) collective-permute-start(bf16[320,2048]{1,0:T(8,128)(2,1)} %slice.54), channel_id=1, source_target_pairs={{0,2},{1,3},{2,0},{3,1},{4,6},{5,7},{6,4},{7,5},{8,10},{9,11},{10,... | collective-permute-start | bytes 3932168 | tf_op jit(solution)/shard_map/ppermute | solution.py:709
  255.7 7.5 %collective-permute-start.38 = (bf16[4,128,256]{2,1,0:T(8,128)(2,1)}, bf16[4,128,256]{2,1,0:T(8,128)(2,1)S(1)}, u32[]{:S(2)}, u32[]{:S(2)}) collective-permute-start(bf16[4,128,256]{2,1,0:T(8,128)(2,1)} %get-tuple-element.100.mine_ref), channel_id=1, source_target_pairs={{0,4},{4,0},{8,12},{12,8},{16,20},{20,16},{24,28},{28,24},{1,5},{5... | collective-permute-start | bytes 786440 | tf_op jit(solution)/shard_map/ppermute | solution.py:794
  255.7 39.2 %collective-permute-start.49 = (bf16[512,2048]{1,0:T(8,128)(2,1)S(1)}, bf16[512,2048]{1,0:T(8,128)(2,1)}, u32[]{:S(2)}, u32[]{:S(2)}) collective-permute-start(bf16[512,2048]{1,0:T(8,128)(2,1)S(1)} %copy-done.2), channel_id=1, source_target_pairs={{0,1},{1,0},{2,3},{3,2},{4,5},{5,4},{6,7},{7,6},{8,9},{9,8},{10,11... | collective-permute-start | bytes 6291464 | tf_op jit(solution)/shard_map/ppermute | solution.py:709
  256.3 23.6 %collective-permute-start.42 = (bf16[192,2048]{1,0:T(8,128)(2,1)}, bf16[192,2048]{1,0:T(8,128)(2,1)}, u32[]{:S(2)}, u32[]{:S(2)}) collective-permute-start(bf16[192,2048]{1,0:T(8,128)(2,1)} %slice.55), channel_id=1, source_target_pairs={{0,2},{1,3},{2,0},{3,1},{4,6},{5,7},{6,4},{7,5},{8,10},{9,11},{10,... | collective-permute-start | bytes 2359304 | tf_op jit(solution)/shard_map/ppermute | solution.py:709
  264.4 6.1 %collective-permute-start.40 = (bf16[4,128,128]{2,1,0:T(8,128)(2,1)S(1)}, bf16[4,128,128]{2,1,0:T(8,128)(2,1)S(1)}, u32[]{:S(2)}, u32[]{:S(2)}) collective-permute-start(bf16[4,128,128]{2,1,0:T(8,128)(2,1)S(1)} %get-tuple-element.104), channel_id=1, source_target_pairs={{0,8},{4,12},{8,16},{12,20},{16,24},{20,28},{1,9},{5,13},{9,17},{1... | collective-permute-start | bytes 393224 | tf_op jit(solution)/shard_map/ppermute | solution.py:24
  270.7 6.1 %collective-permute-start.41 = (bf16[4,128,128]{2,1,0:T(8,128)(2,1)S(1)}, bf16[4,128,128]{2,1,0:T(8,128)(2,1)S(1)}, u32[]{:S(2)}, u32[]{:S(2)}) collective-permute-start(bf16[4,128,128]{2,1,0:T(8,128)(2,1)S(1)} %fusion.2), channel_id=1, source_target_pairs={{0,8},{4,12},{8,16},{12,20},{16,24},{20,28},{1,9},{5,13},{9,17},{1... | collective-permute-start | bytes 393224 | tf_op jit(solution)/shard_map/ppermute | solution.py:24
  279.9 5.7 %collective-permute-start.43 = (bf16[4,128,128]{2,1,0:T(8,128)(2,1)S(1)}, bf16[4,128,128]{2,1,0:T(8,128)(2,1)S(1)}, u32[]{:S(2)}, u32[]{:S(2)}) collective-permute-start(bf16[4,128,128]{2,1,0:T(8,128)(2,1)S(1)} %fusion.3), channel_id=1, source_target_pairs={{0,8},{4,12},{8,16},{12,20},{16,24},{20,28},{1,9},{5,13},{9,17},{1... | collective-permute-start | bytes 393224 | tf_op jit(solution)/shard_map/ppermute | solution.py:24
  285.6 14.7 %collective-permute-start.46 = (bf16[320,2048]{1,0:T(8,128)(2,1)}, bf16[320,2048]{1,0:T(8,128)(2,1)S(1)}, u32[]{:S(2)}, u32[]{:S(2)}) collective-permute-start(bf16[320,2048]{1,0:T(8,128)(2,1)} %collective-permute-done.39.refs_2_), channel_id=1, source_target_pairs={{0,1},{1,0},{2,3},{3,2},{4,5},{5,4},{6,7},{7,6},{8,9},{9,8},{10,11... | collective-permute-start | bytes 3932168 | tf_op jit(solution)/shard_map/ppermute | solution.py:709
  287.9 12.3 %collective-permute-start.47 = (bf16[192,2048]{1,0:T(8,128)(2,1)}, bf16[192,2048]{1,0:T(8,128)(2,1)S(1)}, u32[]{:S(2)}, u32[]{:S(2)}) collective-permute-start(bf16[192,2048]{1,0:T(8,128)(2,1)} %collective-permute-done.42.refs_3_), channel_id=1, source_target_pairs={{0,1},{1,0},{2,3},{3,2},{4,5},{5,4},{6,7},{7,6},{8,9},{9,8},{10,11... | collective-permute-start | bytes 2359304 | tf_op jit(solution)/shard_map/ppermute | solution.py:709
  292.2 6.0 %collective-permute-start.44 = (bf16[128,512]{1,0:T(8,128)(2,1)S(1)}, bf16[128,512]{1,0:T(8,128)(2,1)S(1)}, u32[]{:S(2)}, u32[]{:S(2)}) collective-permute-start(bf16[128,512]{1,0:T(8,128)(2,1)S(1)} %get-tuple-element.119), channel_id=1, source_target_pairs={{0,2},{1,3},{2,0},{3,1},{4,6},{5,7},{6,4},{7,5},{8,10},{9,11},{10,... | collective-permute-start | bytes 393224 | tf_op jit(solution)/shard_map/ppermute | solution.py:709
  293.7 6.6 %collective-permute-start.45 = (bf16[128,512]{1,0:T(8,128)(2,1)S(1)}, bf16[128,512]{1,0:T(8,128)(2,1)S(1)}, u32[]{:S(2)}, u32[]{:S(2)}) collective-permute-start(bf16[128,512]{1,0:T(8,128)(2,1)S(1)} %get-tuple-element.118), channel_id=1, source_target_pairs={{0,3},{1,2},{2,1},{3,0},{4,7},{5,6},{6,5},{7,4},{8,11},{9,10},{10,... | collective-permute-start | bytes 393224 | tf_op jit(solution)/shard_map/ppermute | solution.py:709
  (34 other events, 281.8 us)

commit v3 on v2

--- a/solution.py
+++ b/solution.py
@@ -274,7 +274,7 @@
             out_shape=[jax.ShapeDtypeStruct((local_experts, len(members) * taken, width), bf16)]
             * 2,
             compiler_params=pltpu.CompilerParams(vmem_limit_bytes=40 << 20),
-            cost_estimate=worth(4 + 3 * len(members)),
+            cost_estimate=worth(4 + 3 * len(members) if len(members) > 1 else 1),
             name="experts",
         )(
             after(own_rows[members[0]], *earlier),
@@ -304,7 +304,7 @@
             out_specs=[whole_ref(far_shape), whole_ref(row_shape), whole_ref(row_shape)],
             out_shape=[far_shape, row_shape, row_shape],
             compiler_params=pltpu.CompilerParams(vmem_limit_bytes=28 << 20),
-            cost_estimate=worth(3 * len(members)),
+            cost_estimate=worth(1),
             name="spread",
         )(*(block for member in members for block in blocks[member]), picker, results, got_back)
 
@@ -313,27 +313,30 @@
         collect(steps, blocks[order[-2]][0])
     collect(order[-2], *blocks[last][:3])
     run_experts(order[:-1])
-    far, near, here = spread(batch)
-    collect(last, far)
+    ready = {steps: spread([steps]) for steps in batch}
+    collect(last, *[far for far, _, _ in ready.values()])
     run_experts([last])
-    far_last, near_last, here_last = spread([last])
-    far_own, near_own, here_own = spread([0])
-
-    def joined(near, here, direct, diagonal):
-        near = first((near.astype(f32) + diagonal.astype(f32)).astype(bf16))
-        return here.astype(f32) + direct.astype(f32) + near.astype(f32)
-
-    across = after(second(far), far_last, far_own)
-    sums = joined(near, here, across[:, 0], across[:, 1])
-    moving = lifted(sums[0].astype(bf16), 1)
-    for at in range(1, len(batch)):
-        moving = lifted((sums[at] + moving.astype(f32)).astype(bf16), 1)
-    across = second(far_last)
-    sums = joined(near_last, here_last, across[:, 0], across[:, 1])
-    rising = lifted(sums[0].astype(bf16), -1)
-    diagonal = after(second(far_own[0, 1]), moving)
-    total = joined(near_own[0], here_own[0], second(far_own[0, 0]), diagonal)
-    total += moving.astype(f32) + rising.astype(f32)
+    ready[last], ready[0] = spread([last]), spread([0])
+
+    def joined(steps, direct, diagonal):
+        _, near, here = ready[steps]
+        near = first((near[0].astype(f32) + diagonal.astype(f32)).astype(bf16))
+        return here[0].astype(f32) + direct.astype(f32) + near.astype(f32)
+
+    moving = []
+    for at, steps in enumerate(batch):
+        across = second(ready[steps][0])
+        total = joined(steps, across[0, 0], across[0, 1])
+        if moving:
+            total += moving[-1].astype(f32)
+        moving.append(lifted(total.astype(bf16), 1))
+    across = after(second(ready[last][0]), moving[0])
+    total = joined(last, across[0, 0], across[0, 1])
+    rising = lifted(total.astype(bf16), -1)
+    far = ready[0][0]
+    diagonal = after(second(far[0, 1]), moving[-1])
+    total = joined(0, second(far[0, 0]), diagonal)
+    total += moving[-1].astype(f32) + rising.astype(f32)
     return after(total, *early).astype(bf16)
 
 
@@ -618,27 +621,37 @@
     decay_ref[...] = contract(pieces, weight_refs[5][...], ((1,), (0,)))
 
 
-def pair_kernel(second_ref, mine_ref, other_ref, moved_ref, transfer_ref):
+def pair_kernel(second_ref, mine_ref, other_ref, joined_ref):
+    late = second_ref[0] == 1
     for head in range(mine_ref.shape[0]):
         mine, other = mine_ref[head].astype(f32), other_ref[head].astype(f32)
-        late = second_ref[0] == 1
         earlier = jnp.where(late, other, mine).astype(bf16)
         later = jnp.where(late, mine, other)
         joined = contract(later[:, DK:].astype(bf16), earlier, ((1,), (0,)))
-        moved_ref[head] = (joined[:, :DK] + later[:, :DK]).astype(bf16)
-        transfer_ref[head] = joined[:, DK:].astype(bf16)
+        joined_ref[head, :, :DK] = (joined[:, :DK] + later[:, :DK]).astype(bf16)
+        joined_ref[head, :, DK:] = joined[:, DK:].astype(bf16)
 
 
 def finish_kernel(
-    where_ref, state_ref, other_ref, core_ref, reading_ref, gate_ref, gain_ref, gated_ref
+    where_ref,
+    near_pairs_ref,
+    far_pairs_ref,
+    other_ref,
+    core_ref,
+    reading_ref,
+    near_gate,
+    far_gate,
+    gain_ref,
+    gated_ref,
 ):
     states = []
-    for head in range(state_ref.shape[0]):
-        state = state_ref[head]
-        passed = contract(other_ref[head, :, DK:], state, ((1,), (0,))) + other_ref[
-            head, :, :DK
-        ].astype(f32)
-        states.append(jnp.where(where_ref[0] == 1, passed, state.astype(f32)))
+    for head in range(other_ref.shape[0]):
+        state = contract(near_pairs_ref[head, :, DK:], far_pairs_ref[head], ((1,), (0,)))
+        state += near_pairs_ref[head, :, :DK].astype(f32)
+        passed = contract(other_ref[head, :, DK:], state.astype(bf16), ((1,), (0,)))
+        passed += other_ref[head, :, :DK].astype(f32)
+        states.append(jnp.where(where_ref[0] == 1, passed, state))
+    gates = jnp.where(pl.program_id(0) < 2, near_gate[...].astype(f32), far_gate[...].astype(f32))
     for head, state in enumerate(states):
         columns = slice(head * DK, (head + 1) * DK)
         core = core_ref[:, columns] + contract_close(reading_ref[:, columns], state)
@@ -647,7 +660,7 @@
             * lax.rsqrt(jnp.mean(core * core, axis=-1, keepdims=True) + epsilon)
             * gain_ref[...]
         )
-        gate = gate_ref[:, columns].astype(f32)
+        gate = gates[:, columns]
         gated_ref[:, columns] = (normal * (gate / (1.0 + jnp.exp(-gate)))).astype(bf16)
 
 
@@ -693,7 +706,7 @@
     sources = ctx_count * head_count
     ctx_place = lax.axis_index("ctx")
     experts = (stream, moe_gain, router, expert_ids, expert_gate, expert_up, expert_down)
-    cut = out_weight.shape[0] * 5 // 128 * 16
+    cut = out_weight.shape[0] // 2
     out_halves = (out_weight[:cut], out_weight[cut:])
     if 2 * sources * stream.size <= GATHER_LIMIT and head_count == 4 and ctx_count in (6, 8):
         moe_out = expert_layer_gathered(*experts, sources, out_halves)
@@ -756,7 +769,6 @@
     far_pieces = from_others(mixer_in, near_raw[0], halos[2])
     far_raw = project(far_pieces, halos)
     rim = far_raw[4]
-    gate_raw = jnp.concatenate([near_raw[1], far_raw[1]], axis=0)
     key_heads = key_cols // DK
     taps = jnp.concatenate([query_conv, key_conv, value_conv], axis=1)
     rates = jnp.stack([decay_log, decay_bias])
@@ -793,32 +805,50 @@
     in_pair = (ctx_place % 2).reshape(1)
     other = lax.ppermute(moved, "ctx", [(place, place ^ 1) for place in range(ctx_count)])
     other = after(other, *upper)
-    state_shape = jax.ShapeDtypeStruct((heads, DK, DK), bf16)
-    added, transfer = pl.pallas_call(
+    window = pl.pallas_call(
         pair_kernel,
         in_specs=[in_smem, in_vmem, in_vmem],
-        out_shape=[state_shape, state_shape],
+        out_shape=jax.ShapeDtypeStruct(moved.shape, bf16),
         compiler_params=pltpu.CompilerParams(vmem_limit_bytes=8 << 20),
         name="pair",
     )(in_pair, moved, other)
-    state = passed_along(added, "ctx", 2)
-    for hop in range(ctx_count // 2 - 2):
-        leaving = jnp.einsum("hij,hjk->hik", transfer, state, preferred_element_type=f32)
-        leaving = (leaving + added.astype(f32)).astype(bf16)
-        if hop == ctx_count // 2 - 3:
-            leaving = after(leaving, *lower)
-        state = passed_along(leaving, "ctx", 2)
+
+    def composed(later, earlier, columns):
+        product = jnp.einsum(
+            "hij,hjk->hik",
+            later[:, :, DK:],
+            earlier[:, :, :columns],
+            preferred_element_type=f32,
+        )
+        added = (product[:, :, :DK] + later[:, :, :DK].astype(f32)).astype(bf16)
+        return jnp.concatenate([added, product[:, :, DK:].astype(bf16)], axis=2)
+
+    reach, near_pairs, far_pairs = 1, None, jnp.zeros((heads, DK, DK), bf16)
+    while reach < ctx_count // 2:
+        last = 2 * reach >= ctx_count // 2
+        if last and near_pairs is not None:
+            far_pairs = passed_along(window[:, :, :DK], "ctx", 2 * reach)
+        else:
+            arrived = passed_along(window, "ctx", 2 * reach)
+            if near_pairs is None:
+                near_pairs = arrived
+            else:
+                near_pairs = composed(near_pairs, arrived, 2 * DK)
+            window = composed(window, arrived, DK if 4 * reach >= ctx_count // 2 else 2 * DK)
+        reach *= 2
+    far_pairs = after(far_pairs, *lower)
 
     gated = pl.pallas_call(
         finish_kernel,
         grid_spec=pltpu.PrefetchScalarGridSpec(
             num_scalar_prefetch=1,
             grid=(head_count,),
-            in_specs=[whole_ref(state), whole_ref(other)]
+            in_specs=[whole_ref(near_pairs), whole_ref(far_pairs), whole_ref(other)]
             + [
                 pl.BlockSpec((tok_rows, value_cols), lambda step, where: (where[1] ^ step, 0)),
                 pl.BlockSpec((tok_rows, value_cols), lambda step, where: (where[1] ^ step, 0)),
-                pl.BlockSpec((tok_rows, value_cols), lambda step, where: (step, 0)),
+                pl.BlockSpec((tok_rows, value_cols), lambda step, where: (step % 2, 0)),
+                pl.BlockSpec((tok_rows, value_cols), lambda step, where: (step % 2, 0)),
                 pl.BlockSpec((1, DK), lambda step, where: (0, 0)),
             ],
             out_specs=pl.BlockSpec((tok_rows, value_cols), lambda step, where: (step, 0)),
@@ -828,11 +858,13 @@
         name="finish",
     )(
         jnp.stack([ctx_place % 2, head_place]),
-        state,
+        near_pairs,
+        far_pairs,
         other,
         core,
         reading,
-        gate_raw,
+        near_raw[1],
+        far_raw[1],
         head_gain.reshape(1, -1),
     )
     gated_parts = []
@@ -843,7 +875,7 @@
     far_weights = []
     for shard in zip(upper, lower):
         far_weights += shard
-        far_weights += [crossed(after(part, state), 1) for part in shard]
+        far_weights += [crossed(after(part, far_pairs), 1) for part in shard]
 
     def multiplied(parts, weights, begun, kind):
         columns = pl.BlockSpec((tok_rows, width // 4), lambda n: (0, n))

time: 307 us -> 283 us (0.922)
  starting transfers between devices: 55.4 us -> 43.3 us
  waiting for transfers between devices: 156 us -> 148 us
  other arithmetic: 9.51 us -> 5.77 us
    ppermute x14, starting transfers between devices: 25.1 us -> 10.7 us  [crossed(): return lax.ppermute(value, 'head', pairs)]
    ppermute x31 -> x33, waiting for transfers between devices: 126 us -> 119 us  [sent(): return lax.ppermute(value, ('ctx', 'head'), pairs)]
    ppermute x4 -> x3, waiting for transfers between devices: 16.4 us -> 12.2 us  [passed_along(): lax.ppermute(value, axis, [(source, source + steps) for source in range(f...]
    ppermute x31 -> x33, starting transfers between devices: 24.2 us -> 27.8 us  [sent(): return lax.ppermute(value, ('ctx', 'head'), pairs)]
    unnamed x66 -> x86, local copies, waits for them, and re-layouts: 11.4 us -> 13.9 us
    pallas_call x3 -> x4, Pallas kernels: 7.37 us -> 8.29 us  [spread(): pl.pallas_call(functools.partial(spread_kernel, slots=slots, places=place...]
  transfers between devices with their start and end apart: 50 -> 51, of which waited for: 29 -> 31; matrix products, arithmetic and copies ran while one was open for 3% -> 2% of each run, Pallas kernels for 17% -> 19%
where the time goes in v3:
time: 283 us; the launch traced here: 282 us
  waiting for transfers between devices  148 us (52%)
  Pallas kernels  68.1 us (24%)
  starting transfers between devices  43.3 us (15%)
  local copies, waits for them, and re-layouts  15.9 us (6%)
  other arithmetic  5.77 us (2%)
    ppermute x33, waiting for transfers between devices, sent(): return lax.ppermute(value, ('ctx', 'head'), pairs)  119 us
    ppermute x33, starting transfers between devices, sent(): return lax.ppermute(value, ('ctx', 'head'), pairs)  27.8 us
    pallas_call x2, Pallas kernels, run_experts(): pl.pallas_call(expert_kernel, grid=(local_experts,), in_specs=[row_spec]...  16.5 us
    pallas_call x1, Pallas kernels, on_device(): pl.pallas_call(functools.partial(delta_kernel, key_heads=key_heads, chunk...  16.4 us
    unnamed x86, local copies, waits for them, and re-layouts  13.9 us
    ppermute x3, waiting for transfers between devices, passed_along(): lax.ppermute(value, axis, [(source, source + steps) for source in range(f...  12.2 us
    ppermute x14, starting transfers between devices, crossed(): return lax.ppermute(value, 'head', pairs)  10.7 us
    ppermute x14, waiting for transfers between devices, crossed(): return lax.ppermute(value, 'head', pairs)  8.97 us
  transfers between devices with their start and end apart: 51, of which 31 were waited for; matrix products, arithmetic and copies ran while one was open for 2% of the time, Pallas kernels for 19%

profile of v3, /device:TPU:25, one launch (start us, length us, event | category | flops | bytes accessed | tf_op | source)
XLA Modules:
  0.0 282.4 jit_solution(11908318483503252445)
XLA Ops:
  7.5 9.3 %collective-permute-done.block_10.refs_1_ = bf16[128,2176]{1,0:T(8,128)(2,1)S(1)} collective-permute-done((bf16[128,2176]{1,0:T(8,128)(2,1)S(1)}, bf16[128,2176]{1,0:T(8,128)(2,1)S(1)}, u32[]{:S(2)}, u32[]{:S(2)}) %collective-permute-start) | collective-permute-done | bytes 557088 | tf_op jit(solution)/shard_map/ppermute | solution.py:189
  16.8 3.9 %collective-permute-done.1.block_01.refs_2_ = bf16[128,2176]{1,0:T(8,128)(2,1)S(1)} collective-permute-done((bf16[128,2176]{1,0:T(8,128)(2,1)S(1)}, bf16[128,2176]{1,0:T(8,128)(2,1)S(1)}, u32[]{:S(2)}, u32[]{:S(2)}) %collective-permute-start.1) | collective-permute-done | bytes 557088 | tf_op jit(solution)/shard_map/ppermute | solution.py:189
  22.5 11.1 %collective-permute-done.5.block_10.refs_1_ = bf16[128,2176]{1,0:T(8,128)(2,1)} collective-permute-done((bf16[128,2176]{1,0:T(8,128)(2,1)S(1)}, bf16[128,2176]{1,0:T(8,128)(2,1)}, u32[]{:S(2)}, u32[]{:S(2)}) %collective-permute-start.5) | collective-permute-done | bytes 557088 | tf_op jit(solution)/shard_map/ppermute | solution.py:189
  33.5 2.3 collective-permute-done.4.block_00.refs_0_
  36.7 2.4 collective-permute-start.8
  41.1 9.1 %collective-permute-done.8.block_00.refs_0_ = bf16[128,2176]{1,0:T(8,128)(2,1)} collective-permute-done((bf16[128,2176]{1,0:T(8,128)(2,1)S(1)}, bf16[128,2176]{1,0:T(8,128)(2,1)}, u32[]{:S(2)}, u32[]{:S(2)}) %collective-permute-start.8) | collective-permute-done | bytes 557088 | tf_op jit(solution)/shard_map/ppermute | solution.py:189
  50.2 1.8 collective-permute-done.9.block_10.refs_1_
  55.8 5.0 %collective-permute-done.2.block_11.refs_3_ = bf16[128,2176]{1,0:T(8,128)(2,1)S(1)} collective-permute-done((bf16[128,2176]{1,0:T(8,128)(2,1)S(1)}, bf16[128,2176]{1,0:T(8,128)(2,1)S(1)}, u32[]{:S(2)}, u32[]{:S(2)}) %collective-permute-start.2) | collective-permute-done | bytes 557088 | tf_op jit(solution)/shard_map/ppermute | solution.py:189
  61.9 3.5 %collective-permute-start.14 = (bf16[2,96,2048]{2,1,0:T(8,128)(2,1)S(1)}, bf16[2,96,2048]{2,1,0:T(8,128)(2,1)S(1)}, u32[]{:S(2)}, u32[]{:S(2)}) collective-permute-start(bf16[2,96,2048]{2,1,0:T(8,128)(2,1)S(1)} %get-tuple-element.70), channel_id=1, source_target_pairs={{0,1},{1,0},{2,3},{3,2},{4,5},{5,4},{6,7},{7,6},{8,9},{9,8},{10,11... | collective-permute-start | bytes 2359304 | tf_op jit(solution)/shard_map/ppermute | solution.py:189
  65.4 6.7 %collective-permute-done.7.block_11.refs_3_ = bf16[128,2176]{1,0:T(8,128)(2,1)} collective-permute-done((bf16[128,2176]{1,0:T(8,128)(2,1)}, bf16[128,2176]{1,0:T(8,128)(2,1)}, u32[]{:S(2)}, u32[]{:S(2)}) %collective-permute-start.7) | collective-permute-done | bytes 557088 | tf_op jit(solution)/shard_map/ppermute | solution.py:189
  72.0 2.3 collect.5
  74.7 3.3 %collective-permute-done.12.block_01.refs_2_ = bf16[128,2176]{1,0:T(8,128)(2,1)S(1)} collective-permute-done((bf16[128,2176]{1,0:T(8,128)(2,1)}, bf16[128,2176]{1,0:T(8,128)(2,1)S(1)}, u32[]{:S(2)}, u32[]{:S(2)}) %collective-permute-start.12) | collective-permute-done | bytes 557088 | tf_op jit(solution)/shard_map/ppermute | solution.py:189
  78.0 5.7 %collective-permute-done.13.block_11.refs_3_ = bf16[128,2176]{1,0:T(8,128)(2,1)S(1)} collective-permute-done((bf16[128,2176]{1,0:T(8,128)(2,1)}, bf16[128,2176]{1,0:T(8,128)(2,1)S(1)}, u32[]{:S(2)}, u32[]{:S(2)}) %collective-permute-start.13) | collective-permute-done | bytes 557088 | tf_op jit(solution)/shard_map/ppermute | solution.py:189
  83.7 2.5 collect.6
  86.7 1.9 collective-permute-done.16.refs_5_
  88.6 10.2 %experts.2 = (bf16[2,288,2048]{2,1,0:T(8,128)(2,1)S(1)}, bf16[2,288,2048]{2,1,0:T(8,128)(2,1)S(1)}) custom-call(bf16[2,96,2048]{2,1,0:T(8,128)(2,1)S(1)} %get-tuple-element.61.refs_0_, bf16[2,96,2048]{2,1,0:T(8,128)(2,1)S(1)} %get-tuple-element.64.refs_1_, bf16[2,96,2048]{2,1,0:T(8,128)(2,1)S(1)} %get-tuple-element.69.refs_2_, ...), custom_call_target="tpu_custom_call" | custom-call | flops 14949999616 | bytes 13000000 | tf_op jit(solution)/shard_map/experts/pallas_call | solution.py:264
  99.6 3.8 %collective-permute-done.17.refs_6_ = bf16[2,288,2048]{2,1,0:T(8,128)(2,1)S(1)} collective-permute-done((bf16[2,288,2048]{2,1,0:T(8,128)(2,1)S(1)}, bf16[2,288,2048]{2,1,0:T(8,128)(2,1)S(1)}, u32[]{:S(2)}, u32[]{:S(2)}) %collective-permute-start.17) | collective-permute-done | bytes 2359328 | tf_op jit(solution)/shard_map/ppermute | solution.py:189
  103.4 2.3 spread.6
  106.2 2.3 spread.5
  109.6 2.4 collect.7
  113.0 6.7 %collective-permute-done.22 = bf16[1,2,128,2048]{3,2,1,0:T(8,128)(2,1)S(1)} collective-permute-done((bf16[1,2,128,2048]{3,2,1,0:T(8,128)(2,1)S(1)}, bf16[1,2,128,2048]{3,2,1,0:T(8,128)(2,1)S(1)}, u32[]{:S(2)}, u32[]{:S(2)}) %collective-permute-start.22) | collective-permute-done | bytes 1048608 | tf_op jit(solution)/shard_map/ppermute | solution.py:189
  121.1 6.3 %experts.3 = (bf16[2,96,2048]{2,1,0:T(8,128)(2,1)S(1)}, bf16[2,96,2048]{2,1,0:T(8,128)(2,1)S(1)}) custom-call(bf16[2,96,2048]{2,1,0:T(8,128)(2,1)S(1)} %get-tuple-element.86.refs_0_, bf16[2,96,2048]{2,1,0:T(8,128)(2,1)S(1)} %collective-permute-done.28.refs_1_, bf16[2,2048,512]{2,1,0:T(8,128)(2,1)S(1)} %copy-done.2, bf16[2,2048,512]{2,1,0:T(8,128)(2,1)S(1)} %copy-done.3, ...), custom_call_target="tpu_custom_call" | custom-call | flops 1150000000 | bytes 1000000 | tf_op jit(solution)/shard_map/experts/pallas_call | solution.py:264
  128.3 8.3 %collective-permute-done.20 = bf16[1,2,128,2048]{3,2,1,0:T(8,128)(2,1)S(1)} collective-permute-done((bf16[1,2,128,2048]{3,2,1,0:T(8,128)(2,1)S(1)}, bf16[1,2,128,2048]{3,2,1,0:T(8,128)(2,1)S(1)}, u32[]{:S(2)}, u32[]{:S(2)}) %collective-permute-start.20) | collective-permute-done | bytes 1048608 | tf_op jit(solution)/shard_map/ppermute | solution.py:189
  138.5 2.2 spread.7
  145.1 6.0 %collective-permute-done.24 = bf16[128,2048]{1,0:T(8,128)(2,1)S(1)} collective-permute-done((bf16[128,2048]{1,0:T(8,128)(2,1)S(1)}, bf16[128,2048]{1,0:T(8,128)(2,1)S(1)}, u32[]{:S(2)}, u32[]{:S(2)}) %collective-permute-start.24) | collective-permute-done | bytes 524320 | tf_op jit(solution)/shard_map/ppermute | solution.py:189
  151.5 1.7 collective-permute-start.25
  153.2 4.8 %collective-permute-done.30 = bf16[1,2,128,2048]{3,2,1,0:T(8,128)(2,1)S(1)} collective-permute-done((bf16[1,2,128,2048]{3,2,1,0:T(8,128)(2,1)S(1)}, bf16[1,2,128,2048]{3,2,1,0:T(8,128)(2,1)S(1)}, u32[]{:S(2)}, u32[]{:S(2)}) %collective-permute-start.30) | collective-permute-done | bytes 1048608 | tf_op jit(solution)/shard_map/ppermute | solution.py:189
  159.5 7.6 %collective-permute-done.19 = bf16[128,2048]{1,0:T(8,128)(2,1)S(1)} collective-permute-done((bf16[128,2048]{1,0:T(8,128)(2,1)S(1)}, bf16[128,2048]{1,0:T(8,128)(2,1)S(1)}, u32[]{:S(2)}, u32[]{:S(2)}) %collective-permute-start.19) | collective-permute-done | bytes 524320 | tf_op jit(solution)/shard_map/ppermute | solution.py:189
  168.0 4.2 %collective-permute-done.31 = bf16[128,2048]{1,0:T(8,128)(2,1)S(1)} collective-permute-done((bf16[128,2048]{1,0:T(8,128)(2,1)S(1)}, bf16[128,2048]{1,0:T(8,128)(2,1)S(1)}, u32[]{:S(2)}, u32[]{:S(2)}) %collective-permute-start.31) | collective-permute-done | bytes 524320 | tf_op jit(solution)/shard_map/ppermute | solution.py:189
  174.8 3.5 %collective-permute-done.18 = bf16[128,2048]{1,0:T(8,128)(2,1)S(1)} collective-permute-done((bf16[128,2048]{1,0:T(8,128)(2,1)S(1)}, bf16[128,2048]{1,0:T(8,128)(2,1)S(1)}, u32[]{:S(2)}, u32[]{:S(2)}) %collective-permute-start.18) | collective-permute-done | bytes 524320 | tf_op jit(solution)/shard_map/ppermute | solution.py:189
  178.8 9.4 %collective-permute-done.32 = bf16[128,2048]{1,0:T(8,128)(2,1)S(1)} collective-permute-done((bf16[128,2048]{1,0:T(8,128)(2,1)S(1)}, bf16[128,2048]{1,0:T(8,128)(2,1)S(1)}, u32[]{:S(2)}, u32[]{:S(2)}) %collective-permute-start.32) | collective-permute-done | bytes 524320 | tf_op jit(solution)/shard_map/ppermute | solution.py:189
  190.7 2.3 collective-permute-start.33
  194.3 2.3 collective-permute-done.33.refs_2_
  198.2 1.6 copy-done.18
  199.8 1.6 copy-done.20
  203.9 3.6 %project.2 = (bf16[256,1024]{1,0:T(8,128)(2,1)S(1)}, bf16[256,512]{1,0:T(8,128)(2,1)S(1)}, f32[256,4]{1,0:T(8,128)S(1)}, f32[256,4]{1,0:T(8,128)S(1)}) custom-call(s32[1]{0:T(128)} %bitcast.17.place_ref, bf16[128,2048]{1,0:T(8,128)(2,1)S(1)} %multiply_convert_fusion.refs_0_, bf16[128,2048]{1,0:T(8,128)(2,1)} %collective-permute-done.34.refs_1_, ...), custom_call_target="tpu_custom_call" | custom-call | flops 4600000000 | bytes 4000000 | tf_op jit(solution)/shard_map/project/pallas_call | solution.py:759
  208.2 1.8 collective-permute-start.37
  212.6 3.5 %project.3 = (bf16[256,1024]{1,0:T(8,128)(2,1)S(1)}, bf16[256,512]{1,0:T(8,128)(2,1)S(1)}, f32[256,4]{1,0:T(8,128)S(1)}, f32[256,4]{1,0:T(8,128)S(1)}, f32[16,1024]{1,0:T(8,128)S(1)}) custom-call(s32[1]{0:T(128)} %bitcast.17.place_ref, bf16[128,2048]{1,0:T(8,128)(2,1)} %collective-permute-done.35.refs_0_, ...), custom_call_target="tpu_custom_call" | custom-call | flops 4600000000 | bytes 4000000 | tf_op jit(solution)/shard_map/project/pallas_call | solution.py:759
  216.2 16.4 %delta.1 = (f32[512,512]{1,0:T(8,128)S(1)}, f32[512,512]{1,0:T(8,128)S(1)}, bf16[4,128,256]{2,1,0:T(8,128)(2,1)}) custom-call(s32[1]{0:T(128)} %bitcast.17.place_ref, bf16[256,1024]{1,0:T(8,128)(2,1)S(1)} %get-tuple-element.96.near_raw, bf16[256,1024]{1,0:T(8,128)(2,1)S(1)} %get-tuple-element.98.far_raw, f32[256,4]{1,0:T(8,128)S(1)} %get-tuple-element.99.near_beta, ...), custom_call_target="tpu_custom_call" | custom-call | flops 18400000000 | bytes 16000000 | tf_op jit(solution)/shard_map/delta/pallas_call | solution.py:776
  234.9 7.9 %collective-permute-done.40.other_ref = bf16[4,128,256]{2,1,0:T(8,128)(2,1)S(1)} collective-permute-done((bf16[4,128,256]{2,1,0:T(8,128)(2,1)}, bf16[4,128,256]{2,1,0:T(8,128)(2,1)S(1)}, u32[]{:S(2)}, u32[]{:S(2)}) %collective-permute-start.40) | collective-permute-done | bytes 262176 | tf_op jit(solution)/shard_map/ppermute | solution.py:806
  245.3 7.5 %collective-permute-done.42.near_pairs_ref = bf16[4,128,256]{2,1,0:T(8,128)(2,1)S(1)} collective-permute-done((bf16[4,128,256]{2,1,0:T(8,128)(2,1)S(1)}, bf16[4,128,256]{2,1,0:T(8,128)(2,1)S(1)}, u32[]{:S(2)}, u32[]{:S(2)}) %collective-permute-start.42) | collective-permute-done | bytes 262176 | tf_op jit(solution)/shard_map/ppermute | solution.py:24
  254.3 5.1 %collective-permute-done.44.refs_3_ = bf16[256,2048]{1,0:T(8,128)(2,1)} collective-permute-done((bf16[256,2048]{1,0:T(8,128)(2,1)}, bf16[256,2048]{1,0:T(8,128)(2,1)}, u32[]{:S(2)}, u32[]{:S(2)}) %collective-permute-start.44) | collective-permute-done | bytes 1048608 | tf_op jit(solution)/shard_map/ppermute | solution.py:722
  259.4 2.4 collective-permute-done.43.far_pairs_ref
  261.8 1.5 collective-permute-start.48
  266.6 3.1 %finish.1 = bf16[512,512]{1,0:T(8,128)(2,1)S(1)} custom-call(s32[2]{0:T(128)S(1)} %pad_add_fusion.where_ref, bf16[4,128,256]{2,1,0:T(8,128)(2,1)S(1)} %collective-permute-done.42.near_pairs_ref, bf16[4,128,128]{2,1,0:T(8,128)(2,1)S(1)} %collective-permute-done.43.far_pairs_ref, bf16[4,128,256]{2,1,0:T(8,128)(2,1)S(1)} %collective-permute-done.40.other_ref, ...), custom_call_target="tpu_custom_call" | custom-call | tf_op jit(solution)/shard_map/finish/pallas_call | solution.py:841
  272.5 3.2 %output.2.refs_6_ = f32[128,2048]{1,0:T(8,128)S(1)} custom-call(bf16[128,512]{1,0:T(8,128)(2,1)S(1)} %get-tuple-element.121.refs_0_, bf16[128,512]{1,0:T(8,128)(2,1)S(1)} %collective-permute-done.49.refs_1_, bf16[512,2048]{1,0:T(8,128)(2,1)S(1)} %copy-done.4, bf16[512,2048]{1,0:T(8,128)(2,1)} %collective-permute-done.50.refs_3_), custom_call_target="tpu_custom_call" | custom-call | flops 3449999872 | bytes 3000000 | tf_op jit(solution)/shard_map/output/pallas_call | solution.py:882
  275.7 2.6 collective-permute-done.46.refs_1_
  278.4 4.1 %output.3 = bf16[128,2048]{1,0:T(8,128)(2,1)} custom-call(bf16[128,512]{1,0:T(8,128)(2,1)S(1)} %collective-permute-done.45.refs_0_, bf16[128,512]{1,0:T(8,128)(2,1)S(1)} %collective-permute-done.46.refs_1_, bf16[256,2048]{1,0:T(8,128)(2,1)} %collective-permute-done.41.refs_2_, bf16[256,2048]{1,0:T(8,128)(2,1)} %collective-permute-done.44.refs_3_, ...), custom_call_target="tpu_custom_call" | custom-call | flops 3449999872 | bytes 3000000 | tf_op jit(solution)/shard_map/output/pallas_call | solution.py:882
  (188 shorter events, 58.2 us)
Async XLA Ops:
  4.8 12.0 %collective-permute-start = (bf16[128,2176]{1,0:T(8,128)(2,1)S(1)}, bf16[128,2176]{1,0:T(8,128)(2,1)S(1)}, u32[]{:S(2)}, u32[]{:S(2)}) collective-permute-start(bf16[128,2176]{1,0:T(8,128)(2,1)S(1)} %concatenate.6.block_00.refs_0_), channel_id=1, source_target_pairs={{0,4},{1,3},{2,6},{3,1},{4,0},{5,7},{6,2},{7,5},{8,12},{9,11},{10,... | collective-permute-start | bytes 1671176 | tf_op jit(solution)/shard_map/ppermute | solution.py:189
  6.1 14.6 %collective-permute-start.1 = (bf16[128,2176]{1,0:T(8,128)(2,1)S(1)}, bf16[128,2176]{1,0:T(8,128)(2,1)S(1)}, u32[]{:S(2)}, u32[]{:S(2)}) collective-permute-start(bf16[128,2176]{1,0:T(8,128)(2,1)S(1)} %concatenate.6.block_00.refs_0_), channel_id=1, source_target_pairs={{0,2},{1,5},{2,0},{3,7},{4,6},{5,1},{6,4},{7,3},{8,10},{9,13},{10,... | collective-permute-start | bytes 1671176 | tf_op jit(solution)/shard_map/ppermute | solution.py:189
  7.3 14.7 %collective-permute-start.3 = (bf16[128,2176]{1,0:T(8,128)(2,1)S(1)}, bf16[128,2176]{1,0:T(8,128)(2,1)S(1)}, u32[]{:S(2)}, u32[]{:S(2)}) collective-permute-start(bf16[128,2176]{1,0:T(8,128)(2,1)S(1)} %concatenate.6.block_00.refs_0_), channel_id=1, source_target_pairs={{0,24},{1,25},{2,26},{3,27},{4,28},{5,29},{6,30},{7,31},{8,0},{9,1... | collective-permute-start | bytes 1671176 | tf_op jit(solution)/shard_map/ppermute | solution.py:189
  22.0 11.5 %collective-permute-start.5 = (bf16[128,2176]{1,0:T(8,128)(2,1)S(1)}, bf16[128,2176]{1,0:T(8,128)(2,1)}, u32[]{:S(2)}, u32[]{:S(2)}) collective-permute-start(bf16[128,2176]{1,0:T(8,128)(2,1)S(1)} %collective-permute-done.3.block_00.refs_0_), channel_id=1, source_target_pairs={{0,4},{1,3},{2,6},{3,1},{4,0},{5,7},{6,2},{7,5},{8,12},{9,11},{10,... | collective-permute-start | bytes 1671176 | tf_op jit(solution)/shard_map/ppermute | solution.py:189
  22.2 13.6 %collective-permute-start.4 = (bf16[128,2176]{1,0:T(8,128)(2,1)S(1)}, bf16[128,2176]{1,0:T(8,128)(2,1)}, u32[]{:S(2)}, u32[]{:S(2)}) collective-permute-start(bf16[128,2176]{1,0:T(8,128)(2,1)S(1)} %collective-permute-done.3.block_00.refs_0_), channel_id=1, source_target_pairs={{0,24},{1,25},{2,26},{3,27},{4,28},{5,29},{6,30},{7,31},{8,0},{9,1... | collective-permute-start | bytes 1671176 | tf_op jit(solution)/shard_map/ppermute | solution.py:189
  22.3 13.6 %collective-permute-start.6 = (bf16[128,2176]{1,0:T(8,128)(2,1)S(1)}, bf16[128,2176]{1,0:T(8,128)(2,1)S(1)}, u32[]{:S(2)}, u32[]{:S(2)}) collective-permute-start(bf16[128,2176]{1,0:T(8,128)(2,1)S(1)} %collective-permute-done.3.block_00.refs_0_), channel_id=1, source_target_pairs={{0,2},{1,5},{2,0},{3,7},{4,6},{5,1},{6,4},{7,3},{8,10},{9,13},{10,... | collective-permute-start | bytes 1671176 | tf_op jit(solution)/shard_map/ppermute | solution.py:189
  36.7 13.5 %collective-permute-start.8 = (bf16[128,2176]{1,0:T(8,128)(2,1)S(1)}, bf16[128,2176]{1,0:T(8,128)(2,1)}, u32[]{:S(2)}, u32[]{:S(2)}) collective-permute-start(bf16[128,2176]{1,0:T(8,128)(2,1)S(1)} %concatenate.6.block_00.refs_0_), channel_id=1, source_target_pairs={{0,8},{1,9},{2,10},{3,11},{4,12},{5,13},{6,14},{7,15},{8,16},{9,17... | collective-permute-start | bytes 1671176 | tf_op jit(solution)/shard_map/ppermute | solution.py:189
  39.0 12.9 %collective-permute-start.9 = (bf16[128,2176]{1,0:T(8,128)(2,1)}, bf16[128,2176]{1,0:T(8,128)(2,1)}, u32[]{:S(2)}, u32[]{:S(2)}) collective-permute-start(bf16[128,2176]{1,0:T(8,128)(2,1)} %collective-permute-done.4.block_00.refs_0_), channel_id=1, source_target_pairs={{0,4},{1,3},{2,6},{3,1},{4,0},{5,7},{6,2},{7,5},{8,12},{9,11},{10,... | collective-permute-start | bytes 1671176 | tf_op jit(solution)/shard_map/ppermute | solution.py:189
  39.3 13.6 %collective-permute-start.10 = (bf16[128,2176]{1,0:T(8,128)(2,1)}, bf16[128,2176]{1,0:T(8,128)(2,1)}, u32[]{:S(2)}, u32[]{:S(2)}) collective-permute-start(bf16[128,2176]{1,0:T(8,128)(2,1)} %collective-permute-done.4.block_00.refs_0_), channel_id=1, source_target_pairs={{0,2},{1,5},{2,0},{3,7},{4,6},{5,1},{6,4},{7,3},{8,10},{9,13},{10,... | collective-permute-start | bytes 1671176 | tf_op jit(solution)/shard_map/ppermute | solution.py:189
  39.6 21.2 %collective-permute-start.2 = (bf16[128,2176]{1,0:T(8,128)(2,1)S(1)}, bf16[128,2176]{1,0:T(8,128)(2,1)S(1)}, u32[]{:S(2)}, u32[]{:S(2)}) collective-permute-start(bf16[128,2176]{1,0:T(8,128)(2,1)S(1)} %collective-permute-done.block_10.refs_1_), channel_id=1, source_target_pairs={{0,2},{1,5},{2,0},{3,7},{4,6},{5,1},{6,4},{7,3},{8,10},{9,13},{10,... | collective-permute-start | bytes 1671176 | tf_op jit(solution)/shard_map/ppermute | solution.py:189
  40.8 31.3 %collective-permute-start.7 = (bf16[128,2176]{1,0:T(8,128)(2,1)}, bf16[128,2176]{1,0:T(8,128)(2,1)}, u32[]{:S(2)}, u32[]{:S(2)}) collective-permute-start(bf16[128,2176]{1,0:T(8,128)(2,1)} %collective-permute-done.5.block_10.refs_1_), channel_id=1, source_target_pairs={{0,2},{1,5},{2,0},{3,7},{4,6},{5,1},{6,4},{7,3},{8,10},{9,13},{10,... | collective-permute-start | bytes 1671176 | tf_op jit(solution)/shard_map/ppermute | solution.py:189
  52.9 21.8 %collective-permute-start.11 = (bf16[128,2176]{1,0:T(8,128)(2,1)}, bf16[128,2176]{1,0:T(8,128)(2,1)S(1)}, u32[]{:S(2)}, u32[]{:S(2)}) collective-permute-start(bf16[128,2176]{1,0:T(8,128)(2,1)} %collective-permute-done.8.block_00.refs_0_), channel_id=1, source_target_pairs={{0,4},{1,3},{2,6},{3,1},{4,0},{5,7},{6,2},{7,5},{8,12},{9,11},{10,... | collective-permute-start | bytes 1671176 | tf_op jit(solution)/shard_map/ppermute | solution.py:189
  54.2 23.8 %collective-permute-start.12 = (bf16[128,2176]{1,0:T(8,128)(2,1)}, bf16[128,2176]{1,0:T(8,128)(2,1)S(1)}, u32[]{:S(2)}, u32[]{:S(2)}) collective-permute-start(bf16[128,2176]{1,0:T(8,128)(2,1)} %collective-permute-done.8.block_00.refs_0_), channel_id=1, source_target_pairs={{0,2},{1,5},{2,0},{3,7},{4,6},{5,1},{6,4},{7,3},{8,10},{9,13},{10,... | collective-permute-start | bytes 1671176 | tf_op jit(solution)/shard_map/ppermute | solution.py:189
  54.7 29.0 %collective-permute-start.13 = (bf16[128,2176]{1,0:T(8,128)(2,1)}, bf16[128,2176]{1,0:T(8,128)(2,1)S(1)}, u32[]{:S(2)}, u32[]{:S(2)}) collective-permute-start(bf16[128,2176]{1,0:T(8,128)(2,1)} %collective-permute-done.9.block_10.refs_1_), channel_id=1, source_target_pairs={{0,2},{1,5},{2,0},{3,7},{4,6},{5,1},{6,4},{7,3},{8,10},{9,13},{10,... | collective-permute-start | bytes 1671176 | tf_op jit(solution)/shard_map/ppermute | solution.py:189
  61.9 24.8 %collective-permute-start.14 = (bf16[2,96,2048]{2,1,0:T(8,128)(2,1)S(1)}, bf16[2,96,2048]{2,1,0:T(8,128)(2,1)S(1)}, u32[]{:S(2)}, u32[]{:S(2)}) collective-permute-start(bf16[2,96,2048]{2,1,0:T(8,128)(2,1)S(1)} %get-tuple-element.70), channel_id=1, source_target_pairs={{0,1},{1,0},{2,3},{3,2},{4,5},{5,4},{6,7},{7,6},{8,9},{9,8},{10,11... | collective-permute-start | bytes 2359304 | tf_op jit(solution)/shard_map/ppermute | solution.py:189
  74.4 12.3 %collective-permute-start.15 = (bf16[2,96,2048]{2,1,0:T(8,128)(2,1)S(1)}, bf16[2,96,2048]{2,1,0:T(8,128)(2,1)S(1)}, u32[]{:S(2)}, u32[]{:S(2)}) collective-permute-start(bf16[2,96,2048]{2,1,0:T(8,128)(2,1)S(1)} %get-tuple-element.71), channel_id=1, source_target_pairs={{0,1},{1,0},{2,3},{3,2},{4,5},{5,4},{6,7},{7,6},{8,9},{9,8},{10,11... | collective-permute-start | bytes 2359304 | tf_op jit(solution)/shard_map/ppermute | solution.py:189
  98.8 4.6 %collective-permute-start.17 = (bf16[2,288,2048]{2,1,0:T(8,128)(2,1)S(1)}, bf16[2,288,2048]{2,1,0:T(8,128)(2,1)S(1)}, u32[]{:S(2)}, u32[]{:S(2)}) collective-permute-start(bf16[2,288,2048]{2,1,0:T(8,128)(2,1)S(1)} %get-tuple-element.74), channel_id=1, source_target_pairs={{0,1},{1,0},{2,3},{3,2},{4,5},{5,4},{6,7},{7,6},{8,9},{9,8},{10,11... | collective-permute-start | bytes 7077896 | tf_op jit(solution)/shard_map/ppermute | solution.py:189
  99.2 10.4 %collective-permute-start.27 = (bf16[128,2176]{1,0:T(8,128)(2,1)S(1)}, bf16[128,2176]{1,0:T(8,128)(2,1)S(1)}, u32[]{:S(2)}, u32[]{:S(2)}) collective-permute-start(bf16[128,2176]{1,0:T(8,128)(2,1)S(1)} %collective-permute-done.11.block_10.refs_1_), channel_id=1, source_target_pairs={{0,2},{1,5},{2,0},{3,7},{4,6},{5,1},{6,4},{7,3},{8,10},{9,13},{10,... | collective-permute-start | bytes 1671176 | tf_op jit(solution)/shard_map/ppermute | solution.py:189
  105.7 14.0 %collective-permute-start.22 = (bf16[1,2,128,2048]{3,2,1,0:T(8,128)(2,1)S(1)}, bf16[1,2,128,2048]{3,2,1,0:T(8,128)(2,1)S(1)}, u32[]{:S(2)}, u32[]{:S(2)}) collective-permute-start(bf16[1,2,128,2048]{3,2,1,0:T(8,128)(2,1)S(1)} %get-tuple-element.82), channel_id=1, source_target_pairs={{0,2},{1,5},{2,0},{3,7},{4,6},{5,1},{6,4},{7,3},{8,10},{9,13},{10,... | collective-permute-start | bytes 3145736 | tf_op jit(solution)/shard_map/ppermute | solution.py:189
  108.4 28.2 %collective-permute-start.20 = (bf16[1,2,128,2048]{3,2,1,0:T(8,128)(2,1)S(1)}, bf16[1,2,128,2048]{3,2,1,0:T(8,128)(2,1)S(1)}, u32[]{:S(2)}, u32[]{:S(2)}) collective-permute-start(bf16[1,2,128,2048]{3,2,1,0:T(8,128)(2,1)S(1)} %get-tuple-element.79), channel_id=1, source_target_pairs={{0,2},{1,5},{2,0},{3,7},{4,6},{5,1},{6,4},{7,3},{8,10},{9,13},{10,... | collective-permute-start | bytes 3145736 | tf_op jit(solution)/shard_map/ppermute | solution.py:189
  112.0 9.1 %collective-permute-start.28 = (bf16[2,96,2048]{2,1,0:T(8,128)(2,1)S(1)}, bf16[2,96,2048]{2,1,0:T(8,128)(2,1)S(1)}, u32[]{:S(2)}, u32[]{:S(2)}) collective-permute-start(bf16[2,96,2048]{2,1,0:T(8,128)(2,1)S(1)} %get-tuple-element.87), channel_id=1, source_target_pairs={{0,1},{1,0},{2,3},{3,2},{4,5},{5,4},{6,7},{7,6},{8,9},{9,8},{10,11... | collective-permute-start | bytes 2359304 | tf_op jit(solution)/shard_map/ppermute | solution.py:189
  119.9 18.1 %collective-permute-start.23 = (bf16[128,2048]{1,0:T(8,128)(2,1)S(1)}, bf16[128,2048]{1,0:T(8,128)(2,1)S(1)}, u32[]{:S(2)}, u32[]{:S(2)}) collective-permute-start(bf16[128,2048]{1,0:T(8,128)(2,1)S(1)} %fusion.8), channel_id=1, source_target_pairs={{0,4},{1,3},{2,6},{3,1},{4,0},{5,7},{6,2},{7,5},{8,12},{9,11},{10,... | collective-permute-start | bytes 1572872 | tf_op jit(solution)/shard_map/ppermute | solution.py:189
  127.5 11.0 %collective-permute-start.29 = (bf16[2,96,2048]{2,1,0:T(8,128)(2,1)S(1)}, bf16[2,96,2048]{2,1,0:T(8,128)(2,1)S(1)}, u32[]{:S(2)}, u32[]{:S(2)}) collective-permute-start(bf16[2,96,2048]{2,1,0:T(8,128)(2,1)S(1)} %get-tuple-element.89), channel_id=1, source_target_pairs={{0,1},{1,0},{2,3},{3,2},{4,5},{5,4},{6,7},{7,6},{8,9},{9,8},{10,11... | collective-permute-start | bytes 2359304 | tf_op jit(solution)/shard_map/ppermute | solution.py:189
  136.7 8.4 %collective-permute-start.21 = (bf16[128,2048]{1,0:T(8,128)(2,1)S(1)}, bf16[128,2048]{1,0:T(8,128)(2,1)S(1)}, u32[]{:S(2)}, u32[]{:S(2)}) collective-permute-start(bf16[128,2048]{1,0:T(8,128)(2,1)S(1)} %fusion.11), channel_id=1, source_target_pairs={{0,4},{1,3},{2,6},{3,1},{4,0},{5,7},{6,2},{7,5},{8,12},{9,11},{10,... | collective-permute-start | bytes 1572872 | tf_op jit(solution)/shard_map/ppermute | solution.py:189
  138.2 13.0 %collective-permute-start.24 = (bf16[128,2048]{1,0:T(8,128)(2,1)S(1)}, bf16[128,2048]{1,0:T(8,128)(2,1)S(1)}, u32[]{:S(2)}, u32[]{:S(2)}) collective-permute-start(bf16[128,2048]{1,0:T(8,128)(2,1)S(1)} %fusion.10), channel_id=1, source_target_pairs={{0,8},{1,9},{2,10},{3,11},{4,12},{5,13},{6,14},{7,15},{8,16},{9,17... | collective-permute-start | bytes 1572872 | tf_op jit(solution)/shard_map/ppermute | solution.py:189
  140.7 17.3 %collective-permute-start.30 = (bf16[1,2,128,2048]{3,2,1,0:T(8,128)(2,1)S(1)}, bf16[1,2,128,2048]{3,2,1,0:T(8,128)(2,1)S(1)}, u32[]{:S(2)}, u32[]{:S(2)}) collective-permute-start(bf16[1,2,128,2048]{3,2,1,0:T(8,128)(2,1)S(1)} %get-tuple-element.91), channel_id=1, source_target_pairs={{0,2},{1,5},{2,0},{3,7},{4,6},{5,1},{6,4},{7,3},{8,10},{9,13},{10,... | collective-permute-start | bytes 3145736 | tf_op jit(solution)/shard_map/ppermute | solution.py:189
  142.7 24.4 %collective-permute-start.19 = (bf16[128,2048]{1,0:T(8,128)(2,1)S(1)}, bf16[128,2048]{1,0:T(8,128)(2,1)S(1)}, u32[]{:S(2)}, u32[]{:S(2)}) collective-permute-start(bf16[128,2048]{1,0:T(8,128)(2,1)S(1)} %get-tuple-element.119), channel_id=1, source_target_pairs={{0,2},{1,5},{2,0},{3,7},{4,6},{5,1},{6,4},{7,3},{8,10},{9,13},{10,... | collective-permute-start | bytes 1572872 | tf_op jit(solution)/shard_map/ppermute | solution.py:189
  151.5 15.6 %collective-permute-start.25 = (bf16[128,2048]{1,0:T(8,128)(2,1)S(1)}, bf16[128,2048]{1,0:T(8,128)(2,1)S(1)}, u32[]{:S(2)}, u32[]{:S(2)}) collective-permute-start(bf16[128,2048]{1,0:T(8,128)(2,1)S(1)} %fusion.14), channel_id=1, source_target_pairs={{0,8},{1,9},{2,10},{3,11},{4,12},{5,13},{6,14},{7,15},{8,16},{9,17... | collective-permute-start | bytes 1572872 | tf_op jit(solution)/shard_map/ppermute | solution.py:189
  158.2 14.1 %collective-permute-start.31 = (bf16[128,2048]{1,0:T(8,128)(2,1)S(1)}, bf16[128,2048]{1,0:T(8,128)(2,1)S(1)}, u32[]{:S(2)}, u32[]{:S(2)}) collective-permute-start(bf16[128,2048]{1,0:T(8,128)(2,1)S(1)} %fusion.5), channel_id=1, source_target_pairs={{0,4},{1,3},{2,6},{3,1},{4,0},{5,7},{6,2},{7,5},{8,12},{9,11},{10,... | collective-permute-start | bytes 1572872 | tf_op jit(solution)/shard_map/ppermute | solution.py:189
  159.2 19.2 %collective-permute-start.18 = (bf16[128,2048]{1,0:T(8,128)(2,1)S(1)}, bf16[128,2048]{1,0:T(8,128)(2,1)S(1)}, u32[]{:S(2)}, u32[]{:S(2)}) collective-permute-start(bf16[128,2048]{1,0:T(8,128)(2,1)S(1)} %get-tuple-element.118), channel_id=1, source_target_pairs={{0,2},{1,5},{2,0},{3,7},{4,6},{5,1},{6,4},{7,3},{8,10},{9,13},{10,... | collective-permute-start | bytes 1572872 | tf_op jit(solution)/shard_map/ppermute | solution.py:189
  167.3 11.6 %collective-permute-start.26 = (bf16[128,2048]{1,0:T(8,128)(2,1)S(1)}, bf16[128,2048]{1,0:T(8,128)(2,1)S(1)}, u32[]{:S(2)}, u32[]{:S(2)}) collective-permute-start(bf16[128,2048]{1,0:T(8,128)(2,1)S(1)} %fusion.15), channel_id=1, source_target_pairs={{0,4},{1,3},{2,6},{3,1},{4,0},{5,7},{6,2},{7,5},{8,12},{9,11},{10,... | collective-permute-start | bytes 1572872 | tf_op jit(solution)/shard_map/ppermute | solution.py:189
  172.5 15.8 %collective-permute-start.32 = (bf16[128,2048]{1,0:T(8,128)(2,1)S(1)}, bf16[128,2048]{1,0:T(8,128)(2,1)S(1)}, u32[]{:S(2)}, u32[]{:S(2)}) collective-permute-start(bf16[128,2048]{1,0:T(8,128)(2,1)S(1)} %fusion.7), channel_id=1, source_target_pairs={{0,24},{1,25},{2,26},{3,27},{4,28},{5,29},{6,30},{7,31},{8,0},{9,1... | collective-permute-start | bytes 1572872 | tf_op jit(solution)/shard_map/ppermute | solution.py:189
  189.2 7.9 %collective-permute-start.34 = (bf16[128,2048]{1,0:T(8,128)(2,1)S(1)}, bf16[128,2048]{1,0:T(8,128)(2,1)}, u32[]{:S(2)}, u32[]{:S(2)}) collective-permute-start(bf16[128,2048]{1,0:T(8,128)(2,1)S(1)} %multiply_convert_fusion.refs_0_), channel_id=1, source_target_pairs={{0,1},{1,0},{2,3},{3,2},{4,5},{5,4},{6,7},{7,6},{8,9},{9,8},{10,11... | collective-permute-start | bytes 1572872 | tf_op jit(solution)/shard_map/ppermute | solution.py:722
  189.7 18.4 %collective-permute-start.35 = (bf16[128,2048]{1,0:T(8,128)(2,1)S(1)}, bf16[128,2048]{1,0:T(8,128)(2,1)}, u32[]{:S(2)}, u32[]{:S(2)}) collective-permute-start(bf16[128,2048]{1,0:T(8,128)(2,1)S(1)} %multiply_convert_fusion.refs_0_), channel_id=1, source_target_pairs={{0,2},{1,3},{2,0},{3,1},{4,6},{5,7},{6,4},{7,5},{8,10},{9,11},{10,... | collective-permute-start | bytes 1572872 | tf_op jit(solution)/shard_map/ppermute | solution.py:722
  190.7 5.9 %collective-permute-start.33 = (bf16[16,2048]{1,0:T(8,128)(2,1)S(1)}, bf16[16,2048]{1,0:T(8,128)(2,1)S(1)}, u32[]{:S(2)}, u32[]{:S(2)}) collective-permute-start(bf16[16,2048]{1,0:T(8,128)(2,1)S(1)} %slice.76), channel_id=1, source_target_pairs={{0,4},{4,8},{8,12},{12,16},{16,20},{20,24},{24,28},{1,5},{5,9},{9,... | collective-permute-start | bytes 196616 | tf_op jit(solution)/shard_map/ppermute | solution.py:24
  196.6 11.6 %collective-permute-start.36 = (bf16[16,2048]{1,0:T(8,128)(2,1)S(1)}, bf16[16,2048]{1,0:T(8,128)(2,1)S(1)}, u32[]{:S(2)}, u32[]{:S(2)}) collective-permute-start(bf16[16,2048]{1,0:T(8,128)(2,1)S(1)} %collective-permute-done.33.refs_2_), channel_id=1, source_target_pairs={{0,2},{1,3},{2,0},{3,1},{4,6},{5,7},{6,4},{7,5},{8,10},{9,11},{10,... | collective-permute-start | bytes 196616 | tf_op jit(solution)/shard_map/ppermute | solution.py:722
  208.2 3.5 %collective-permute-start.37 = (bf16[128,2048]{1,0:T(8,128)(2,1)}, bf16[128,2048]{1,0:T(8,128)(2,1)S(1)}, u32[]{:S(2)}, u32[]{:S(2)}) collective-permute-start(bf16[128,2048]{1,0:T(8,128)(2,1)} %collective-permute-done.35.refs_0_), channel_id=1, source_target_pairs={{0,1},{1,0},{2,3},{3,2},{4,5},{5,4},{6,7},{7,6},{8,9},{9,8},{10,11... | collective-permute-start | bytes 1572872 | tf_op jit(solution)/shard_map/ppermute | solution.py:722
  210.0 2.7 collective-permute-start.38
  211.7 31.1 %collective-permute-start.41 = (bf16[256,2048]{1,0:T(8,128)(2,1)}, bf16[256,2048]{1,0:T(8,128)(2,1)}, u32[]{:S(2)}, u32[]{:S(2)}) collective-permute-start(bf16[256,2048]{1,0:T(8,128)(2,1)} %get-tuple-element.105), channel_id=1, source_target_pairs={{0,2},{1,3},{2,0},{3,1},{4,6},{5,7},{6,4},{7,5},{8,10},{9,11},{10,... | collective-permute-start | bytes 3145736 | tf_op jit(solution)/shard_map/ppermute | solution.py:722
  233.7 38.8 %collective-permute-start.50 = (bf16[512,2048]{1,0:T(8,128)(2,1)S(1)}, bf16[512,2048]{1,0:T(8,128)(2,1)}, u32[]{:S(2)}, u32[]{:S(2)}) collective-permute-start(bf16[512,2048]{1,0:T(8,128)(2,1)S(1)} %copy-done.4), channel_id=1, source_target_pairs={{0,1},{1,0},{2,3},{3,2},{4,5},{5,4},{6,7},{7,6},{8,9},{9,8},{10,11... | collective-permute-start | bytes 6291464 | tf_op jit(solution)/shard_map/ppermute | solution.py:722
  234.3 25.1 %collective-permute-start.44 = (bf16[256,2048]{1,0:T(8,128)(2,1)}, bf16[256,2048]{1,0:T(8,128)(2,1)}, u32[]{:S(2)}, u32[]{:S(2)}) collective-permute-start(bf16[256,2048]{1,0:T(8,128)(2,1)} %get-tuple-element.107), channel_id=1, source_target_pairs={{0,2},{1,3},{2,0},{3,1},{4,6},{5,7},{6,4},{7,5},{8,10},{9,11},{10,... | collective-permute-start | bytes 3145736 | tf_op jit(solution)/shard_map/ppermute | solution.py:722
  234.8 7.9 %collective-permute-start.40 = (bf16[4,128,256]{2,1,0:T(8,128)(2,1)}, bf16[4,128,256]{2,1,0:T(8,128)(2,1)S(1)}, u32[]{:S(2)}, u32[]{:S(2)}) collective-permute-start(bf16[4,128,256]{2,1,0:T(8,128)(2,1)} %get-tuple-element.104.mine_ref), channel_id=1, source_target_pairs={{0,4},{4,0},{8,12},{12,8},{16,20},{20,16},{24,28},{28,24},{1,5},{5... | collective-permute-start | bytes 786440 | tf_op jit(solution)/shard_map/ppermute | solution.py:806
  244.0 8.8 %collective-permute-start.42 = (bf16[4,128,256]{2,1,0:T(8,128)(2,1)S(1)}, bf16[4,128,256]{2,1,0:T(8,128)(2,1)S(1)}, u32[]{:S(2)}, u32[]{:S(2)}) collective-permute-start(bf16[4,128,256]{2,1,0:T(8,128)(2,1)S(1)} %pair.1), channel_id=1, source_target_pairs={{0,8},{4,12},{8,16},{12,20},{16,24},{20,28},{1,9},{5,13},{9,17},{1... | collective-permute-start | bytes 786440 | tf_op jit(solution)/shard_map/ppermute | solution.py:24
  253.0 8.9 %collective-permute-start.43 = (bf16[4,128,128]{2,1,0:T(8,128)(2,1)S(1)}, bf16[4,128,128]{2,1,0:T(8,128)(2,1)S(1)}, u32[]{:S(2)}, u32[]{:S(2)}) collective-permute-start(bf16[4,128,128]{2,1,0:T(8,128)(2,1)S(1)} %fusion), channel_id=1, source_target_pairs={{0,16},{4,20},{8,24},{12,28},{1,17},{5,21},{9,25},{13,29},{2,18},{... | collective-permute-start | bytes 393224 | tf_op jit(solution)/shard_map/ppermute | solution.py:24
  261.8 16.5 %collective-permute-start.48 = (bf16[256,2048]{1,0:T(8,128)(2,1)}, bf16[256,2048]{1,0:T(8,128)(2,1)S(1)}, u32[]{:S(2)}, u32[]{:S(2)}) collective-permute-start(bf16[256,2048]{1,0:T(8,128)(2,1)} %collective-permute-done.44.refs_3_), channel_id=1, source_target_pairs={{0,1},{1,0},{2,3},{3,2},{4,5},{5,4},{6,7},{7,6},{8,9},{9,8},{10,11... | collective-permute-start | bytes 3145736 | tf_op jit(solution)/shard_map/ppermute | solution.py:722
  263.4 15.0 %collective-permute-start.47 = (bf16[256,2048]{1,0:T(8,128)(2,1)}, bf16[256,2048]{1,0:T(8,128)(2,1)S(1)}, u32[]{:S(2)}, u32[]{:S(2)}) collective-permute-start(bf16[256,2048]{1,0:T(8,128)(2,1)} %collective-permute-done.41.refs_2_), channel_id=1, source_target_pairs={{0,1},{1,0},{2,3},{3,2},{4,5},{5,4},{6,7},{7,6},{8,9},{9,8},{10,11... | collective-permute-start | bytes 3145736 | tf_op jit(solution)/shard_map/ppermute | solution.py:722
  270.3 5.4 %collective-permute-start.45 = (bf16[128,512]{1,0:T(8,128)(2,1)S(1)}, bf16[128,512]{1,0:T(8,128)(2,1)S(1)}, u32[]{:S(2)}, u32[]{:S(2)}) collective-permute-start(bf16[128,512]{1,0:T(8,128)(2,1)S(1)} %get-tuple-element.123), channel_id=1, source_target_pairs={{0,2},{1,3},{2,0},{3,1},{4,6},{5,7},{6,4},{7,5},{8,10},{9,11},{10,... | collective-permute-start | bytes 393224 | tf_op jit(solution)/shard_map/ppermute | solution.py:722
  271.3 7.1 %collective-permute-start.46 = (bf16[128,512]{1,0:T(8,128)(2,1)S(1)}, bf16[128,512]{1,0:T(8,128)(2,1)S(1)}, u32[]{:S(2)}, u32[]{:S(2)}) collective-permute-start(bf16[128,512]{1,0:T(8,128)(2,1)S(1)} %get-tuple-element.122), channel_id=1, source_target_pairs={{0,3},{1,2},{2,1},{3,0},{4,7},{5,6},{6,5},{7,4},{8,11},{9,10},{10,... | collective-permute-start | bytes 393224 | tf_op jit(solution)/shard_map/ppermute | solution.py:722
  (45 other events, 417.8 us)

commit v4 on v3

--- a/solution.py
+++ b/solution.py
@@ -333,7 +333,7 @@
     across = after(second(ready[last][0]), moving[0])
     total = joined(last, across[0, 0], across[0, 1])
     rising = lifted(total.astype(bf16), -1)
-    far = ready[0][0]
+    far = after(ready[0][0], across)
     diagonal = after(second(far[0, 1]), moving[-1])
     total = joined(0, second(far[0, 0]), diagonal)
     total += moving[-1].astype(f32) + rising.astype(f32)
@@ -766,7 +766,7 @@
         )(head_place.reshape(1), *pieces, *halos, *matrices)
 
     near_raw = project(from_chip(mixer_in, halo), [])
-    far_pieces = from_others(mixer_in, near_raw[0], halos[2])
+    far_pieces = from_others(mixer_in, halos[2])
     far_raw = project(far_pieces, halos)
     rim = far_raw[4]
     key_heads = key_cols // DK

time: 283 us -> 286 us (1.011)
  waiting for transfers between devices: 148 us -> 141 us
  starting transfers between devices: 43.3 us -> 47.8 us
  other arithmetic: 5.77 us -> 9.94 us
    ppermute x33, waiting for transfers between devices: 119 us -> 110 us  [sent(): return lax.ppermute(value, ('ctx', 'head'), pairs)]
    ppermute x14, starting transfers between devices: 10.7 us -> 15.1 us  [crossed(): return lax.ppermute(value, 'head', pairs)]
    unnamed x86 -> x74, local copies, waits for them, and re-layouts: 13.9 us -> 13.9 us
  transfers between devices with their start and end apart: 51 -> 51, of which waited for: 31 -> 33; matrix products, arithmetic and copies ran while one was open for 2% -> 3% of each run, Pallas kernels for 19% -> 19%
where the time goes in v4:
time: 286 us; the launch traced here: 285 us
  waiting for transfers between devices  141 us (49%)
  Pallas kernels  68.1 us (24%)
  starting transfers between devices  47.8 us (17%)
  local copies, waits for them, and re-layouts  15.9 us (6%)
  other arithmetic  9.94 us (3%)
    ppermute x33, waiting for transfers between devices, sent(): return lax.ppermute(value, ('ctx', 'head'), pairs)  110 us
    ppermute x33, starting transfers between devices, sent(): return lax.ppermute(value, ('ctx', 'head'), pairs)  27 us
    pallas_call x2, Pallas kernels, run_experts(): pl.pallas_call(expert_kernel, grid=(local_experts,), in_specs=[row_spec]...  16.4 us
    pallas_call x1, Pallas kernels, on_device(): pl.pallas_call(functools.partial(delta_kernel, key_heads=key_heads, chunk...  16.4 us
    ppermute x14, starting transfers between devices, crossed(): return lax.ppermute(value, 'head', pairs)  15.1 us
    unnamed x74, local copies, waits for them, and re-layouts  13.9 us
    ppermute x3, waiting for transfers between devices, passed_along(): lax.ppermute(value, axis, [(source, source + steps) for source in range(f...  11.7 us
    ppermute x14, waiting for transfers between devices, crossed(): return lax.ppermute(value, 'head', pairs)  11.3 us
  transfers between devices with their start and end apart: 51, of which 33 were waited for; matrix products, arithmetic and copies ran while one was open for 3% of the time, Pallas kernels for 19%

profile of v4, /device:TPU:25, one launch (start us, length us, event | category | flops | bytes accessed | tf_op | source)
XLA Modules:
  0.0 284.7 jit_solution(3069727814069769569)
XLA Ops:
  7.5 9.3 %collective-permute-done.block_10.refs_1_ = bf16[128,2176]{1,0:T(8,128)(2,1)S(1)} collective-permute-done((bf16[128,2176]{1,0:T(8,128)(2,1)S(1)}, bf16[128,2176]{1,0:T(8,128)(2,1)S(1)}, u32[]{:S(2)}, u32[]{:S(2)}) %collective-permute-start) | collective-permute-done | bytes 557088 | tf_op jit(solution)/shard_map/ppermute | solution.py:189
  16.8 3.9 %collective-permute-done.1.block_01.refs_2_ = bf16[128,2176]{1,0:T(8,128)(2,1)S(1)} collective-permute-done((bf16[128,2176]{1,0:T(8,128)(2,1)S(1)}, bf16[128,2176]{1,0:T(8,128)(2,1)S(1)}, u32[]{:S(2)}, u32[]{:S(2)}) %collective-permute-start.1) | collective-permute-done | bytes 557088 | tf_op jit(solution)/shard_map/ppermute | solution.py:189
  22.5 11.1 %collective-permute-done.5.block_10.refs_1_ = bf16[128,2176]{1,0:T(8,128)(2,1)} collective-permute-done((bf16[128,2176]{1,0:T(8,128)(2,1)S(1)}, bf16[128,2176]{1,0:T(8,128)(2,1)}, u32[]{:S(2)}, u32[]{:S(2)}) %collective-permute-start.5) | collective-permute-done | bytes 557088 | tf_op jit(solution)/shard_map/ppermute | solution.py:189
  33.5 2.3 collective-permute-done.4.block_00.refs_0_
  36.7 2.4 collective-permute-start.8
  41.1 9.1 %collective-permute-done.8.block_00.refs_0_ = bf16[128,2176]{1,0:T(8,128)(2,1)} collective-permute-done((bf16[128,2176]{1,0:T(8,128)(2,1)S(1)}, bf16[128,2176]{1,0:T(8,128)(2,1)}, u32[]{:S(2)}, u32[]{:S(2)}) %collective-permute-start.8) | collective-permute-done | bytes 557088 | tf_op jit(solution)/shard_map/ppermute | solution.py:189
  50.2 1.8 collective-permute-done.9.block_10.refs_1_
  55.8 5.0 %collective-permute-done.2.block_11.refs_3_ = bf16[128,2176]{1,0:T(8,128)(2,1)S(1)} collective-permute-done((bf16[128,2176]{1,0:T(8,128)(2,1)S(1)}, bf16[128,2176]{1,0:T(8,128)(2,1)S(1)}, u32[]{:S(2)}, u32[]{:S(2)}) %collective-permute-start.2) | collective-permute-done | bytes 557088 | tf_op jit(solution)/shard_map/ppermute | solution.py:189
  61.9 3.5 %collective-permute-start.14 = (bf16[2,96,2048]{2,1,0:T(8,128)(2,1)S(1)}, bf16[2,96,2048]{2,1,0:T(8,128)(2,1)S(1)}, u32[]{:S(2)}, u32[]{:S(2)}) collective-permute-start(bf16[2,96,2048]{2,1,0:T(8,128)(2,1)S(1)} %get-tuple-element.71), channel_id=1, source_target_pairs={{0,1},{1,0},{2,3},{3,2},{4,5},{5,4},{6,7},{7,6},{8,9},{9,8},{10,11... | collective-permute-start | bytes 2359304 | tf_op jit(solution)/shard_map/ppermute | solution.py:189
  65.4 6.7 %collective-permute-done.7.block_11.refs_3_ = bf16[128,2176]{1,0:T(8,128)(2,1)} collective-permute-done((bf16[128,2176]{1,0:T(8,128)(2,1)}, bf16[128,2176]{1,0:T(8,128)(2,1)}, u32[]{:S(2)}, u32[]{:S(2)}) %collective-permute-start.7) | collective-permute-done | bytes 557088 | tf_op jit(solution)/shard_map/ppermute | solution.py:189
  72.1 2.3 collect.5
  74.7 3.3 %collective-permute-done.12.block_01.refs_2_ = bf16[128,2176]{1,0:T(8,128)(2,1)S(1)} collective-permute-done((bf16[128,2176]{1,0:T(8,128)(2,1)}, bf16[128,2176]{1,0:T(8,128)(2,1)S(1)}, u32[]{:S(2)}, u32[]{:S(2)}) %collective-permute-start.12) | collective-permute-done | bytes 557088 | tf_op jit(solution)/shard_map/ppermute | solution.py:189
  78.0 5.7 %collective-permute-done.13.block_11.refs_3_ = bf16[128,2176]{1,0:T(8,128)(2,1)S(1)} collective-permute-done((bf16[128,2176]{1,0:T(8,128)(2,1)}, bf16[128,2176]{1,0:T(8,128)(2,1)S(1)}, u32[]{:S(2)}, u32[]{:S(2)}) %collective-permute-start.13) | collective-permute-done | bytes 557088 | tf_op jit(solution)/shard_map/ppermute | solution.py:189
  83.8 2.5 collect.6
  86.7 1.9 collective-permute-done.16.refs_5_
  88.6 10.2 %experts.2 = (bf16[2,288,2048]{2,1,0:T(8,128)(2,1)S(1)}, bf16[2,288,2048]{2,1,0:T(8,128)(2,1)S(1)}) custom-call(bf16[2,96,2048]{2,1,0:T(8,128)(2,1)S(1)} %get-tuple-element.62.refs_0_, bf16[2,96,2048]{2,1,0:T(8,128)(2,1)S(1)} %get-tuple-element.65.refs_1_, bf16[2,96,2048]{2,1,0:T(8,128)(2,1)S(1)} %get-tuple-element.70.refs_2_, ...), custom_call_target="tpu_custom_call" | custom-call | flops 14949999616 | bytes 13000000 | tf_op jit(solution)/shard_map/experts/pallas_call | solution.py:264
  99.7 3.8 %collective-permute-done.17.refs_6_ = bf16[2,288,2048]{2,1,0:T(8,128)(2,1)S(1)} collective-permute-done((bf16[2,288,2048]{2,1,0:T(8,128)(2,1)S(1)}, bf16[2,288,2048]{2,1,0:T(8,128)(2,1)S(1)}, u32[]{:S(2)}, u32[]{:S(2)}) %collective-permute-start.17) | collective-permute-done | bytes 2359328 | tf_op jit(solution)/shard_map/ppermute | solution.py:189
  103.5 2.3 spread.5
  106.2 2.3 spread.6
  108.5 2.4 collect.7
  114.1 6.2 %experts.3 = (bf16[2,96,2048]{2,1,0:T(8,128)(2,1)S(1)}, bf16[2,96,2048]{2,1,0:T(8,128)(2,1)S(1)}) custom-call(bf16[2,96,2048]{2,1,0:T(8,128)(2,1)S(1)} %get-tuple-element.81.refs_0_, bf16[2,96,2048]{2,1,0:T(8,128)(2,1)S(1)} %collective-permute-done.19.refs_1_, bf16[2,2048,512]{2,1,0:T(8,128)(2,1)S(1)} %copy-done.2, bf16[2,2048,512]{2,1,0:T(8,128)(2,1)S(1)} %copy-done.3, ...), custom_call_target="tpu_custom_call" | custom-call | flops 1150000000 | bytes 1000000 | tf_op jit(solution)/shard_map/experts/pallas_call | solution.py:264
  122.6 14.0 %collective-permute-done.27 = bf16[1,2,128,2048]{3,2,1,0:T(8,128)(2,1)} collective-permute-done((bf16[1,2,128,2048]{3,2,1,0:T(8,128)(2,1)S(1)}, bf16[1,2,128,2048]{3,2,1,0:T(8,128)(2,1)}, u32[]{:S(2)}, u32[]{:S(2)}) %collective-permute-start.27) | collective-permute-done | bytes 1048608 | tf_op jit(solution)/shard_map/ppermute | solution.py:189
  139.2 2.2 spread.7
  144.7 2.2 collective-permute-done.28
  146.9 8.1 %collective-permute-done.24 = bf16[128,2048]{1,0:T(8,128)(2,1)S(1)} collective-permute-done((bf16[128,2048]{1,0:T(8,128)(2,1)S(1)}, bf16[128,2048]{1,0:T(8,128)(2,1)S(1)}, u32[]{:S(2)}, u32[]{:S(2)}) %collective-permute-start.24) | collective-permute-done | bytes 524320 | tf_op jit(solution)/shard_map/ppermute | solution.py:189
  156.4 1.9 collective-permute-start.29
  161.7 5.7 %collective-permute-done.29 = bf16[128,2048]{1,0:T(8,128)(2,1)S(1)} collective-permute-done((bf16[128,2048]{1,0:T(8,128)(2,1)S(1)}, bf16[128,2048]{1,0:T(8,128)(2,1)S(1)}, u32[]{:S(2)}, u32[]{:S(2)}) %collective-permute-start.29) | collective-permute-done | bytes 524320 | tf_op jit(solution)/shard_map/ppermute | solution.py:189
  167.4 1.9 collective-permute-done.26
  174.6 4.1 %collective-permute-done.25 = bf16[128,2048]{1,0:T(8,128)(2,1)S(1)} collective-permute-done((bf16[128,2048]{1,0:T(8,128)(2,1)S(1)}, bf16[128,2048]{1,0:T(8,128)(2,1)S(1)}, u32[]{:S(2)}, u32[]{:S(2)}) %collective-permute-start.25) | collective-permute-done | bytes 524320 | tf_op jit(solution)/shard_map/ppermute | solution.py:189
  178.7 4.8 %collective-permute-done.30 = bf16[128,2048]{1,0:T(8,128)(2,1)S(1)} collective-permute-done((bf16[128,2048]{1,0:T(8,128)(2,1)S(1)}, bf16[128,2048]{1,0:T(8,128)(2,1)S(1)}, u32[]{:S(2)}, u32[]{:S(2)}) %collective-permute-start.30) | collective-permute-done | bytes 524320 | tf_op jit(solution)/shard_map/ppermute | solution.py:189
  185.7 5.2 %collective-permute-start.34 = (bf16[128,2048]{1,0:T(8,128)(2,1)S(1)}, bf16[128,2048]{1,0:T(8,128)(2,1)}, u32[]{:S(2)}, u32[]{:S(2)}) collective-permute-start(bf16[128,2048]{1,0:T(8,128)(2,1)S(1)} %multiply_convert_fusion.refs_0_), channel_id=1, source_target_pairs={{0,1},{1,0},{2,3},{3,2},{4,5},{5,4},{6,7},{7,6},{8,9},{9,8},{10,11... | collective-permute-start | bytes 1572872 | tf_op jit(solution)/shard_map/ppermute | solution.py:722
  190.9 3.0 %collective-permute-start.33 = (bf16[16,2048]{1,0:T(8,128)(2,1)S(1)}, bf16[16,2048]{1,0:T(8,128)(2,1)S(1)}, u32[]{:S(2)}, u32[]{:S(2)}) collective-permute-start(bf16[16,2048]{1,0:T(8,128)(2,1)S(1)} %slice.76), channel_id=1, source_target_pairs={{0,4},{4,8},{8,12},{12,16},{16,20},{20,24},{24,28},{1,5},{5,9},{9,... | collective-permute-start | bytes 196616 | tf_op jit(solution)/shard_map/ppermute | solution.py:24
  195.3 2.1 collective-permute-done.33.refs_2_
  198.3 2.2 collective-permute-done.36.refs_4_
  200.5 1.9 collective-permute-start.37
  204.1 1.6 copy-done.18
  209.8 3.6 %project.2 = (bf16[256,1024]{1,0:T(8,128)(2,1)S(1)}, bf16[256,512]{1,0:T(8,128)(2,1)S(1)}, f32[256,4]{1,0:T(8,128)S(1)}, f32[256,4]{1,0:T(8,128)S(1)}) custom-call(s32[1]{0:T(128)} %bitcast.17.place_ref, bf16[128,2048]{1,0:T(8,128)(2,1)S(1)} %multiply_convert_fusion.refs_0_, bf16[128,2048]{1,0:T(8,128)(2,1)} %collective-permute-done.34.refs_1_, ...), custom_call_target="tpu_custom_call" | custom-call | flops 4600000000 | bytes 4000000 | tf_op jit(solution)/shard_map/project/pallas_call | solution.py:759
  215.0 3.5 %project.3 = (bf16[256,1024]{1,0:T(8,128)(2,1)S(1)}, bf16[256,512]{1,0:T(8,128)(2,1)S(1)}, f32[256,4]{1,0:T(8,128)S(1)}, f32[256,4]{1,0:T(8,128)S(1)}, f32[16,1024]{1,0:T(8,128)S(1)}) custom-call(s32[1]{0:T(128)} %bitcast.17.place_ref, bf16[128,2048]{1,0:T(8,128)(2,1)} %collective-permute-done.35.refs_0_, ...), custom_call_target="tpu_custom_call" | custom-call | flops 4600000000 | bytes 4000000 | tf_op jit(solution)/shard_map/project/pallas_call | solution.py:759
  218.5 16.4 %delta.1 = (f32[512,512]{1,0:T(8,128)S(1)}, f32[512,512]{1,0:T(8,128)S(1)}, bf16[4,128,256]{2,1,0:T(8,128)(2,1)}) custom-call(s32[1]{0:T(128)} %bitcast.17.place_ref, bf16[256,1024]{1,0:T(8,128)(2,1)S(1)} %get-tuple-element.98.near_raw, bf16[256,1024]{1,0:T(8,128)(2,1)S(1)} %get-tuple-element.100.far_raw, f32[256,4]{1,0:T(8,128)S(1)} %get-tuple-element.101.near_beta, ...), custom_call_target="tpu_custom_call" | custom-call | flops 18400000000 | bytes 16000000 | tf_op jit(solution)/shard_map/delta/pallas_call | solution.py:776
  236.9 7.8 %collective-permute-done.40.other_ref = bf16[4,128,256]{2,1,0:T(8,128)(2,1)S(1)} collective-permute-done((bf16[4,128,256]{2,1,0:T(8,128)(2,1)}, bf16[4,128,256]{2,1,0:T(8,128)(2,1)S(1)}, u32[]{:S(2)}, u32[]{:S(2)}) %collective-permute-start.40) | collective-permute-done | bytes 262176 | tf_op jit(solution)/shard_map/ppermute | solution.py:806
  247.2 7.3 %collective-permute-done.42.near_pairs_ref = bf16[4,128,256]{2,1,0:T(8,128)(2,1)S(1)} collective-permute-done((bf16[4,128,256]{2,1,0:T(8,128)(2,1)S(1)}, bf16[4,128,256]{2,1,0:T(8,128)(2,1)S(1)}, u32[]{:S(2)}, u32[]{:S(2)}) %collective-permute-start.42) | collective-permute-done | bytes 262176 | tf_op jit(solution)/shard_map/ppermute | solution.py:24
  256.0 5.6 %collective-permute-done.44.refs_3_ = bf16[256,2048]{1,0:T(8,128)(2,1)} collective-permute-done((bf16[256,2048]{1,0:T(8,128)(2,1)}, bf16[256,2048]{1,0:T(8,128)(2,1)}, u32[]{:S(2)}, u32[]{:S(2)}) %collective-permute-start.44) | collective-permute-done | bytes 1048608 | tf_op jit(solution)/shard_map/ppermute | solution.py:722
  261.6 2.3 collective-permute-done.43.far_pairs_ref
  264.0 1.6 collective-permute-start.48
  268.8 3.1 %finish.1 = bf16[512,512]{1,0:T(8,128)(2,1)S(1)} custom-call(s32[2]{0:T(128)S(1)} %pad_add_fusion.where_ref, bf16[4,128,256]{2,1,0:T(8,128)(2,1)S(1)} %collective-permute-done.42.near_pairs_ref, bf16[4,128,128]{2,1,0:T(8,128)(2,1)S(1)} %collective-permute-done.43.far_pairs_ref, bf16[4,128,256]{2,1,0:T(8,128)(2,1)S(1)} %collective-permute-done.40.other_ref, ...), custom_call_target="tpu_custom_call" | custom-call | tf_op jit(solution)/shard_map/finish/pallas_call | solution.py:841
  274.3 3.2 %output.2.refs_6_ = f32[128,2048]{1,0:T(8,128)S(1)} custom-call(bf16[128,512]{1,0:T(8,128)(2,1)S(1)} %get-tuple-element.123.refs_0_, bf16[128,512]{1,0:T(8,128)(2,1)S(1)} %collective-permute-done.49.refs_1_, bf16[512,2048]{1,0:T(8,128)(2,1)S(1)} %copy-done.4, bf16[512,2048]{1,0:T(8,128)(2,1)} %collective-permute-done.50.refs_3_), custom_call_target="tpu_custom_call" | custom-call | flops 3449999872 | bytes 3000000 | tf_op jit(solution)/shard_map/output/pallas_call | solution.py:882
  277.6 3.0 %collective-permute-done.46.refs_1_ = bf16[128,512]{1,0:T(8,128)(2,1)S(1)} collective-permute-done((bf16[128,512]{1,0:T(8,128)(2,1)S(1)}, bf16[128,512]{1,0:T(8,128)(2,1)S(1)}, u32[]{:S(2)}, u32[]{:S(2)}) %collective-permute-start.46) | collective-permute-done | bytes 131104 | tf_op jit(solution)/shard_map/ppermute | solution.py:722
  280.6 4.1 %output.3 = bf16[128,2048]{1,0:T(8,128)(2,1)} custom-call(bf16[128,512]{1,0:T(8,128)(2,1)S(1)} %collective-permute-done.45.refs_0_, bf16[128,512]{1,0:T(8,128)(2,1)S(1)} %collective-permute-done.46.refs_1_, bf16[256,2048]{1,0:T(8,128)(2,1)} %collective-permute-done.41.refs_2_, bf16[256,2048]{1,0:T(8,128)(2,1)} %collective-permute-done.44.refs_3_, ...), custom_call_target="tpu_custom_call" | custom-call | flops 3449999872 | bytes 3000000 | tf_op jit(solution)/shard_map/output/pallas_call | solution.py:882
  (176 shorter events, 63.2 us)
Async XLA Ops:
  4.8 12.0 %collective-permute-start = (bf16[128,2176]{1,0:T(8,128)(2,1)S(1)}, bf16[128,2176]{1,0:T(8,128)(2,1)S(1)}, u32[]{:S(2)}, u32[]{:S(2)}) collective-permute-start(bf16[128,2176]{1,0:T(8,128)(2,1)S(1)} %concatenate.6.block_00.refs_0_), channel_id=1, source_target_pairs={{0,4},{1,3},{2,6},{3,1},{4,0},{5,7},{6,2},{7,5},{8,12},{9,11},{10,... | collective-permute-start | bytes 1671176 | tf_op jit(solution)/shard_map/ppermute | solution.py:189
  6.1 14.6 %collective-permute-start.1 = (bf16[128,2176]{1,0:T(8,128)(2,1)S(1)}, bf16[128,2176]{1,0:T(8,128)(2,1)S(1)}, u32[]{:S(2)}, u32[]{:S(2)}) collective-permute-start(bf16[128,2176]{1,0:T(8,128)(2,1)S(1)} %concatenate.6.block_00.refs_0_), channel_id=1, source_target_pairs={{0,2},{1,5},{2,0},{3,7},{4,6},{5,1},{6,4},{7,3},{8,10},{9,13},{10,... | collective-permute-start | bytes 1671176 | tf_op jit(solution)/shard_map/ppermute | solution.py:189
  7.3 14.7 %collective-permute-start.3 = (bf16[128,2176]{1,0:T(8,128)(2,1)S(1)}, bf16[128,2176]{1,0:T(8,128)(2,1)S(1)}, u32[]{:S(2)}, u32[]{:S(2)}) collective-permute-start(bf16[128,2176]{1,0:T(8,128)(2,1)S(1)} %concatenate.6.block_00.refs_0_), channel_id=1, source_target_pairs={{0,24},{1,25},{2,26},{3,27},{4,28},{5,29},{6,30},{7,31},{8,0},{9,1... | collective-permute-start | bytes 1671176 | tf_op jit(solution)/shard_map/ppermute | solution.py:189
  22.0 11.5 %collective-permute-start.5 = (bf16[128,2176]{1,0:T(8,128)(2,1)S(1)}, bf16[128,2176]{1,0:T(8,128)(2,1)}, u32[]{:S(2)}, u32[]{:S(2)}) collective-permute-start(bf16[128,2176]{1,0:T(8,128)(2,1)S(1)} %collective-permute-done.3.block_00.refs_0_), channel_id=1, source_target_pairs={{0,4},{1,3},{2,6},{3,1},{4,0},{5,7},{6,2},{7,5},{8,12},{9,11},{10,... | collective-permute-start | bytes 1671176 | tf_op jit(solution)/shard_map/ppermute | solution.py:189
  22.2 13.6 %collective-permute-start.4 = (bf16[128,2176]{1,0:T(8,128)(2,1)S(1)}, bf16[128,2176]{1,0:T(8,128)(2,1)}, u32[]{:S(2)}, u32[]{:S(2)}) collective-permute-start(bf16[128,2176]{1,0:T(8,128)(2,1)S(1)} %collective-permute-done.3.block_00.refs_0_), channel_id=1, source_target_pairs={{0,24},{1,25},{2,26},{3,27},{4,28},{5,29},{6,30},{7,31},{8,0},{9,1... | collective-permute-start | bytes 1671176 | tf_op jit(solution)/shard_map/ppermute | solution.py:189
  22.3 13.6 %collective-permute-start.6 = (bf16[128,2176]{1,0:T(8,128)(2,1)S(1)}, bf16[128,2176]{1,0:T(8,128)(2,1)S(1)}, u32[]{:S(2)}, u32[]{:S(2)}) collective-permute-start(bf16[128,2176]{1,0:T(8,128)(2,1)S(1)} %collective-permute-done.3.block_00.refs_0_), channel_id=1, source_target_pairs={{0,2},{1,5},{2,0},{3,7},{4,6},{5,1},{6,4},{7,3},{8,10},{9,13},{10,... | collective-permute-start | bytes 1671176 | tf_op jit(solution)/shard_map/ppermute | solution.py:189
  36.7 13.5 %collective-permute-start.8 = (bf16[128,2176]{1,0:T(8,128)(2,1)S(1)}, bf16[128,2176]{1,0:T(8,128)(2,1)}, u32[]{:S(2)}, u32[]{:S(2)}) collective-permute-start(bf16[128,2176]{1,0:T(8,128)(2,1)S(1)} %concatenate.6.block_00.refs_0_), channel_id=1, source_target_pairs={{0,8},{1,9},{2,10},{3,11},{4,12},{5,13},{6,14},{7,15},{8,16},{9,17... | collective-permute-start | bytes 1671176 | tf_op jit(solution)/shard_map/ppermute | solution.py:189
  39.1 12.9 %collective-permute-start.9 = (bf16[128,2176]{1,0:T(8,128)(2,1)}, bf16[128,2176]{1,0:T(8,128)(2,1)}, u32[]{:S(2)}, u32[]{:S(2)}) collective-permute-start(bf16[128,2176]{1,0:T(8,128)(2,1)} %collective-permute-done.4.block_00.refs_0_), channel_id=1, source_target_pairs={{0,4},{1,3},{2,6},{3,1},{4,0},{5,7},{6,2},{7,5},{8,12},{9,11},{10,... | collective-permute-start | bytes 1671176 | tf_op jit(solution)/shard_map/ppermute | solution.py:189
  39.3 13.6 %collective-permute-start.10 = (bf16[128,2176]{1,0:T(8,128)(2,1)}, bf16[128,2176]{1,0:T(8,128)(2,1)}, u32[]{:S(2)}, u32[]{:S(2)}) collective-permute-start(bf16[128,2176]{1,0:T(8,128)(2,1)} %collective-permute-done.4.block_00.refs_0_), channel_id=1, source_target_pairs={{0,2},{1,5},{2,0},{3,7},{4,6},{5,1},{6,4},{7,3},{8,10},{9,13},{10,... | collective-permute-start | bytes 1671176 | tf_op jit(solution)/shard_map/ppermute | solution.py:189
  39.7 21.2 %collective-permute-start.2 = (bf16[128,2176]{1,0:T(8,128)(2,1)S(1)}, bf16[128,2176]{1,0:T(8,128)(2,1)S(1)}, u32[]{:S(2)}, u32[]{:S(2)}) collective-permute-start(bf16[128,2176]{1,0:T(8,128)(2,1)S(1)} %collective-permute-done.block_10.refs_1_), channel_id=1, source_target_pairs={{0,2},{1,5},{2,0},{3,7},{4,6},{5,1},{6,4},{7,3},{8,10},{9,13},{10,... | collective-permute-start | bytes 1671176 | tf_op jit(solution)/shard_map/ppermute | solution.py:189
  40.8 31.3 %collective-permute-start.7 = (bf16[128,2176]{1,0:T(8,128)(2,1)}, bf16[128,2176]{1,0:T(8,128)(2,1)}, u32[]{:S(2)}, u32[]{:S(2)}) collective-permute-start(bf16[128,2176]{1,0:T(8,128)(2,1)} %collective-permute-done.5.block_10.refs_1_), channel_id=1, source_target_pairs={{0,2},{1,5},{2,0},{3,7},{4,6},{5,1},{6,4},{7,3},{8,10},{9,13},{10,... | collective-permute-start | bytes 1671176 | tf_op jit(solution)/shard_map/ppermute | solution.py:189
  53.0 21.8 %collective-permute-start.11 = (bf16[128,2176]{1,0:T(8,128)(2,1)}, bf16[128,2176]{1,0:T(8,128)(2,1)S(1)}, u32[]{:S(2)}, u32[]{:S(2)}) collective-permute-start(bf16[128,2176]{1,0:T(8,128)(2,1)} %collective-permute-done.8.block_00.refs_0_), channel_id=1, source_target_pairs={{0,4},{1,3},{2,6},{3,1},{4,0},{5,7},{6,2},{7,5},{8,12},{9,11},{10,... | collective-permute-start | bytes 1671176 | tf_op jit(solution)/shard_map/ppermute | solution.py:189
  54.3 23.8 %collective-permute-start.12 = (bf16[128,2176]{1,0:T(8,128)(2,1)}, bf16[128,2176]{1,0:T(8,128)(2,1)S(1)}, u32[]{:S(2)}, u32[]{:S(2)}) collective-permute-start(bf16[128,2176]{1,0:T(8,128)(2,1)} %collective-permute-done.8.block_00.refs_0_), channel_id=1, source_target_pairs={{0,2},{1,5},{2,0},{3,7},{4,6},{5,1},{6,4},{7,3},{8,10},{9,13},{10,... | collective-permute-start | bytes 1671176 | tf_op jit(solution)/shard_map/ppermute | solution.py:189
  54.8 29.0 %collective-permute-start.13 = (bf16[128,2176]{1,0:T(8,128)(2,1)}, bf16[128,2176]{1,0:T(8,128)(2,1)S(1)}, u32[]{:S(2)}, u32[]{:S(2)}) collective-permute-start(bf16[128,2176]{1,0:T(8,128)(2,1)} %collective-permute-done.9.block_10.refs_1_), channel_id=1, source_target_pairs={{0,2},{1,5},{2,0},{3,7},{4,6},{5,1},{6,4},{7,3},{8,10},{9,13},{10,... | collective-permute-start | bytes 1671176 | tf_op jit(solution)/shard_map/ppermute | solution.py:189
  61.9 24.8 %collective-permute-start.14 = (bf16[2,96,2048]{2,1,0:T(8,128)(2,1)S(1)}, bf16[2,96,2048]{2,1,0:T(8,128)(2,1)S(1)}, u32[]{:S(2)}, u32[]{:S(2)}) collective-permute-start(bf16[2,96,2048]{2,1,0:T(8,128)(2,1)S(1)} %get-tuple-element.71), channel_id=1, source_target_pairs={{0,1},{1,0},{2,3},{3,2},{4,5},{5,4},{6,7},{7,6},{8,9},{9,8},{10,11... | collective-permute-start | bytes 2359304 | tf_op jit(solution)/shard_map/ppermute | solution.py:189
  74.4 12.3 %collective-permute-start.15 = (bf16[2,96,2048]{2,1,0:T(8,128)(2,1)S(1)}, bf16[2,96,2048]{2,1,0:T(8,128)(2,1)S(1)}, u32[]{:S(2)}, u32[]{:S(2)}) collective-permute-start(bf16[2,96,2048]{2,1,0:T(8,128)(2,1)S(1)} %get-tuple-element.72), channel_id=1, source_target_pairs={{0,1},{1,0},{2,3},{3,2},{4,5},{5,4},{6,7},{7,6},{8,9},{9,8},{10,11... | collective-permute-start | bytes 2359304 | tf_op jit(solution)/shard_map/ppermute | solution.py:189
  98.9 4.6 %collective-permute-start.17 = (bf16[2,288,2048]{2,1,0:T(8,128)(2,1)S(1)}, bf16[2,288,2048]{2,1,0:T(8,128)(2,1)S(1)}, u32[]{:S(2)}, u32[]{:S(2)}) collective-permute-start(bf16[2,288,2048]{2,1,0:T(8,128)(2,1)S(1)} %get-tuple-element.75), channel_id=1, source_target_pairs={{0,1},{1,0},{2,3},{3,2},{4,5},{5,4},{6,7},{7,6},{8,9},{9,8},{10,11... | collective-permute-start | bytes 7077896 | tf_op jit(solution)/shard_map/ppermute | solution.py:189
  99.3 9.2 %collective-permute-start.18 = (bf16[128,2176]{1,0:T(8,128)(2,1)S(1)}, bf16[128,2176]{1,0:T(8,128)(2,1)S(1)}, u32[]{:S(2)}, u32[]{:S(2)}) collective-permute-start(bf16[128,2176]{1,0:T(8,128)(2,1)S(1)} %collective-permute-done.11.block_10.refs_1_), channel_id=1, source_target_pairs={{0,2},{1,5},{2,0},{3,7},{4,6},{5,1},{6,4},{7,3},{8,10},{9,13},{10,... | collective-permute-start | bytes 1671176 | tf_op jit(solution)/shard_map/ppermute | solution.py:189
  105.8 15.0 %collective-permute-start.22 = (bf16[1,2,128,2048]{3,2,1,0:T(8,128)(2,1)S(1)}, bf16[1,2,128,2048]{3,2,1,0:T(8,128)(2,1)}, u32[]{:S(2)}, u32[]{:S(2)}) collective-permute-start(bf16[1,2,128,2048]{3,2,1,0:T(8,128)(2,1)S(1)} %get-tuple-element.78), channel_id=1, source_target_pairs={{0,2},{1,5},{2,0},{3,7},{4,6},{5,1},{6,4},{7,3},{8,10},{9,13},{10,... | collective-permute-start | bytes 3145736 | tf_op jit(solution)/shard_map/ppermute | solution.py:189
  110.9 3.2 %collective-permute-start.19 = (bf16[2,96,2048]{2,1,0:T(8,128)(2,1)S(1)}, bf16[2,96,2048]{2,1,0:T(8,128)(2,1)S(1)}, u32[]{:S(2)}, u32[]{:S(2)}) collective-permute-start(bf16[2,96,2048]{2,1,0:T(8,128)(2,1)S(1)} %get-tuple-element.82), channel_id=1, source_target_pairs={{0,1},{1,0},{2,3},{3,2},{4,5},{5,4},{6,7},{7,6},{8,9},{9,8},{10,11... | collective-permute-start | bytes 2359304 | tf_op jit(solution)/shard_map/ppermute | solution.py:189
  112.2 24.4 %collective-permute-start.27 = (bf16[1,2,128,2048]{3,2,1,0:T(8,128)(2,1)S(1)}, bf16[1,2,128,2048]{3,2,1,0:T(8,128)(2,1)}, u32[]{:S(2)}, u32[]{:S(2)}) collective-permute-start(bf16[1,2,128,2048]{3,2,1,0:T(8,128)(2,1)S(1)} %get-tuple-element.79), channel_id=1, source_target_pairs={{0,2},{1,5},{2,0},{3,7},{4,6},{5,1},{6,4},{7,3},{8,10},{9,13},{10,... | collective-permute-start | bytes 3145736 | tf_op jit(solution)/shard_map/ppermute | solution.py:189
  120.3 18.8 %collective-permute-start.20 = (bf16[2,96,2048]{2,1,0:T(8,128)(2,1)S(1)}, bf16[2,96,2048]{2,1,0:T(8,128)(2,1)S(1)}, u32[]{:S(2)}, u32[]{:S(2)}) collective-permute-start(bf16[2,96,2048]{2,1,0:T(8,128)(2,1)S(1)} %get-tuple-element.84), channel_id=1, source_target_pairs={{0,1},{1,0},{2,3},{3,2},{4,5},{5,4},{6,7},{7,6},{8,9},{9,8},{10,11... | collective-permute-start | bytes 2359304 | tf_op jit(solution)/shard_map/ppermute | solution.py:189
  122.0 19.9 %collective-permute-start.23 = (bf16[128,2048]{1,0:T(8,128)(2,1)S(1)}, bf16[128,2048]{1,0:T(8,128)(2,1)S(1)}, u32[]{:S(2)}, u32[]{:S(2)}) collective-permute-start(bf16[128,2048]{1,0:T(8,128)(2,1)S(1)} %fusion.13), channel_id=1, source_target_pairs={{0,4},{1,3},{2,6},{3,1},{4,0},{5,7},{6,2},{7,5},{8,12},{9,11},{10,... | collective-permute-start | bytes 1572872 | tf_op jit(solution)/shard_map/ppermute | solution.py:189
  137.8 9.1 %collective-permute-start.28 = (bf16[128,2048]{1,0:T(8,128)(2,1)S(1)}, bf16[128,2048]{1,0:T(8,128)(2,1)S(1)}, u32[]{:S(2)}, u32[]{:S(2)}) collective-permute-start(bf16[128,2048]{1,0:T(8,128)(2,1)S(1)} %fusion.8), channel_id=1, source_target_pairs={{0,4},{1,3},{2,6},{3,1},{4,0},{5,7},{6,2},{7,5},{8,12},{9,11},{10,... | collective-permute-start | bytes 1572872 | tf_op jit(solution)/shard_map/ppermute | solution.py:189
  141.4 17.5 %collective-permute-start.21 = (bf16[1,2,128,2048]{3,2,1,0:T(8,128)(2,1)S(1)}, bf16[1,2,128,2048]{3,2,1,0:T(8,128)(2,1)S(1)}, u32[]{:S(2)}, u32[]{:S(2)}) collective-permute-start(bf16[1,2,128,2048]{3,2,1,0:T(8,128)(2,1)S(1)} %get-tuple-element.85), channel_id=1, source_target_pairs={{0,2},{1,5},{2,0},{3,7},{4,6},{5,1},{6,4},{7,3},{8,10},{9,13},{10,... | collective-permute-start | bytes 3145736 | tf_op jit(solution)/shard_map/ppermute | solution.py:189
  143.1 11.9 %collective-permute-start.24 = (bf16[128,2048]{1,0:T(8,128)(2,1)S(1)}, bf16[128,2048]{1,0:T(8,128)(2,1)S(1)}, u32[]{:S(2)}, u32[]{:S(2)}) collective-permute-start(bf16[128,2048]{1,0:T(8,128)(2,1)S(1)} %fusion.15), channel_id=1, source_target_pairs={{0,8},{1,9},{2,10},{3,11},{4,12},{5,13},{6,14},{7,15},{8,16},{9,17... | collective-permute-start | bytes 1572872 | tf_op jit(solution)/shard_map/ppermute | solution.py:189
  156.4 11.0 %collective-permute-start.29 = (bf16[128,2048]{1,0:T(8,128)(2,1)S(1)}, bf16[128,2048]{1,0:T(8,128)(2,1)S(1)}, u32[]{:S(2)}, u32[]{:S(2)}) collective-permute-start(bf16[128,2048]{1,0:T(8,128)(2,1)S(1)} %fusion.11), channel_id=1, source_target_pairs={{0,8},{1,9},{2,10},{3,11},{4,12},{5,13},{6,14},{7,15},{8,16},{9,17... | collective-permute-start | bytes 1572872 | tf_op jit(solution)/shard_map/ppermute | solution.py:189
  159.1 10.2 %collective-permute-start.26 = (bf16[128,2048]{1,0:T(8,128)(2,1)S(1)}, bf16[128,2048]{1,0:T(8,128)(2,1)S(1)}, u32[]{:S(2)}, u32[]{:S(2)}) collective-permute-start(bf16[128,2048]{1,0:T(8,128)(2,1)S(1)} %get-tuple-element.121), channel_id=1, source_target_pairs={{0,2},{1,5},{2,0},{3,7},{4,6},{5,1},{6,4},{7,3},{8,10},{9,13},{10,... | collective-permute-start | bytes 1572872 | tf_op jit(solution)/shard_map/ppermute | solution.py:189
  159.7 12.1 %collective-permute-start.31 = (bf16[128,2048]{1,0:T(8,128)(2,1)S(1)}, bf16[128,2048]{1,0:T(8,128)(2,1)S(1)}, u32[]{:S(2)}, u32[]{:S(2)}) collective-permute-start(bf16[128,2048]{1,0:T(8,128)(2,1)S(1)} %fusion.5), channel_id=1, source_target_pairs={{0,4},{1,3},{2,6},{3,1},{4,0},{5,7},{6,2},{7,5},{8,12},{9,11},{10,... | collective-permute-start | bytes 1572872 | tf_op jit(solution)/shard_map/ppermute | solution.py:189
  160.6 18.1 %collective-permute-start.25 = (bf16[128,2048]{1,0:T(8,128)(2,1)S(1)}, bf16[128,2048]{1,0:T(8,128)(2,1)S(1)}, u32[]{:S(2)}, u32[]{:S(2)}) collective-permute-start(bf16[128,2048]{1,0:T(8,128)(2,1)S(1)} %get-tuple-element.120), channel_id=1, source_target_pairs={{0,2},{1,5},{2,0},{3,7},{4,6},{5,1},{6,4},{7,3},{8,10},{9,13},{10,... | collective-permute-start | bytes 1572872 | tf_op jit(solution)/shard_map/ppermute | solution.py:189
  169.4 14.1 %collective-permute-start.30 = (bf16[128,2048]{1,0:T(8,128)(2,1)S(1)}, bf16[128,2048]{1,0:T(8,128)(2,1)S(1)}, u32[]{:S(2)}, u32[]{:S(2)}) collective-permute-start(bf16[128,2048]{1,0:T(8,128)(2,1)S(1)} %fusion.12), channel_id=1, source_target_pairs={{0,4},{1,3},{2,6},{3,1},{4,0},{5,7},{6,2},{7,5},{8,12},{9,11},{10,... | collective-permute-start | bytes 1572872 | tf_op jit(solution)/shard_map/ppermute | solution.py:189
  172.1 11.4 %collective-permute-start.32 = (bf16[128,2048]{1,0:T(8,128)(2,1)S(1)}, bf16[128,2048]{1,0:T(8,128)(2,1)S(1)}, u32[]{:S(2)}, u32[]{:S(2)}) collective-permute-start(bf16[128,2048]{1,0:T(8,128)(2,1)S(1)} %fusion.7), channel_id=1, source_target_pairs={{0,24},{1,25},{2,26},{3,27},{4,28},{5,29},{6,30},{7,31},{8,0},{9,1... | collective-permute-start | bytes 1572872 | tf_op jit(solution)/shard_map/ppermute | solution.py:189
  184.5 16.0 %collective-permute-start.35 = (bf16[128,2048]{1,0:T(8,128)(2,1)S(1)}, bf16[128,2048]{1,0:T(8,128)(2,1)}, u32[]{:S(2)}, u32[]{:S(2)}) collective-permute-start(bf16[128,2048]{1,0:T(8,128)(2,1)S(1)} %multiply_convert_fusion.refs_0_), channel_id=1, source_target_pairs={{0,2},{1,3},{2,0},{3,1},{4,6},{5,7},{6,4},{7,5},{8,10},{9,11},{10,... | collective-permute-start | bytes 1572872 | tf_op jit(solution)/shard_map/ppermute | solution.py:722
  185.7 17.4 %collective-permute-start.34 = (bf16[128,2048]{1,0:T(8,128)(2,1)S(1)}, bf16[128,2048]{1,0:T(8,128)(2,1)}, u32[]{:S(2)}, u32[]{:S(2)}) collective-permute-start(bf16[128,2048]{1,0:T(8,128)(2,1)S(1)} %multiply_convert_fusion.refs_0_), channel_id=1, source_target_pairs={{0,1},{1,0},{2,3},{3,2},{4,5},{5,4},{6,7},{7,6},{8,9},{9,8},{10,11... | collective-permute-start | bytes 1572872 | tf_op jit(solution)/shard_map/ppermute | solution.py:722
  190.9 6.5 %collective-permute-start.33 = (bf16[16,2048]{1,0:T(8,128)(2,1)S(1)}, bf16[16,2048]{1,0:T(8,128)(2,1)S(1)}, u32[]{:S(2)}, u32[]{:S(2)}) collective-permute-start(bf16[16,2048]{1,0:T(8,128)(2,1)S(1)} %slice.76), channel_id=1, source_target_pairs={{0,4},{4,8},{8,12},{12,16},{16,20},{20,24},{24,28},{1,5},{5,9},{9,... | collective-permute-start | bytes 196616 | tf_op jit(solution)/shard_map/ppermute | solution.py:24
  200.5 13.5 %collective-permute-start.37 = (bf16[128,2048]{1,0:T(8,128)(2,1)}, bf16[128,2048]{1,0:T(8,128)(2,1)S(1)}, u32[]{:S(2)}, u32[]{:S(2)}) collective-permute-start(bf16[128,2048]{1,0:T(8,128)(2,1)} %collective-permute-done.35.refs_0_), channel_id=1, source_target_pairs={{0,1},{1,0},{2,3},{3,2},{4,5},{5,4},{6,7},{7,6},{8,9},{9,8},{10,11... | collective-permute-start | bytes 1572872 | tf_op jit(solution)/shard_map/ppermute | solution.py:722
  202.5 12.5 %collective-permute-start.38 = (bf16[16,2048]{1,0:T(8,128)(2,1)S(1)}, bf16[16,2048]{1,0:T(8,128)(2,1)S(1)}, u32[]{:S(2)}, u32[]{:S(2)}) collective-permute-start(bf16[16,2048]{1,0:T(8,128)(2,1)S(1)} %collective-permute-done.33.refs_2_), channel_id=1, source_target_pairs={{0,1},{1,0},{2,3},{3,2},{4,5},{5,4},{6,7},{7,6},{8,9},{9,8},{10,11... | collective-permute-start | bytes 196616 | tf_op jit(solution)/shard_map/ppermute | solution.py:722
  202.6 12.4 %collective-permute-start.39 = (bf16[16,2048]{1,0:T(8,128)(2,1)S(1)}, bf16[16,2048]{1,0:T(8,128)(2,1)S(1)}, u32[]{:S(2)}, u32[]{:S(2)}) collective-permute-start(bf16[16,2048]{1,0:T(8,128)(2,1)S(1)} %collective-permute-done.36.refs_4_), channel_id=1, source_target_pairs={{0,1},{1,0},{2,3},{3,2},{4,5},{5,4},{6,7},{7,6},{8,9},{9,8},{10,11... | collective-permute-start | bytes 196616 | tf_op jit(solution)/shard_map/ppermute | solution.py:722
  214.1 30.7 %collective-permute-start.41 = (bf16[256,2048]{1,0:T(8,128)(2,1)}, bf16[256,2048]{1,0:T(8,128)(2,1)}, u32[]{:S(2)}, u32[]{:S(2)}) collective-permute-start(bf16[256,2048]{1,0:T(8,128)(2,1)} %get-tuple-element.107), channel_id=1, source_target_pairs={{0,2},{1,3},{2,0},{3,1},{4,6},{5,7},{6,4},{7,5},{8,10},{9,11},{10,... | collective-permute-start | bytes 3145736 | tf_op jit(solution)/shard_map/ppermute | solution.py:722
  236.0 38.3 %collective-permute-start.50 = (bf16[512,2048]{1,0:T(8,128)(2,1)S(1)}, bf16[512,2048]{1,0:T(8,128)(2,1)}, u32[]{:S(2)}, u32[]{:S(2)}) collective-permute-start(bf16[512,2048]{1,0:T(8,128)(2,1)S(1)} %copy-done.4), channel_id=1, source_target_pairs={{0,1},{1,0},{2,3},{3,2},{4,5},{5,4},{6,7},{7,6},{8,9},{9,8},{10,11... | collective-permute-start | bytes 6291464 | tf_op jit(solution)/shard_map/ppermute | solution.py:722
  236.4 25.3 %collective-permute-start.44 = (bf16[256,2048]{1,0:T(8,128)(2,1)}, bf16[256,2048]{1,0:T(8,128)(2,1)}, u32[]{:S(2)}, u32[]{:S(2)}) collective-permute-start(bf16[256,2048]{1,0:T(8,128)(2,1)} %get-tuple-element.109), channel_id=1, source_target_pairs={{0,2},{1,3},{2,0},{3,1},{4,6},{5,7},{6,4},{7,5},{8,10},{9,11},{10,... | collective-permute-start | bytes 3145736 | tf_op jit(solution)/shard_map/ppermute | solution.py:722
  236.9 7.8 %collective-permute-start.40 = (bf16[4,128,256]{2,1,0:T(8,128)(2,1)}, bf16[4,128,256]{2,1,0:T(8,128)(2,1)S(1)}, u32[]{:S(2)}, u32[]{:S(2)}) collective-permute-start(bf16[4,128,256]{2,1,0:T(8,128)(2,1)} %get-tuple-element.106.mine_ref), channel_id=1, source_target_pairs={{0,4},{4,0},{8,12},{12,8},{16,20},{20,16},{24,28},{28,24},{1,5},{5... | collective-permute-start | bytes 786440 | tf_op jit(solution)/shard_map/ppermute | solution.py:806
  245.9 8.6 %collective-permute-start.42 = (bf16[4,128,256]{2,1,0:T(8,128)(2,1)S(1)}, bf16[4,128,256]{2,1,0:T(8,128)(2,1)S(1)}, u32[]{:S(2)}, u32[]{:S(2)}) collective-permute-start(bf16[4,128,256]{2,1,0:T(8,128)(2,1)S(1)} %pair.1), channel_id=1, source_target_pairs={{0,8},{4,12},{8,16},{12,20},{16,24},{20,28},{1,9},{5,13},{9,17},{1... | collective-permute-start | bytes 786440 | tf_op jit(solution)/shard_map/ppermute | solution.py:24
  254.7 9.3 %collective-permute-start.43 = (bf16[4,128,128]{2,1,0:T(8,128)(2,1)S(1)}, bf16[4,128,128]{2,1,0:T(8,128)(2,1)S(1)}, u32[]{:S(2)}, u32[]{:S(2)}) collective-permute-start(bf16[4,128,128]{2,1,0:T(8,128)(2,1)S(1)} %fusion), channel_id=1, source_target_pairs={{0,16},{4,20},{8,24},{12,28},{1,17},{5,21},{9,25},{13,29},{2,18},{... | collective-permute-start | bytes 393224 | tf_op jit(solution)/shard_map/ppermute | solution.py:24
  264.0 16.6 %collective-permute-start.48 = (bf16[256,2048]{1,0:T(8,128)(2,1)}, bf16[256,2048]{1,0:T(8,128)(2,1)S(1)}, u32[]{:S(2)}, u32[]{:S(2)}) collective-permute-start(bf16[256,2048]{1,0:T(8,128)(2,1)} %collective-permute-done.44.refs_3_), channel_id=1, source_target_pairs={{0,1},{1,0},{2,3},{3,2},{4,5},{5,4},{6,7},{7,6},{8,9},{9,8},{10,11... | collective-permute-start | bytes 3145736 | tf_op jit(solution)/shard_map/ppermute | solution.py:722
  265.6 15.0 %collective-permute-start.47 = (bf16[256,2048]{1,0:T(8,128)(2,1)}, bf16[256,2048]{1,0:T(8,128)(2,1)S(1)}, u32[]{:S(2)}, u32[]{:S(2)}) collective-permute-start(bf16[256,2048]{1,0:T(8,128)(2,1)} %collective-permute-done.41.refs_2_), channel_id=1, source_target_pairs={{0,1},{1,0},{2,3},{3,2},{4,5},{5,4},{6,7},{7,6},{8,9},{9,8},{10,11... | collective-permute-start | bytes 3145736 | tf_op jit(solution)/shard_map/ppermute | solution.py:722
  272.5 5.1 %collective-permute-start.45 = (bf16[128,512]{1,0:T(8,128)(2,1)S(1)}, bf16[128,512]{1,0:T(8,128)(2,1)S(1)}, u32[]{:S(2)}, u32[]{:S(2)}) collective-permute-start(bf16[128,512]{1,0:T(8,128)(2,1)S(1)} %get-tuple-element.125), channel_id=1, source_target_pairs={{0,2},{1,3},{2,0},{3,1},{4,6},{5,7},{6,4},{7,5},{8,10},{9,11},{10,... | collective-permute-start | bytes 393224 | tf_op jit(solution)/shard_map/ppermute | solution.py:722
  273.5 7.1 %collective-permute-start.46 = (bf16[128,512]{1,0:T(8,128)(2,1)S(1)}, bf16[128,512]{1,0:T(8,128)(2,1)S(1)}, u32[]{:S(2)}, u32[]{:S(2)}) collective-permute-start(bf16[128,512]{1,0:T(8,128)(2,1)S(1)} %get-tuple-element.124), channel_id=1, source_target_pairs={{0,3},{1,2},{2,1},{3,0},{4,7},{5,6},{6,5},{7,4},{8,11},{9,10},{10,... | collective-permute-start | bytes 393224 | tf_op jit(solution)/shard_map/ppermute | solution.py:722
  (39 other events, 356.8 us)

commit v5 on v3

--- a/solution.py
+++ b/solution.py
@@ -760,7 +760,7 @@
             functools.partial(project_kernel, blocks=len(pieces), halos=len(halos)),
             in_specs=[in_smem] + [in_vmem] * (len(pieces) + len(halos) + 6),
             out_shape=shapes,
-            compiler_params=pltpu.CompilerParams(vmem_limit_bytes=28 << 20),
+            compiler_params=pltpu.CompilerParams(vmem_limit_bytes=52 << 20),
             cost_estimate=worth(4),
             name="project",
         )(head_place.reshape(1), *pieces, *halos, *matrices)

time: 283 us -> 280 us (0.989)
  local copies, waits for them, and re-layouts: 15.9 us -> 9.98 us
  Pallas kernels: 68.1 us -> 72.3 us
    unnamed x86 -> x72, local copies, waits for them, and re-layouts: 13.9 us -> 8 us
    pallas_call x2, Pallas kernels: 7.09 us -> 11.2 us  [project(): pl.pallas_call(functools.partial(project_kernel, blocks=len(pieces), halo...]
  transfers between devices with their start and end apart: 51 -> 51, of which waited for: 31 -> 32; matrix products, arithmetic and copies ran while one was open for 2% -> 2% of each run, Pallas kernels for 19% -> 21%
where the time goes in v5:
time: 280 us
  waiting for transfers between devices  147 us (52%)
  Pallas kernels  72.3 us (26%)
  starting transfers between devices  43 us (15%)
  local copies, waits for them, and re-layouts  9.98 us (4%)
  other arithmetic  5.77 us (2%)
    ppermute x33, waiting for transfers between devices, sent(): return lax.ppermute(value, ('ctx', 'head'), pairs)  119 us
    ppermute x33, starting transfers between devices, sent(): return lax.ppermute(value, ('ctx', 'head'), pairs)  27.7 us
    pallas_call x2, Pallas kernels, run_experts(): pl.pallas_call(expert_kernel, grid=(local_experts,), in_specs=[row_spec]...  16.5 us
    pallas_call x1, Pallas kernels, on_device(): pl.pallas_call(functools.partial(delta_kernel, key_heads=key_heads, chunk...  16.4 us
    pallas_call x2, Pallas kernels, project(): pl.pallas_call(functools.partial(project_kernel, blocks=len(pieces), halo...  11.2 us
    ppermute x3, waiting for transfers between devices, passed_along(): lax.ppermute(value, axis, [(source, source + steps) for source in range(f...  11.1 us
    ppermute x14, starting transfers between devices, crossed(): return lax.ppermute(value, 'head', pairs)  10 us
    ppermute x14, waiting for transfers between devices, crossed(): return lax.ppermute(value, 'head', pairs)  9.83 us
  transfers between devices with their start and end apart: 51, of which 32 were waited for; matrix products, arithmetic and copies ran while one was open for 2% of the time, Pallas kernels for 21%

profile of v5, /device:TPU:25, one launch (start us, length us, event | category | flops | bytes accessed | tf_op | source)
XLA Modules:
  0.0 279.7 jit_solution(93458232557903396)
XLA Ops:
  7.5 9.3 %collective-permute-done.block_10.refs_1_ = bf16[128,2176]{1,0:T(8,128)(2,1)S(1)} collective-permute-done((bf16[128,2176]{1,0:T(8,128)(2,1)S(1)}, bf16[128,2176]{1,0:T(8,128)(2,1)S(1)}, u32[]{:S(2)}, u32[]{:S(2)}) %collective-permute-start) | collective-permute-done | bytes 557088 | tf_op jit(solution)/shard_map/ppermute | solution.py:189
  16.8 3.9 %collective-permute-done.1.block_01.refs_2_ = bf16[128,2176]{1,0:T(8,128)(2,1)S(1)} collective-permute-done((bf16[128,2176]{1,0:T(8,128)(2,1)S(1)}, bf16[128,2176]{1,0:T(8,128)(2,1)S(1)}, u32[]{:S(2)}, u32[]{:S(2)}) %collective-permute-start.1) | collective-permute-done | bytes 557088 | tf_op jit(solution)/shard_map/ppermute | solution.py:189
  20.6 1.4 collective-permute-done.3.block_00.refs_0_
  22.5 11.1 %collective-permute-done.5.block_10.refs_1_ = bf16[128,2176]{1,0:T(8,128)(2,1)} collective-permute-done((bf16[128,2176]{1,0:T(8,128)(2,1)S(1)}, bf16[128,2176]{1,0:T(8,128)(2,1)}, u32[]{:S(2)}, u32[]{:S(2)}) %collective-permute-start.5) | collective-permute-done | bytes 557088 | tf_op jit(solution)/shard_map/ppermute | solution.py:189
  33.5 2.3 collective-permute-done.4.block_00.refs_0_
  36.7 2.4 collective-permute-start.8
  41.1 9.1 %collective-permute-done.8.block_00.refs_0_ = bf16[128,2176]{1,0:T(8,128)(2,1)} collective-permute-done((bf16[128,2176]{1,0:T(8,128)(2,1)S(1)}, bf16[128,2176]{1,0:T(8,128)(2,1)}, u32[]{:S(2)}, u32[]{:S(2)}) %collective-permute-start.8) | collective-permute-done | bytes 557088 | tf_op jit(solution)/shard_map/ppermute | solution.py:189
  50.2 1.8 collective-permute-done.9.block_10.refs_1_
  55.8 5.0 %collective-permute-done.2.block_11.refs_3_ = bf16[128,2176]{1,0:T(8,128)(2,1)S(1)} collective-permute-done((bf16[128,2176]{1,0:T(8,128)(2,1)S(1)}, bf16[128,2176]{1,0:T(8,128)(2,1)S(1)}, u32[]{:S(2)}, u32[]{:S(2)}) %collective-permute-start.2) | collective-permute-done | bytes 557088 | tf_op jit(solution)/shard_map/ppermute | solution.py:189
  61.9 3.5 %collective-permute-start.14 = (bf16[2,96,2048]{2,1,0:T(8,128)(2,1)S(1)}, bf16[2,96,2048]{2,1,0:T(8,128)(2,1)S(1)}, u32[]{:S(2)}, u32[]{:S(2)}) collective-permute-start(bf16[2,96,2048]{2,1,0:T(8,128)(2,1)S(1)} %get-tuple-element.70), channel_id=1, source_target_pairs={{0,1},{1,0},{2,3},{3,2},{4,5},{5,4},{6,7},{7,6},{8,9},{9,8},{10,11... | collective-permute-start | bytes 2359304 | tf_op jit(solution)/shard_map/ppermute | solution.py:189
  65.4 6.7 %collective-permute-done.7.block_11.refs_3_ = bf16[128,2176]{1,0:T(8,128)(2,1)} collective-permute-done((bf16[128,2176]{1,0:T(8,128)(2,1)}, bf16[128,2176]{1,0:T(8,128)(2,1)}, u32[]{:S(2)}, u32[]{:S(2)}) %collective-permute-start.7) | collective-permute-done | bytes 557088 | tf_op jit(solution)/shard_map/ppermute | solution.py:189
  72.1 2.3 collect.5
  74.7 3.3 %collective-permute-done.12.block_01.refs_2_ = bf16[128,2176]{1,0:T(8,128)(2,1)S(1)} collective-permute-done((bf16[128,2176]{1,0:T(8,128)(2,1)}, bf16[128,2176]{1,0:T(8,128)(2,1)S(1)}, u32[]{:S(2)}, u32[]{:S(2)}) %collective-permute-start.12) | collective-permute-done | bytes 557088 | tf_op jit(solution)/shard_map/ppermute | solution.py:189
  78.0 5.7 %collective-permute-done.13.block_11.refs_3_ = bf16[128,2176]{1,0:T(8,128)(2,1)S(1)} collective-permute-done((bf16[128,2176]{1,0:T(8,128)(2,1)}, bf16[128,2176]{1,0:T(8,128)(2,1)S(1)}, u32[]{:S(2)}, u32[]{:S(2)}) %collective-permute-start.13) | collective-permute-done | bytes 557088 | tf_op jit(solution)/shard_map/ppermute | solution.py:189
  83.7 2.5 collect.6
  86.7 1.9 collective-permute-done.16.refs_5_
  88.6 10.2 %experts.2 = (bf16[2,288,2048]{2,1,0:T(8,128)(2,1)S(1)}, bf16[2,288,2048]{2,1,0:T(8,128)(2,1)S(1)}) custom-call(bf16[2,96,2048]{2,1,0:T(8,128)(2,1)S(1)} %get-tuple-element.61.refs_0_, bf16[2,96,2048]{2,1,0:T(8,128)(2,1)S(1)} %get-tuple-element.64.refs_1_, bf16[2,96,2048]{2,1,0:T(8,128)(2,1)S(1)} %get-tuple-element.69.refs_2_, ...), custom_call_target="tpu_custom_call" | custom-call | flops 14949999616 | bytes 13000000 | tf_op jit(solution)/shard_map/experts/pallas_call | solution.py:264
  99.6 3.8 %collective-permute-done.17.refs_6_ = bf16[2,288,2048]{2,1,0:T(8,128)(2,1)S(1)} collective-permute-done((bf16[2,288,2048]{2,1,0:T(8,128)(2,1)S(1)}, bf16[2,288,2048]{2,1,0:T(8,128)(2,1)S(1)}, u32[]{:S(2)}, u32[]{:S(2)}) %collective-permute-start.17) | collective-permute-done | bytes 2359328 | tf_op jit(solution)/shard_map/ppermute | solution.py:189
  103.4 2.3 spread.6
  106.2 2.2 spread.5
  109.6 2.4 collect.7
  113.0 6.7 %collective-permute-done.22 = bf16[1,2,128,2048]{3,2,1,0:T(8,128)(2,1)S(1)} collective-permute-done((bf16[1,2,128,2048]{3,2,1,0:T(8,128)(2,1)S(1)}, bf16[1,2,128,2048]{3,2,1,0:T(8,128)(2,1)S(1)}, u32[]{:S(2)}, u32[]{:S(2)}) %collective-permute-start.22) | collective-permute-done | bytes 1048608 | tf_op jit(solution)/shard_map/ppermute | solution.py:189
  121.1 6.3 %experts.3 = (bf16[2,96,2048]{2,1,0:T(8,128)(2,1)S(1)}, bf16[2,96,2048]{2,1,0:T(8,128)(2,1)S(1)}) custom-call(bf16[2,96,2048]{2,1,0:T(8,128)(2,1)S(1)} %get-tuple-element.86.refs_0_, bf16[2,96,2048]{2,1,0:T(8,128)(2,1)S(1)} %collective-permute-done.28.refs_1_, bf16[2,2048,512]{2,1,0:T(8,128)(2,1)S(1)} %copy-done.2, bf16[2,2048,512]{2,1,0:T(8,128)(2,1)S(1)} %copy-done.3, ...), custom_call_target="tpu_custom_call" | custom-call | flops 1150000000 | bytes 1000000 | tf_op jit(solution)/shard_map/experts/pallas_call | solution.py:264
  128.3 8.3 %collective-permute-done.20 = bf16[1,2,128,2048]{3,2,1,0:T(8,128)(2,1)S(1)} collective-permute-done((bf16[1,2,128,2048]{3,2,1,0:T(8,128)(2,1)S(1)}, bf16[1,2,128,2048]{3,2,1,0:T(8,128)(2,1)S(1)}, u32[]{:S(2)}, u32[]{:S(2)}) %collective-permute-start.20) | collective-permute-done | bytes 1048608 | tf_op jit(solution)/shard_map/ppermute | solution.py:189
  138.5 2.2 spread.7
  141.2 1.5 spread.4
  145.1 6.0 %collective-permute-done.24 = bf16[128,2048]{1,0:T(8,128)(2,1)S(1)} collective-permute-done((bf16[128,2048]{1,0:T(8,128)(2,1)S(1)}, bf16[128,2048]{1,0:T(8,128)(2,1)S(1)}, u32[]{:S(2)}, u32[]{:S(2)}) %collective-permute-start.24) | collective-permute-done | bytes 524320 | tf_op jit(solution)/shard_map/ppermute | solution.py:189
  151.5 1.7 collective-permute-start.25
  153.2 4.8 %collective-permute-done.30 = bf16[1,2,128,2048]{3,2,1,0:T(8,128)(2,1)S(1)} collective-permute-done((bf16[1,2,128,2048]{3,2,1,0:T(8,128)(2,1)S(1)}, bf16[1,2,128,2048]{3,2,1,0:T(8,128)(2,1)S(1)}, u32[]{:S(2)}, u32[]{:S(2)}) %collective-permute-start.30) | collective-permute-done | bytes 1048608 | tf_op jit(solution)/shard_map/ppermute | solution.py:189
  159.5 7.6 %collective-permute-done.19 = bf16[128,2048]{1,0:T(8,128)(2,1)S(1)} collective-permute-done((bf16[128,2048]{1,0:T(8,128)(2,1)S(1)}, bf16[128,2048]{1,0:T(8,128)(2,1)S(1)}, u32[]{:S(2)}, u32[]{:S(2)}) %collective-permute-start.19) | collective-permute-done | bytes 524320 | tf_op jit(solution)/shard_map/ppermute | solution.py:189
  168.0 4.2 %collective-permute-done.31 = bf16[128,2048]{1,0:T(8,128)(2,1)S(1)} collective-permute-done((bf16[128,2048]{1,0:T(8,128)(2,1)S(1)}, bf16[128,2048]{1,0:T(8,128)(2,1)S(1)}, u32[]{:S(2)}, u32[]{:S(2)}) %collective-permute-start.31) | collective-permute-done | bytes 524320 | tf_op jit(solution)/shard_map/ppermute | solution.py:189
  173.3 1.5 fusion.24
  174.8 3.6 %collective-permute-done.18 = bf16[128,2048]{1,0:T(8,128)(2,1)S(1)} collective-permute-done((bf16[128,2048]{1,0:T(8,128)(2,1)S(1)}, bf16[128,2048]{1,0:T(8,128)(2,1)S(1)}, u32[]{:S(2)}, u32[]{:S(2)}) %collective-permute-start.18) | collective-permute-done | bytes 524320 | tf_op jit(solution)/shard_map/ppermute | solution.py:189
  178.8 9.4 %collective-permute-done.32 = bf16[128,2048]{1,0:T(8,128)(2,1)S(1)} collective-permute-done((bf16[128,2048]{1,0:T(8,128)(2,1)S(1)}, bf16[128,2048]{1,0:T(8,128)(2,1)S(1)}, u32[]{:S(2)}, u32[]{:S(2)}) %collective-permute-start.32) | collective-permute-done | bytes 524320 | tf_op jit(solution)/shard_map/ppermute | solution.py:189
  190.7 2.3 collective-permute-start.33
  195.1 1.5 collective-permute-done.33.refs_2_
  197.2 5.6 %project.2 = (bf16[256,1024]{1,0:T(8,128)(2,1)S(1)}, bf16[256,512]{1,0:T(8,128)(2,1)S(1)}, f32[256,4]{1,0:T(8,128)S(1)}, f32[256,4]{1,0:T(8,128)S(1)}) custom-call(s32[1]{0:T(128)} %bitcast.17.place_ref, bf16[128,2048]{1,0:T(8,128)(2,1)S(1)} %multiply_convert_fusion.refs_0_, bf16[128,2048]{1,0:T(8,128)(2,1)} %collective-permute-done.34.refs_1_, ...), custom_call_target="tpu_custom_call" | custom-call | flops 4600000000 | bytes 4000000 | tf_op jit(solution)/shard_map/project/pallas_call | solution.py:759
  208.0 5.6 %project.3 = (bf16[256,1024]{1,0:T(8,128)(2,1)S(1)}, bf16[256,512]{1,0:T(8,128)(2,1)S(1)}, f32[256,4]{1,0:T(8,128)S(1)}, f32[256,4]{1,0:T(8,128)S(1)}, f32[16,1024]{1,0:T(8,128)S(1)}) custom-call(s32[1]{0:T(128)} %bitcast.17.place_ref, bf16[128,2048]{1,0:T(8,128)(2,1)S(1)} %collective-permute-done.35.refs_0_, bf16[128,2048]{1,0:T(8,128)(2,1)} %copy-done.34, ...), custom_call_target="tpu_custom_call" | custom-call | flops 4600000000 | bytes 4000000 | tf_op jit(solution)/shard_map/project/pallas_call | solution.py:759
  213.6 16.4 %delta.1 = (f32[512,512]{1,0:T(8,128)S(1)}, f32[512,512]{1,0:T(8,128)S(1)}, bf16[4,128,256]{2,1,0:T(8,128)(2,1)}) custom-call(s32[1]{0:T(128)} %bitcast.17.place_ref, bf16[256,1024]{1,0:T(8,128)(2,1)S(1)} %get-tuple-element.96.near_raw, bf16[256,1024]{1,0:T(8,128)(2,1)S(1)} %get-tuple-element.98.far_raw, f32[256,4]{1,0:T(8,128)S(1)} %get-tuple-element.99.near_beta, ...), custom_call_target="tpu_custom_call" | custom-call | flops 18400000000 | bytes 16000000 | tf_op jit(solution)/shard_map/delta/pallas_call | solution.py:776
  232.7 7.5 %collective-permute-done.40.other_ref = bf16[4,128,256]{2,1,0:T(8,128)(2,1)S(1)} collective-permute-done((bf16[4,128,256]{2,1,0:T(8,128)(2,1)}, bf16[4,128,256]{2,1,0:T(8,128)(2,1)S(1)}, u32[]{:S(2)}, u32[]{:S(2)}) %collective-permute-start.40) | collective-permute-done | bytes 262176 | tf_op jit(solution)/shard_map/ppermute | solution.py:806
  242.7 7.4 %collective-permute-done.42.near_pairs_ref = bf16[4,128,256]{2,1,0:T(8,128)(2,1)S(1)} collective-permute-done((bf16[4,128,256]{2,1,0:T(8,128)(2,1)S(1)}, bf16[4,128,256]{2,1,0:T(8,128)(2,1)S(1)}, u32[]{:S(2)}, u32[]{:S(2)}) %collective-permute-start.42) | collective-permute-done | bytes 262176 | tf_op jit(solution)/shard_map/ppermute | solution.py:24
  251.5 5.3 %collective-permute-done.44.refs_3_ = bf16[256,2048]{1,0:T(8,128)(2,1)} collective-permute-done((bf16[256,2048]{1,0:T(8,128)(2,1)}, bf16[256,2048]{1,0:T(8,128)(2,1)}, u32[]{:S(2)}, u32[]{:S(2)}) %collective-permute-start.44) | collective-permute-done | bytes 1048608 | tf_op jit(solution)/shard_map/ppermute | solution.py:722
  256.8 2.2 collective-permute-done.43.far_pairs_ref
  259.0 1.6 collective-permute-start.48
  263.8 3.1 %finish.1 = bf16[512,512]{1,0:T(8,128)(2,1)S(1)} custom-call(s32[2]{0:T(128)S(1)} %pad_add_fusion.where_ref, bf16[4,128,256]{2,1,0:T(8,128)(2,1)S(1)} %collective-permute-done.42.near_pairs_ref, bf16[4,128,128]{2,1,0:T(8,128)(2,1)S(1)} %collective-permute-done.43.far_pairs_ref, bf16[4,128,256]{2,1,0:T(8,128)(2,1)S(1)} %collective-permute-done.40.other_ref, ...), custom_call_target="tpu_custom_call" | custom-call | tf_op jit(solution)/shard_map/finish/pallas_call | solution.py:841
  269.9 3.2 %output.2.refs_6_ = f32[128,2048]{1,0:T(8,128)S(1)} custom-call(bf16[128,512]{1,0:T(8,128)(2,1)S(1)} %get-tuple-element.121.refs_0_, bf16[128,512]{1,0:T(8,128)(2,1)S(1)} %collective-permute-done.49.refs_1_, bf16[512,2048]{1,0:T(8,128)(2,1)S(1)} %copy-done.4, bf16[512,2048]{1,0:T(8,128)(2,1)} %collective-permute-done.50.refs_3_), custom_call_target="tpu_custom_call" | custom-call | flops 3449999872 | bytes 3000000 | tf_op jit(solution)/shard_map/output/pallas_call | solution.py:882
  273.2 2.5 collective-permute-done.46.refs_1_
  275.6 4.1 %output.3 = bf16[128,2048]{1,0:T(8,128)(2,1)} custom-call(bf16[128,512]{1,0:T(8,128)(2,1)S(1)} %collective-permute-done.45.refs_0_, bf16[128,512]{1,0:T(8,128)(2,1)S(1)} %collective-permute-done.46.refs_1_, bf16[256,2048]{1,0:T(8,128)(2,1)} %collective-permute-done.41.refs_2_, bf16[256,2048]{1,0:T(8,128)(2,1)} %collective-permute-done.44.refs_3_, ...), custom_call_target="tpu_custom_call" | custom-call | flops 3449999872 | bytes 3000000 | tf_op jit(solution)/shard_map/output/pallas_call | solution.py:882
  (174 shorter events, 53.4 us)
Async XLA Ops:
  4.8 12.0 %collective-permute-start = (bf16[128,2176]{1,0:T(8,128)(2,1)S(1)}, bf16[128,2176]{1,0:T(8,128)(2,1)S(1)}, u32[]{:S(2)}, u32[]{:S(2)}) collective-permute-start(bf16[128,2176]{1,0:T(8,128)(2,1)S(1)} %concatenate.6.block_00.refs_0_), channel_id=1, source_target_pairs={{0,4},{1,3},{2,6},{3,1},{4,0},{5,7},{6,2},{7,5},{8,12},{9,11},{10,... | collective-permute-start | bytes 1671176 | tf_op jit(solution)/shard_map/ppermute | solution.py:189
  6.1 14.6 %collective-permute-start.1 = (bf16[128,2176]{1,0:T(8,128)(2,1)S(1)}, bf16[128,2176]{1,0:T(8,128)(2,1)S(1)}, u32[]{:S(2)}, u32[]{:S(2)}) collective-permute-start(bf16[128,2176]{1,0:T(8,128)(2,1)S(1)} %concatenate.6.block_00.refs_0_), channel_id=1, source_target_pairs={{0,2},{1,5},{2,0},{3,7},{4,6},{5,1},{6,4},{7,3},{8,10},{9,13},{10,... | collective-permute-start | bytes 1671176 | tf_op jit(solution)/shard_map/ppermute | solution.py:189
  7.3 14.7 %collective-permute-start.3 = (bf16[128,2176]{1,0:T(8,128)(2,1)S(1)}, bf16[128,2176]{1,0:T(8,128)(2,1)S(1)}, u32[]{:S(2)}, u32[]{:S(2)}) collective-permute-start(bf16[128,2176]{1,0:T(8,128)(2,1)S(1)} %concatenate.6.block_00.refs_0_), channel_id=1, source_target_pairs={{0,24},{1,25},{2,26},{3,27},{4,28},{5,29},{6,30},{7,31},{8,0},{9,1... | collective-permute-start | bytes 1671176 | tf_op jit(solution)/shard_map/ppermute | solution.py:189
  22.0 11.5 %collective-permute-start.5 = (bf16[128,2176]{1,0:T(8,128)(2,1)S(1)}, bf16[128,2176]{1,0:T(8,128)(2,1)}, u32[]{:S(2)}, u32[]{:S(2)}) collective-permute-start(bf16[128,2176]{1,0:T(8,128)(2,1)S(1)} %collective-permute-done.3.block_00.refs_0_), channel_id=1, source_target_pairs={{0,4},{1,3},{2,6},{3,1},{4,0},{5,7},{6,2},{7,5},{8,12},{9,11},{10,... | collective-permute-start | bytes 1671176 | tf_op jit(solution)/shard_map/ppermute | solution.py:189
  22.2 13.6 %collective-permute-start.4 = (bf16[128,2176]{1,0:T(8,128)(2,1)S(1)}, bf16[128,2176]{1,0:T(8,128)(2,1)}, u32[]{:S(2)}, u32[]{:S(2)}) collective-permute-start(bf16[128,2176]{1,0:T(8,128)(2,1)S(1)} %collective-permute-done.3.block_00.refs_0_), channel_id=1, source_target_pairs={{0,24},{1,25},{2,26},{3,27},{4,28},{5,29},{6,30},{7,31},{8,0},{9,1... | collective-permute-start | bytes 1671176 | tf_op jit(solution)/shard_map/ppermute | solution.py:189
  22.3 13.6 %collective-permute-start.6 = (bf16[128,2176]{1,0:T(8,128)(2,1)S(1)}, bf16[128,2176]{1,0:T(8,128)(2,1)S(1)}, u32[]{:S(2)}, u32[]{:S(2)}) collective-permute-start(bf16[128,2176]{1,0:T(8,128)(2,1)S(1)} %collective-permute-done.3.block_00.refs_0_), channel_id=1, source_target_pairs={{0,2},{1,5},{2,0},{3,7},{4,6},{5,1},{6,4},{7,3},{8,10},{9,13},{10,... | collective-permute-start | bytes 1671176 | tf_op jit(solution)/shard_map/ppermute | solution.py:189
  36.7 13.5 %collective-permute-start.8 = (bf16[128,2176]{1,0:T(8,128)(2,1)S(1)}, bf16[128,2176]{1,0:T(8,128)(2,1)}, u32[]{:S(2)}, u32[]{:S(2)}) collective-permute-start(bf16[128,2176]{1,0:T(8,128)(2,1)S(1)} %concatenate.6.block_00.refs_0_), channel_id=1, source_target_pairs={{0,8},{1,9},{2,10},{3,11},{4,12},{5,13},{6,14},{7,15},{8,16},{9,17... | collective-permute-start | bytes 1671176 | tf_op jit(solution)/shard_map/ppermute | solution.py:189
  39.0 12.9 %collective-permute-start.9 = (bf16[128,2176]{1,0:T(8,128)(2,1)}, bf16[128,2176]{1,0:T(8,128)(2,1)}, u32[]{:S(2)}, u32[]{:S(2)}) collective-permute-start(bf16[128,2176]{1,0:T(8,128)(2,1)} %collective-permute-done.4.block_00.refs_0_), channel_id=1, source_target_pairs={{0,4},{1,3},{2,6},{3,1},{4,0},{5,7},{6,2},{7,5},{8,12},{9,11},{10,... | collective-permute-start | bytes 1671176 | tf_op jit(solution)/shard_map/ppermute | solution.py:189
  39.3 13.6 %collective-permute-start.10 = (bf16[128,2176]{1,0:T(8,128)(2,1)}, bf16[128,2176]{1,0:T(8,128)(2,1)}, u32[]{:S(2)}, u32[]{:S(2)}) collective-permute-start(bf16[128,2176]{1,0:T(8,128)(2,1)} %collective-permute-done.4.block_00.refs_0_), channel_id=1, source_target_pairs={{0,2},{1,5},{2,0},{3,7},{4,6},{5,1},{6,4},{7,3},{8,10},{9,13},{10,... | collective-permute-start | bytes 1671176 | tf_op jit(solution)/shard_map/ppermute | solution.py:189
  39.6 21.2 %collective-permute-start.2 = (bf16[128,2176]{1,0:T(8,128)(2,1)S(1)}, bf16[128,2176]{1,0:T(8,128)(2,1)S(1)}, u32[]{:S(2)}, u32[]{:S(2)}) collective-permute-start(bf16[128,2176]{1,0:T(8,128)(2,1)S(1)} %collective-permute-done.block_10.refs_1_), channel_id=1, source_target_pairs={{0,2},{1,5},{2,0},{3,7},{4,6},{5,1},{6,4},{7,3},{8,10},{9,13},{10,... | collective-permute-start | bytes 1671176 | tf_op jit(solution)/shard_map/ppermute | solution.py:189
  40.8 31.3 %collective-permute-start.7 = (bf16[128,2176]{1,0:T(8,128)(2,1)}, bf16[128,2176]{1,0:T(8,128)(2,1)}, u32[]{:S(2)}, u32[]{:S(2)}) collective-permute-start(bf16[128,2176]{1,0:T(8,128)(2,1)} %collective-permute-done.5.block_10.refs_1_), channel_id=1, source_target_pairs={{0,2},{1,5},{2,0},{3,7},{4,6},{5,1},{6,4},{7,3},{8,10},{9,13},{10,... | collective-permute-start | bytes 1671176 | tf_op jit(solution)/shard_map/ppermute | solution.py:189
  52.9 21.8 %collective-permute-start.11 = (bf16[128,2176]{1,0:T(8,128)(2,1)}, bf16[128,2176]{1,0:T(8,128)(2,1)S(1)}, u32[]{:S(2)}, u32[]{:S(2)}) collective-permute-start(bf16[128,2176]{1,0:T(8,128)(2,1)} %collective-permute-done.8.block_00.refs_0_), channel_id=1, source_target_pairs={{0,4},{1,3},{2,6},{3,1},{4,0},{5,7},{6,2},{7,5},{8,12},{9,11},{10,... | collective-permute-start | bytes 1671176 | tf_op jit(solution)/shard_map/ppermute | solution.py:189
  54.3 23.8 %collective-permute-start.12 = (bf16[128,2176]{1,0:T(8,128)(2,1)}, bf16[128,2176]{1,0:T(8,128)(2,1)S(1)}, u32[]{:S(2)}, u32[]{:S(2)}) collective-permute-start(bf16[128,2176]{1,0:T(8,128)(2,1)} %collective-permute-done.8.block_00.refs_0_), channel_id=1, source_target_pairs={{0,2},{1,5},{2,0},{3,7},{4,6},{5,1},{6,4},{7,3},{8,10},{9,13},{10,... | collective-permute-start | bytes 1671176 | tf_op jit(solution)/shard_map/ppermute | solution.py:189
  54.8 29.0 %collective-permute-start.13 = (bf16[128,2176]{1,0:T(8,128)(2,1)}, bf16[128,2176]{1,0:T(8,128)(2,1)S(1)}, u32[]{:S(2)}, u32[]{:S(2)}) collective-permute-start(bf16[128,2176]{1,0:T(8,128)(2,1)} %collective-permute-done.9.block_10.refs_1_), channel_id=1, source_target_pairs={{0,2},{1,5},{2,0},{3,7},{4,6},{5,1},{6,4},{7,3},{8,10},{9,13},{10,... | collective-permute-start | bytes 1671176 | tf_op jit(solution)/shard_map/ppermute | solution.py:189
  61.9 24.8 %collective-permute-start.14 = (bf16[2,96,2048]{2,1,0:T(8,128)(2,1)S(1)}, bf16[2,96,2048]{2,1,0:T(8,128)(2,1)S(1)}, u32[]{:S(2)}, u32[]{:S(2)}) collective-permute-start(bf16[2,96,2048]{2,1,0:T(8,128)(2,1)S(1)} %get-tuple-element.70), channel_id=1, source_target_pairs={{0,1},{1,0},{2,3},{3,2},{4,5},{5,4},{6,7},{7,6},{8,9},{9,8},{10,11... | collective-permute-start | bytes 2359304 | tf_op jit(solution)/shard_map/ppermute | solution.py:189
  74.4 12.3 %collective-permute-start.15 = (bf16[2,96,2048]{2,1,0:T(8,128)(2,1)S(1)}, bf16[2,96,2048]{2,1,0:T(8,128)(2,1)S(1)}, u32[]{:S(2)}, u32[]{:S(2)}) collective-permute-start(bf16[2,96,2048]{2,1,0:T(8,128)(2,1)S(1)} %get-tuple-element.71), channel_id=1, source_target_pairs={{0,1},{1,0},{2,3},{3,2},{4,5},{5,4},{6,7},{7,6},{8,9},{9,8},{10,11... | collective-permute-start | bytes 2359304 | tf_op jit(solution)/shard_map/ppermute | solution.py:189
  98.8 4.6 %collective-permute-start.17 = (bf16[2,288,2048]{2,1,0:T(8,128)(2,1)S(1)}, bf16[2,288,2048]{2,1,0:T(8,128)(2,1)S(1)}, u32[]{:S(2)}, u32[]{:S(2)}) collective-permute-start(bf16[2,288,2048]{2,1,0:T(8,128)(2,1)S(1)} %get-tuple-element.74), channel_id=1, source_target_pairs={{0,1},{1,0},{2,3},{3,2},{4,5},{5,4},{6,7},{7,6},{8,9},{9,8},{10,11... | collective-permute-start | bytes 7077896 | tf_op jit(solution)/shard_map/ppermute | solution.py:189
  99.3 10.4 %collective-permute-start.27 = (bf16[128,2176]{1,0:T(8,128)(2,1)S(1)}, bf16[128,2176]{1,0:T(8,128)(2,1)S(1)}, u32[]{:S(2)}, u32[]{:S(2)}) collective-permute-start(bf16[128,2176]{1,0:T(8,128)(2,1)S(1)} %collective-permute-done.11.block_10.refs_1_), channel_id=1, source_target_pairs={{0,2},{1,5},{2,0},{3,7},{4,6},{5,1},{6,4},{7,3},{8,10},{9,13},{10,... | collective-permute-start | bytes 1671176 | tf_op jit(solution)/shard_map/ppermute | solution.py:189
  105.7 14.0 %collective-permute-start.22 = (bf16[1,2,128,2048]{3,2,1,0:T(8,128)(2,1)S(1)}, bf16[1,2,128,2048]{3,2,1,0:T(8,128)(2,1)S(1)}, u32[]{:S(2)}, u32[]{:S(2)}) collective-permute-start(bf16[1,2,128,2048]{3,2,1,0:T(8,128)(2,1)S(1)} %get-tuple-element.82), channel_id=1, source_target_pairs={{0,2},{1,5},{2,0},{3,7},{4,6},{5,1},{6,4},{7,3},{8,10},{9,13},{10,... | collective-permute-start | bytes 3145736 | tf_op jit(solution)/shard_map/ppermute | solution.py:189
  108.4 28.2 %collective-permute-start.20 = (bf16[1,2,128,2048]{3,2,1,0:T(8,128)(2,1)S(1)}, bf16[1,2,128,2048]{3,2,1,0:T(8,128)(2,1)S(1)}, u32[]{:S(2)}, u32[]{:S(2)}) collective-permute-start(bf16[1,2,128,2048]{3,2,1,0:T(8,128)(2,1)S(1)} %get-tuple-element.79), channel_id=1, source_target_pairs={{0,2},{1,5},{2,0},{3,7},{4,6},{5,1},{6,4},{7,3},{8,10},{9,13},{10,... | collective-permute-start | bytes 3145736 | tf_op jit(solution)/shard_map/ppermute | solution.py:189
  112.0 9.1 %collective-permute-start.28 = (bf16[2,96,2048]{2,1,0:T(8,128)(2,1)S(1)}, bf16[2,96,2048]{2,1,0:T(8,128)(2,1)S(1)}, u32[]{:S(2)}, u32[]{:S(2)}) collective-permute-start(bf16[2,96,2048]{2,1,0:T(8,128)(2,1)S(1)} %get-tuple-element.87), channel_id=1, source_target_pairs={{0,1},{1,0},{2,3},{3,2},{4,5},{5,4},{6,7},{7,6},{8,9},{9,8},{10,11... | collective-permute-start | bytes 2359304 | tf_op jit(solution)/shard_map/ppermute | solution.py:189
  119.9 18.1 %collective-permute-start.23 = (bf16[128,2048]{1,0:T(8,128)(2,1)S(1)}, bf16[128,2048]{1,0:T(8,128)(2,1)S(1)}, u32[]{:S(2)}, u32[]{:S(2)}) collective-permute-start(bf16[128,2048]{1,0:T(8,128)(2,1)S(1)} %fusion.8), channel_id=1, source_target_pairs={{0,4},{1,3},{2,6},{3,1},{4,0},{5,7},{6,2},{7,5},{8,12},{9,11},{10,... | collective-permute-start | bytes 1572872 | tf_op jit(solution)/shard_map/ppermute | solution.py:189
  127.5 11.0 %collective-permute-start.29 = (bf16[2,96,2048]{2,1,0:T(8,128)(2,1)S(1)}, bf16[2,96,2048]{2,1,0:T(8,128)(2,1)S(1)}, u32[]{:S(2)}, u32[]{:S(2)}) collective-permute-start(bf16[2,96,2048]{2,1,0:T(8,128)(2,1)S(1)} %get-tuple-element.89), channel_id=1, source_target_pairs={{0,1},{1,0},{2,3},{3,2},{4,5},{5,4},{6,7},{7,6},{8,9},{9,8},{10,11... | collective-permute-start | bytes 2359304 | tf_op jit(solution)/shard_map/ppermute | solution.py:189
  136.7 8.4 %collective-permute-start.21 = (bf16[128,2048]{1,0:T(8,128)(2,1)S(1)}, bf16[128,2048]{1,0:T(8,128)(2,1)S(1)}, u32[]{:S(2)}, u32[]{:S(2)}) collective-permute-start(bf16[128,2048]{1,0:T(8,128)(2,1)S(1)} %fusion.11), channel_id=1, source_target_pairs={{0,4},{1,3},{2,6},{3,1},{4,0},{5,7},{6,2},{7,5},{8,12},{9,11},{10,... | collective-permute-start | bytes 1572872 | tf_op jit(solution)/shard_map/ppermute | solution.py:189
  138.2 13.0 %collective-permute-start.24 = (bf16[128,2048]{1,0:T(8,128)(2,1)S(1)}, bf16[128,2048]{1,0:T(8,128)(2,1)S(1)}, u32[]{:S(2)}, u32[]{:S(2)}) collective-permute-start(bf16[128,2048]{1,0:T(8,128)(2,1)S(1)} %fusion.10), channel_id=1, source_target_pairs={{0,8},{1,9},{2,10},{3,11},{4,12},{5,13},{6,14},{7,15},{8,16},{9,17... | collective-permute-start | bytes 1572872 | tf_op jit(solution)/shard_map/ppermute | solution.py:189
  140.7 17.3 %collective-permute-start.30 = (bf16[1,2,128,2048]{3,2,1,0:T(8,128)(2,1)S(1)}, bf16[1,2,128,2048]{3,2,1,0:T(8,128)(2,1)S(1)}, u32[]{:S(2)}, u32[]{:S(2)}) collective-permute-start(bf16[1,2,128,2048]{3,2,1,0:T(8,128)(2,1)S(1)} %get-tuple-element.91), channel_id=1, source_target_pairs={{0,2},{1,5},{2,0},{3,7},{4,6},{5,1},{6,4},{7,3},{8,10},{9,13},{10,... | collective-permute-start | bytes 3145736 | tf_op jit(solution)/shard_map/ppermute | solution.py:189
  142.7 24.4 %collective-permute-start.19 = (bf16[128,2048]{1,0:T(8,128)(2,1)S(1)}, bf16[128,2048]{1,0:T(8,128)(2,1)S(1)}, u32[]{:S(2)}, u32[]{:S(2)}) collective-permute-start(bf16[128,2048]{1,0:T(8,128)(2,1)S(1)} %get-tuple-element.119), channel_id=1, source_target_pairs={{0,2},{1,5},{2,0},{3,7},{4,6},{5,1},{6,4},{7,3},{8,10},{9,13},{10,... | collective-permute-start | bytes 1572872 | tf_op jit(solution)/shard_map/ppermute | solution.py:189
  151.5 15.6 %collective-permute-start.25 = (bf16[128,2048]{1,0:T(8,128)(2,1)S(1)}, bf16[128,2048]{1,0:T(8,128)(2,1)S(1)}, u32[]{:S(2)}, u32[]{:S(2)}) collective-permute-start(bf16[128,2048]{1,0:T(8,128)(2,1)S(1)} %fusion.14), channel_id=1, source_target_pairs={{0,8},{1,9},{2,10},{3,11},{4,12},{5,13},{6,14},{7,15},{8,16},{9,17... | collective-permute-start | bytes 1572872 | tf_op jit(solution)/shard_map/ppermute | solution.py:189
  158.2 14.1 %collective-permute-start.31 = (bf16[128,2048]{1,0:T(8,128)(2,1)S(1)}, bf16[128,2048]{1,0:T(8,128)(2,1)S(1)}, u32[]{:S(2)}, u32[]{:S(2)}) collective-permute-start(bf16[128,2048]{1,0:T(8,128)(2,1)S(1)} %fusion.5), channel_id=1, source_target_pairs={{0,4},{1,3},{2,6},{3,1},{4,0},{5,7},{6,2},{7,5},{8,12},{9,11},{10,... | collective-permute-start | bytes 1572872 | tf_op jit(solution)/shard_map/ppermute | solution.py:189
  159.2 19.2 %collective-permute-start.18 = (bf16[128,2048]{1,0:T(8,128)(2,1)S(1)}, bf16[128,2048]{1,0:T(8,128)(2,1)S(1)}, u32[]{:S(2)}, u32[]{:S(2)}) collective-permute-start(bf16[128,2048]{1,0:T(8,128)(2,1)S(1)} %get-tuple-element.118), channel_id=1, source_target_pairs={{0,2},{1,5},{2,0},{3,7},{4,6},{5,1},{6,4},{7,3},{8,10},{9,13},{10,... | collective-permute-start | bytes 1572872 | tf_op jit(solution)/shard_map/ppermute | solution.py:189
  167.3 11.6 %collective-permute-start.26 = (bf16[128,2048]{1,0:T(8,128)(2,1)S(1)}, bf16[128,2048]{1,0:T(8,128)(2,1)S(1)}, u32[]{:S(2)}, u32[]{:S(2)}) collective-permute-start(bf16[128,2048]{1,0:T(8,128)(2,1)S(1)} %fusion.15), channel_id=1, source_target_pairs={{0,4},{1,3},{2,6},{3,1},{4,0},{5,7},{6,2},{7,5},{8,12},{9,11},{10,... | collective-permute-start | bytes 1572872 | tf_op jit(solution)/shard_map/ppermute | solution.py:189
  172.5 15.8 %collective-permute-start.32 = (bf16[128,2048]{1,0:T(8,128)(2,1)S(1)}, bf16[128,2048]{1,0:T(8,128)(2,1)S(1)}, u32[]{:S(2)}, u32[]{:S(2)}) collective-permute-start(bf16[128,2048]{1,0:T(8,128)(2,1)S(1)} %fusion.7), channel_id=1, source_target_pairs={{0,24},{1,25},{2,26},{3,27},{4,28},{5,29},{6,30},{7,31},{8,0},{9,1... | collective-permute-start | bytes 1572872 | tf_op jit(solution)/shard_map/ppermute | solution.py:189
  189.2 7.9 %collective-permute-start.34 = (bf16[128,2048]{1,0:T(8,128)(2,1)S(1)}, bf16[128,2048]{1,0:T(8,128)(2,1)}, u32[]{:S(2)}, u32[]{:S(2)}) collective-permute-start(bf16[128,2048]{1,0:T(8,128)(2,1)S(1)} %multiply_convert_fusion.refs_0_), channel_id=1, source_target_pairs={{0,1},{1,0},{2,3},{3,2},{4,5},{5,4},{6,7},{7,6},{8,9},{9,8},{10,11... | collective-permute-start | bytes 1572872 | tf_op jit(solution)/shard_map/ppermute | solution.py:722
  189.7 14.9 %collective-permute-start.35 = (bf16[128,2048]{1,0:T(8,128)(2,1)S(1)}, bf16[128,2048]{1,0:T(8,128)(2,1)S(1)}, u32[]{:S(2)}, u32[]{:S(2)}) collective-permute-start(bf16[128,2048]{1,0:T(8,128)(2,1)S(1)} %multiply_convert_fusion.refs_0_), channel_id=1, source_target_pairs={{0,2},{1,3},{2,0},{3,1},{4,6},{5,7},{6,4},{7,5},{8,10},{9,11},{10,... | collective-permute-start | bytes 1572872 | tf_op jit(solution)/shard_map/ppermute | solution.py:722
  190.7 5.9 %collective-permute-start.33 = (bf16[16,2048]{1,0:T(8,128)(2,1)S(1)}, bf16[16,2048]{1,0:T(8,128)(2,1)S(1)}, u32[]{:S(2)}, u32[]{:S(2)}) collective-permute-start(bf16[16,2048]{1,0:T(8,128)(2,1)S(1)} %slice.76), channel_id=1, source_target_pairs={{0,4},{4,8},{8,12},{12,16},{16,20},{20,24},{24,28},{1,5},{5,9},{9,... | collective-permute-start | bytes 196616 | tf_op jit(solution)/shard_map/ppermute | solution.py:24
  196.6 8.0 %collective-permute-start.36 = (bf16[16,2048]{1,0:T(8,128)(2,1)S(1)}, bf16[16,2048]{1,0:T(8,128)(2,1)S(1)}, u32[]{:S(2)}, u32[]{:S(2)}) collective-permute-start(bf16[16,2048]{1,0:T(8,128)(2,1)S(1)} %collective-permute-done.33.refs_2_), channel_id=1, source_target_pairs={{0,2},{1,3},{2,0},{3,1},{4,6},{5,7},{6,4},{7,5},{8,10},{9,11},{10,... | collective-permute-start | bytes 196616 | tf_op jit(solution)/shard_map/ppermute | solution.py:722
  204.6 2.4 collective-permute-start.37
  205.5 2.4 collective-permute-start.38
  207.0 33.1 %collective-permute-start.41 = (bf16[256,2048]{1,0:T(8,128)(2,1)}, bf16[256,2048]{1,0:T(8,128)(2,1)}, u32[]{:S(2)}, u32[]{:S(2)}) collective-permute-start(bf16[256,2048]{1,0:T(8,128)(2,1)} %get-tuple-element.105), channel_id=1, source_target_pairs={{0,2},{1,3},{2,0},{3,1},{4,6},{5,7},{6,4},{7,5},{8,10},{9,11},{10,... | collective-permute-start | bytes 3145736 | tf_op jit(solution)/shard_map/ppermute | solution.py:722
  231.1 38.8 %collective-permute-start.50 = (bf16[512,2048]{1,0:T(8,128)(2,1)S(1)}, bf16[512,2048]{1,0:T(8,128)(2,1)}, u32[]{:S(2)}, u32[]{:S(2)}) collective-permute-start(bf16[512,2048]{1,0:T(8,128)(2,1)S(1)} %copy-done.4), channel_id=1, source_target_pairs={{0,1},{1,0},{2,3},{3,2},{4,5},{5,4},{6,7},{7,6},{8,9},{9,8},{10,11... | collective-permute-start | bytes 6291464 | tf_op jit(solution)/shard_map/ppermute | solution.py:722
  231.7 25.1 %collective-permute-start.44 = (bf16[256,2048]{1,0:T(8,128)(2,1)}, bf16[256,2048]{1,0:T(8,128)(2,1)}, u32[]{:S(2)}, u32[]{:S(2)}) collective-permute-start(bf16[256,2048]{1,0:T(8,128)(2,1)} %get-tuple-element.107), channel_id=1, source_target_pairs={{0,2},{1,3},{2,0},{3,1},{4,6},{5,7},{6,4},{7,5},{8,10},{9,11},{10,... | collective-permute-start | bytes 3145736 | tf_op jit(solution)/shard_map/ppermute | solution.py:722
  232.3 7.9 %collective-permute-start.40 = (bf16[4,128,256]{2,1,0:T(8,128)(2,1)}, bf16[4,128,256]{2,1,0:T(8,128)(2,1)S(1)}, u32[]{:S(2)}, u32[]{:S(2)}) collective-permute-start(bf16[4,128,256]{2,1,0:T(8,128)(2,1)} %get-tuple-element.104.mine_ref), channel_id=1, source_target_pairs={{0,4},{4,0},{8,12},{12,8},{16,20},{20,16},{24,28},{28,24},{1,5},{5... | collective-permute-start | bytes 786440 | tf_op jit(solution)/shard_map/ppermute | solution.py:806
  241.4 8.7 %collective-permute-start.42 = (bf16[4,128,256]{2,1,0:T(8,128)(2,1)S(1)}, bf16[4,128,256]{2,1,0:T(8,128)(2,1)S(1)}, u32[]{:S(2)}, u32[]{:S(2)}) collective-permute-start(bf16[4,128,256]{2,1,0:T(8,128)(2,1)S(1)} %pair.1), channel_id=1, source_target_pairs={{0,8},{4,12},{8,16},{12,20},{16,24},{20,28},{1,9},{5,13},{9,17},{1... | collective-permute-start | bytes 786440 | tf_op jit(solution)/shard_map/ppermute | solution.py:24
  250.2 8.8 %collective-permute-start.43 = (bf16[4,128,128]{2,1,0:T(8,128)(2,1)S(1)}, bf16[4,128,128]{2,1,0:T(8,128)(2,1)S(1)}, u32[]{:S(2)}, u32[]{:S(2)}) collective-permute-start(bf16[4,128,128]{2,1,0:T(8,128)(2,1)S(1)} %fusion), channel_id=1, source_target_pairs={{0,16},{4,20},{8,24},{12,28},{1,17},{5,21},{9,25},{13,29},{2,18},{... | collective-permute-start | bytes 393224 | tf_op jit(solution)/shard_map/ppermute | solution.py:24
  259.0 16.6 %collective-permute-start.48 = (bf16[256,2048]{1,0:T(8,128)(2,1)}, bf16[256,2048]{1,0:T(8,128)(2,1)S(1)}, u32[]{:S(2)}, u32[]{:S(2)}) collective-permute-start(bf16[256,2048]{1,0:T(8,128)(2,1)} %collective-permute-done.44.refs_3_), channel_id=1, source_target_pairs={{0,1},{1,0},{2,3},{3,2},{4,5},{5,4},{6,7},{7,6},{8,9},{9,8},{10,11... | collective-permute-start | bytes 3145736 | tf_op jit(solution)/shard_map/ppermute | solution.py:722
  260.6 15.0 %collective-permute-start.47 = (bf16[256,2048]{1,0:T(8,128)(2,1)}, bf16[256,2048]{1,0:T(8,128)(2,1)S(1)}, u32[]{:S(2)}, u32[]{:S(2)}) collective-permute-start(bf16[256,2048]{1,0:T(8,128)(2,1)} %collective-permute-done.41.refs_2_), channel_id=1, source_target_pairs={{0,1},{1,0},{2,3},{3,2},{4,5},{5,4},{6,7},{7,6},{8,9},{9,8},{10,11... | collective-permute-start | bytes 3145736 | tf_op jit(solution)/shard_map/ppermute | solution.py:722
  267.6 5.6 %collective-permute-start.45 = (bf16[128,512]{1,0:T(8,128)(2,1)S(1)}, bf16[128,512]{1,0:T(8,128)(2,1)S(1)}, u32[]{:S(2)}, u32[]{:S(2)}) collective-permute-start(bf16[128,512]{1,0:T(8,128)(2,1)S(1)} %get-tuple-element.123), channel_id=1, source_target_pairs={{0,2},{1,3},{2,0},{3,1},{4,6},{5,7},{6,4},{7,5},{8,10},{9,11},{10,... | collective-permute-start | bytes 393224 | tf_op jit(solution)/shard_map/ppermute | solution.py:722
  268.7 6.9 %collective-permute-start.46 = (bf16[128,512]{1,0:T(8,128)(2,1)S(1)}, bf16[128,512]{1,0:T(8,128)(2,1)S(1)}, u32[]{:S(2)}, u32[]{:S(2)}) collective-permute-start(bf16[128,512]{1,0:T(8,128)(2,1)S(1)} %get-tuple-element.122), channel_id=1, source_target_pairs={{0,3},{1,2},{2,1},{3,0},{4,7},{5,6},{6,5},{7,4},{8,11},{9,10},{10,... | collective-permute-start | bytes 393224 | tf_op jit(solution)/shard_map/ppermute | solution.py:722
  (38 other events, 397.4 us)
